TPU v7x, 32 devices: a whole 2x2x4 slice. The times are simulated.
32 devices in a mesh: lat: 4 (over y, x), lon: 8 (over z, core).
Axes of the slice: x: 2, y: 2, z: 4, core: 2. Of those that a mesh axis runs over, the one named last changes fastest.
Arguments:
- tokens: bfloat16 [48, 384, 512], P('lat', 'lon'), may hold values from -6 to 6
- expert_ids: int32 [2, 4, 8, 576, 1], P(None, 'lat', 'lon'), may hold values from 0 to 15; in each aligned block of 576 rows (0 to 575, 576 to 1151, ..., all dimensions but the last counted through in order) at most 48 rows name the same one
- norm_gain: float32 [2, 2, 512], replicated, may hold values from 0.5 to 2
- weight_qkv: bfloat16 [2, 512, 1536], replicated, may hold values from -0.25 to 0.25
- weight_proj: bfloat16 [2, 512, 512], replicated, may hold values from -0.25 to 0.25
- temper: float32 [2, 16], replicated, may hold values from 0.5 to 12
- router: bfloat16 [2, 512, 16], replicated, may hold values from -0.25 to 0.25
- weight_in: bfloat16 [2, 32, 512, 1024], P(None, 'lon'), may hold values from -0.25 to 0.25
- weight_out: bfloat16 [2, 32, 1024, 512], P(None, 'lon'), may hold values from -0.125 to 0.125
Outputs:
- result: bfloat16 [48, 384, 512], P('lat', 'lon')
Inputs may be any that keep to these rules, and one draw needn't show every extreme that they name: `expert_ids`: in each layer, among the 576 cells of one device's tile no expert is named more than 48 times.
All inputs are finite; a program needn't handle non-finite values.
Results may differ from a plain program's by a relative error of at most 0.028.
The roundings to bfloat16 on the way count: a program that leaves them out, or rounds other values in their place, can miss the bound.
Values may be sent and summed in bfloat16 or wider, within the bound.
No kernel may reach another device: no remote copies, remote signals or barrier semaphores. Data moves between devices by JAX's collectives and lax.ppermute only.
A program may use at most 128 MiB of HBM per device.

v0:
```python
import functools
import math

import jax
import jax.numpy as jnp
import numpy as np
from jax import lax
from jax.experimental import pallas as pl
from jax.experimental.pallas import tpu as pltpu
from jax.sharding import PartitionSpec as P

WIN = 12
HALF = WIN // 2
EXPERTS = 16
LAYERS = 2
CAP = 48
EPSILON = 1e-05
LANES = 128
MIB = 1 << 20

F32 = jnp.float32
BF16 = jnp.bfloat16


def norm_rows(values, gain_row):
    centered = values - jnp.mean(values, axis=-1, keepdims=True)
    variance = jnp.mean(centered * centered, axis=-1, keepdims=True)
    return (centered * lax.rsqrt(variance + EPSILON) * gain_row).astype(BF16)


def dot(left, right, dims=((1,), (0,))):
    return lax.dot_general(left, right, (dims, ((), ())), preferred_element_type=F32)


def one_hot_columns(column, count):
    spread = lax.broadcasted_iota(jnp.int32, (column.shape[0], count), 1)
    return jnp.where(spread == column, 1.0, 0.0).astype(BF16)


def one_hot_rows(row, count):
    spread = lax.broadcasted_iota(jnp.int32, (count, row.shape[1]), 0)
    return jnp.where(spread == row, 1.0, 0.0).astype(BF16)


def route(ynorm, router, experts, target_row, gate_ref, piece_refs):
    logits = dot(ynorm, router)
    chosen = lax.broadcasted_iota(jnp.int32, logits.shape, 1) == experts
    picked = jnp.sum(jnp.where(chosen, logits, 0.0), axis=1, keepdims=True)
    gate_ref[...] = jax.nn.sigmoid(picked)
    slots = piece_refs[0].shape[0]
    for index, piece_ref in enumerate(piece_refs):
        spread = one_hot_rows(target_row - index * slots, slots)
        piece_ref[...] = dot(spread, ynorm).astype(BF16)


def attend(frame, layer, seam_ref, temper_ref, gain_ref, wqkv_ref, wproj_ref, qkv_ref, context_ref):
    total, channels = frame.shape
    heads = temper_ref.shape[1]
    width = channels // heads
    area = WIN * WIN
    windows = total // area
    group = LANES // width
    main = LANES
    rest = area - main
    lanes = group * area
    normed = norm_rows(frame, gain_ref[0, 0:1, :])
    qkv_ref[...] = dot(normed, wqkv_ref[0]).astype(BF16)

    lane = lax.broadcasted_iota(jnp.int32, (1, lanes), 1)
    leftover = lane >= group * main
    head_of = jnp.where(leftover, (lane - group * main) // rest, lane // main)
    query_of = jnp.where(leftover, main + (lane - group * main) % rest, lane % main)
    late = query_of >= area // 2
    seam = seam_ref[0, 0] > 0
    bias_early = jnp.where(jnp.logical_and(seam, late), -1e30, 0.0)
    bias_late = jnp.where(jnp.logical_and(seam, jnp.logical_not(late)), -1e30, 0.0)
    channel_head = lax.broadcasted_iota(jnp.int32, (1, LANES), 1) // width
    keep = [jnp.where(channel_head == h, 1.0, 0.0).astype(BF16) for h in range(group)]
    keep_f = [jnp.where(channel_head == h, 1.0, 0.0) for h in range(group)]

    def one_window(window):
        rows = pl.ds(window * area, area)
        for g in range(channels // LANES):
            q = qkv_ref[rows, g * LANES : (g + 1) * LANES]
            k = qkv_ref[rows, channels + g * LANES : channels + (g + 1) * LANES]
            v = qkv_ref[rows, 2 * channels + g * LANES : 2 * channels + (g + 1) * LANES]
            stacked = jnp.concatenate(
                [q[:main] * keep[h] for h in range(group)] + [q[main:] * keep[h] for h in range(group)], axis=0
            )
            scores = dot(k, stacked, ((1,), (1,)))
            scale = jnp.zeros((1, lanes), F32)
            for h in range(group):
                factor = temper_ref[layer, g * group + h] * (math.log2(math.e) / math.sqrt(width))
                scale = jnp.where(head_of == h, factor, scale)
            if layer % 2 == 1:
                scores = jnp.concatenate(
                    [scores[: area // 2] + bias_early, scores[area // 2 :] + bias_late], axis=0
                )
            peak = jnp.max(scores, axis=0, keepdims=True)
            weights = jnp.exp2((scores - peak) * scale)
            shares = (weights * (1.0 / jnp.sum(weights, axis=0, keepdims=True))).astype(BF16)
            mixed_t = dot(v, shares, ((0,), (0,)))
            picked = jnp.concatenate(
                [mixed_t[h * width : (h + 1) * width, h * main : (h + 1) * main] for h in range(group)], axis=0
            )
            first = jnp.transpose(picked)
            tail = jnp.transpose(mixed_t[:, group * main :])
            second = tail[:rest] * keep_f[0]
            for h in range(1, group):
                second = second + tail[h * rest : (h + 1) * rest] * keep_f[h]
            context = jnp.concatenate([first, second], axis=0).astype(BF16)
            context_ref[rows, g * LANES : (g + 1) * LANES] = context

    for window in range(windows):
        one_window(window)
    attended = dot(context_ref[...], wproj_ref[0])
    return (frame + attended).astype(BF16)


def first_kernel(
    seam_ref, temper_ref, tokens_ref, order_ref, experts_ref, target_ref, gain_ref, wqkv_ref, wproj_ref, router_ref,
    mixed_ref, gate_ref, *refs, layer
):
    *piece_refs, qkv_ref, context_ref = refs
    tokens = tokens_ref[...]
    frame = dot(one_hot_columns(order_ref[...], tokens.shape[0]), tokens)
    mixed = attend(frame, layer, seam_ref, temper_ref, gain_ref, wqkv_ref, wproj_ref, qkv_ref, context_ref)
    mixed_ref[...] = mixed
    ynorm = norm_rows(mixed.astype(F32), gain_ref[0, 1:2, :])
    route(ynorm, router_ref[0], experts_ref[...], target_ref[...], gate_ref, piece_refs)


def shifted_kernel(
    seam_ref, temper_ref, own_ref, north_ref, east_ref, corner_ref, gain_ref, wqkv_ref, wproj_ref,
    low_ref, high_ref, low_edge_ref, high_edge_ref, low_scratch, high_scratch, qkv_ref, context_ref, *, layer
):
    half, channels = own_ref.shape
    strip = HALF * HALF
    part = WIN * HALF
    edge = east_ref.shape[0]
    low_scratch[0:half] = own_ref[...].astype(F32)
    low_scratch[half : half + edge] = east_ref[...].astype(F32)
    high_scratch[0:half] = north_ref[...].astype(F32)
    high_scratch[half : half + edge] = corner_ref[...].astype(F32)
    pieces = []
    for window in range(half // part):
        start = strip + window * part
        pieces += [low_scratch[start : start + part], high_scratch[start : start + part]]
    frame = jnp.concatenate(pieces, axis=0)
    mixed = attend(frame, layer, seam_ref, temper_ref, gain_ref, wqkv_ref, wproj_ref, qkv_ref, context_ref)
    mixed = mixed.astype(F32)
    low, high = split_halves(mixed)
    low_ref[...] = low.astype(BF16)
    high_ref[...] = high.astype(BF16)
    low_edge_ref[...] = low[half - edge :].astype(BF16)
    high_edge_ref[...] = high[half - edge :].astype(BF16)


def split_halves(rows):
    part = WIN * HALF
    pieces = [rows[start : start + part] for start in range(0, rows.shape[0], part)]
    return jnp.concatenate(pieces[0::2], axis=0), jnp.concatenate(pieces[1::2], axis=0)


def route_kernel(own_ref, south_ref, west_ref, corner_ref, experts_ref, target_ref, gain_ref, router_ref,
                 rows_ref, gate_ref, *piece_refs):
    mixed = jnp.concatenate([own_ref[...], south_ref[...], west_ref[...], corner_ref[...]], axis=0)
    rows_ref[...] = mixed
    ynorm = norm_rows(mixed.astype(F32), gain_ref[0, 1:2, :])
    route(ynorm, router_ref[0], experts_ref[...], target_ref[...], gate_ref, piece_refs)


def expert_kernel(*refs, sources, steps, local):
    piece_refs = refs[:sources]
    own_in, own_out, far_in, far_out = refs[sources : sources + 4]
    out_refs = refs[sources + 4 : 2 * sources + 4]
    total_ref = refs[-1]
    step = pl.program_id(0)
    slots, channels = piece_refs[0].shape
    groups = slots // CAP
    mine = step // (steps // max(1, local // 2)) if local > 1 else 0
    other = mine + groups // 2 if local > 1 else 0

    @pl.when(step == 0)
    def _():
        total_ref[...] = jnp.zeros_like(total_ref)

    for place, first_ref, second_ref in ((mine, own_in, own_out), (other, far_in, far_out)):
        start = place * CAP
        if local > 1:
            start = pl.multiple_of(start, CAP)
        rows = jnp.concatenate([ref[pl.ds(start, CAP), :] for ref in piece_refs], axis=0)
        hidden = jax.nn.gelu(dot(rows, first_ref[0, 0])).astype(BF16)
        total_ref[place] += dot(hidden, second_ref[0, 0])

    @pl.when(step == steps - 1)
    def _():
        for index, ref in enumerate(out_refs):
            for g in range(groups):
                ref[g * CAP : (g + 1) * CAP, :] = total_ref[g, index * CAP : (index + 1) * CAP].astype(BF16)


def gathered_state(mixed_ref, gate_ref, target_ref, piece_refs):
    produced = jnp.concatenate([ref[...] for ref in piece_refs], axis=0)
    spread = one_hot_columns(target_ref[...], produced.shape[0])
    combined = dot(spread, produced)
    return (mixed_ref[...].astype(F32) + gate_ref[...] * combined).astype(BF16)


def combine_kernel(mixed_ref, gate_ref, target_ref, *refs):
    *piece_refs, north_ref, own_ref, corner_ref, east_ref = refs
    state = gathered_state(mixed_ref, gate_ref, target_ref, piece_refs).astype(F32)
    low, high = split_halves(state)
    edge = east_ref.shape[0]
    north_ref[...] = low.astype(BF16)
    own_ref[...] = high.astype(BF16)
    corner_ref[...] = low[:edge].astype(BF16)
    east_ref[...] = high[:edge].astype(BF16)


def last_kernel(mixed_ref, gate_ref, target_ref, order_ref, *refs):
    *piece_refs, out_ref = refs
    state = gathered_state(mixed_ref, gate_ref, target_ref, piece_refs)
    out_ref[...] = dot(one_hot_rows(order_ref[...], out_ref.shape[0]), state).astype(BF16)


def whole(shape):
    return pl.BlockSpec(shape, lambda *_: (0,) * len(shape))


def of_layer(array, layer):
    rest = array.shape[1:]
    return pl.BlockSpec((1,) + rest, lambda *_: (layer,) + (0,) * len(rest))


SCALARS = pl.BlockSpec(memory_space=pltpu.SMEM)


def call(kernel, ins, outs, scratch=(), limit=40, flops=0):
    arrays = [array for array, _ in ins]
    size = sum(a.size * a.dtype.itemsize for a in arrays)
    return pl.pallas_call(
        kernel,
        grid=(1,),
        in_specs=[spec if spec is not None else whole(array.shape) for array, spec in ins],
        out_specs=[whole(o.shape) for o in outs],
        out_shape=outs,
        scratch_shapes=list(scratch),
        compiler_params=pltpu.CompilerParams(vmem_limit_bytes=limit * MIB),
        cost_estimate=pl.CostEstimate(flops=flops, bytes_accessed=size, transcendentals=0),
    )(*arrays)


def run_experts(pieces, own_in, own_out, far_in, far_out, layer):
    sources = len(pieces)
    slots, channels = pieces[0].shape
    local, units = own_in.shape[1], own_in.shape[3]
    split = 2
    steps = local * split
    block = units // split
    first = pl.BlockSpec((1, 1, channels, block), lambda i: (layer, i // split, 0, i % split))
    second = pl.BlockSpec((1, 1, block, channels), lambda i: (layer, i // split, i % split, 0))
    groups = slots // CAP
    return pl.pallas_call(
        functools.partial(expert_kernel, sources=sources, steps=steps, local=local),
        grid=(steps,),
        in_specs=[whole(p.shape) for p in pieces] + [first, second, first, second],
        out_specs=[whole(p.shape) for p in pieces],
        out_shape=[jax.ShapeDtypeStruct(p.shape, BF16) for p in pieces],
        scratch_shapes=[pltpu.VMEM((groups, sources * CAP, channels), F32)],
        compiler_params=pltpu.CompilerParams(vmem_limit_bytes=24 * MIB),
        cost_estimate=pl.CostEstimate(
            flops=sources * slots * 8 * channels * units, bytes_accessed=4 * local * channels * units * 2,
            transcendentals=0
        ),
    )(*pieces, own_in, own_out, far_in, far_out)


def lat_lon_pairs(lat_step, lon_step):
    bands, sectors = lax.axis_size("lat"), lax.axis_size("lon")
    pairs = []
    for i in range(bands):
        for j in range(sectors):
            target = (i + lat_step) % bands * sectors + (j + lon_step) % sectors
            pairs.append((i * sectors + j, target))
    return pairs


def shift(value, lat_step, lon_step):
    return lax.ppermute(value, ("lat", "lon"), lat_lon_pairs(lat_step, lon_step))


def between(value, distance):
    sectors = lax.axis_size("lon")
    return lax.ppermute(value, "lon", [(s, s ^ distance) for s in range(sectors)])


def exchange(pieces):
    return [pieces[0]] + [between(pieces[k], 2 * k) for k in range(1, len(pieces))]


def per_device(tokens, expert_ids, norm_gain, weight_qkv, weight_proj, temper, router, weight_in, weight_out):
    row_count, col_count, channels = tokens.shape
    token_count = row_count * col_count
    half = token_count // 2
    strip = HALF * HALF
    part = WIN * HALF
    edge = 48
    sectors = lax.axis_size("lon")
    local = weight_in.shape[1]
    pieces_count = sectors // 2
    pair_experts = EXPERTS // pieces_count
    slots = pair_experts * CAP
    lon = lax.axis_index("lon")
    lat = lax.axis_index("lat")

    far_in = between(weight_in, 1)
    far_out = between(weight_out, 1)

    ids = expert_ids[:, 0, 0, :, 0]
    same = ids[:, :, None] == ids[:, None, :]
    earlier = jnp.arange(token_count)[:, None] > jnp.arange(token_count)[None, :]
    place = jnp.sum(jnp.where(same & earlier, 1, 0), axis=2)
    piece = (ids // pair_experts) ^ (lon // 2)
    inner = (ids % pair_experts) ^ (lon % 2 * (pair_experts // 2))
    target = piece * slots + inner * CAP + place

    def blocks(values):
        cut = values.reshape(row_count // HALF, HALF, col_count // HALF, HALF)
        return cut.transpose(0, 2, 1, 3).reshape(row_count // HALF, half)

    def plain_order(values):
        return blocks(values).reshape(2, half // part, part).transpose(1, 0, 2).reshape(token_count)

    def split_order(values, void):
        low, high = blocks(values)
        gap = lambda n: jnp.full((n,), void, jnp.int32)
        return jnp.concatenate([
            high[strip:], gap(strip), low[strip:], gap(strip),
            gap(edge - strip), high[:strip], gap(edge - strip), low[:strip],
        ])

    positions = jnp.arange(token_count, dtype=jnp.int32)
    order0 = plain_order(positions)
    target0, experts0 = plain_order(target[0]), plain_order(ids[0])
    order1 = split_order(positions, -1)
    target1, experts1 = split_order(target[1], -1), split_order(ids[1], -1)
    rows1 = target1.shape[0]
    seam = jnp.where(lat == lax.axis_size("lat") - 1, 1, 0).astype(jnp.int32).reshape(1, 1)

    shape = jax.ShapeDtypeStruct
    piece_shapes = [shape((slots, channels), BF16)] * pieces_count
    attention_scratch = [pltpu.VMEM((token_count, 3 * channels), BF16), pltpu.VMEM((token_count, channels), BF16)]

    layer = 0
    mixed, gate, *pieces = call(
        functools.partial(first_kernel, layer=layer),
        [(seam, SCALARS), (temper, SCALARS), (tokens.reshape(token_count, channels), None),
         (order0[:, None], None), (experts0[:, None], None), (target0[None, :], None),
         (norm_gain, of_layer(norm_gain, layer)), (weight_qkv, of_layer(weight_qkv, layer)),
         (weight_proj, of_layer(weight_proj, layer)), (router, of_layer(router, layer))],
        [shape((token_count, channels), BF16), shape((token_count, 1), F32)] + piece_shapes,
        attention_scratch,
        flops=4_000_000_000,
    )
    produced = moe(pieces, weight_in, weight_out, far_in, far_out, layer)
    north, own, corner, east = call(
        combine_kernel,
        [(mixed, None), (gate, None), (target0[:, None], None)] + [(p, None) for p in produced],
        [shape((half, channels), BF16)] * 2 + [shape((edge, channels), BF16)] * 2,
        flops=1_000_000_000,
    )

    layer = 1
    north = shift(north, -1, 0)
    east = shift(east, 0, -1)
    corner = shift(corner, -1, -1)
    low, high, low_edge, high_edge = call(
        functools.partial(shifted_kernel, layer=layer),
        [(seam, SCALARS), (temper, SCALARS), (own, None), (north, None), (east, None), (corner, None),
         (norm_gain, of_layer(norm_gain, layer)), (weight_qkv, of_layer(weight_qkv, layer)),
         (weight_proj, of_layer(weight_proj, layer))],
        [shape((half, channels), BF16)] * 2 + [shape((edge, channels), BF16)] * 2,
        [pltpu.VMEM((half + edge, channels), F32)] * 2 + attention_scratch,
        flops=3_000_000_000,
    )
    high = shift(high, 1, 0)
    low_edge = shift(low_edge, 0, 1)
    high_edge = shift(high_edge, 1, 1)
    mixed, gate, *pieces = call(
        route_kernel,
        [(low, None), (high, None), (low_edge, None), (high_edge, None),
         (experts1[:, None], None), (target1[None, :], None),
         (norm_gain, of_layer(norm_gain, layer)), (router, of_layer(router, layer))],
        [shape((rows1, channels), BF16), shape((rows1, 1), F32)] + piece_shapes,
        flops=1_000_000_000,
    )
    produced = moe(pieces, weight_in, weight_out, far_in, far_out, layer)
    (out,) = call(
        last_kernel,
        [(mixed, None), (gate, None), (target1[:, None], None), (order1[None, :], None)]
        + [(p, None) for p in produced],
        [shape((token_count, channels), BF16)],
        flops=1_000_000_000,
    )
    return out.reshape(row_count, col_count, channels)


def moe(pieces, own_in, own_out, far_in, far_out, layer):
    arrived = exchange(pieces)
    if len(arrived) == 4:
        order = [[2], [3], [0, 1]]
    else:
        order = [[k] for k in range(len(arrived))]
    produced = [None] * len(arrived)
    for members in order:
        outs = run_experts([arrived[k] for k in members], own_in, own_out, far_in, far_out, layer)
        for k, value in zip(members, outs):
            produced[k] = value
    return exchange(produced)


def solution(mesh):
    in_specs = (
        P("lat", "lon", None),
        P(None, "lat", "lon", None, None),
        P(),
        P(),
        P(),
        P(),
        P(),
        P(None, "lon", None, None),
        P(None, "lon", None, None),
    )
    out_specs = P("lat", "lon", None)
    return jax.shard_map(per_device, mesh=mesh, in_specs=in_specs, out_specs=out_specs, check_vma=False)
```

profile of v0, /device:TPU:0, one launch (start us, length us, event | category | flops | bytes accessed | tf_op | source)
XLA Modules:
  0.0 174.0 jit_solution(7993265810919787495)
XLA Ops:
  0.0 0.5 collective-permute-start.1
  0.5 0.7 copy.50
  1.3 1.2 select_reduce_fusion
  2.5 0.7 add_add_fusion
  3.3 0.1 reshape_squeeze.13
  3.6 0.7 slice_reduce_fusion.6
  4.3 0.1 reshape_squeeze.12
  4.6 0.1 broadcast_in_dim_reshape.13.experts_ref
  4.8 0.9 copy.36.router_ref
  5.8 0.1 reshape.186.order_ref
  6.0 1.9 %copy-done.5 = bf16[2,512,1536]{2,1,0:T(8,128)(2,1)S(1)} copy-done((bf16[2,512,1536]{2,1,0:T(8,128)(2,1)S(1)}, bf16[2,512,1536]{2,1,0:T(8,128)(2,1)}, u32[]{:S(2)}) %copy-start.5) | copy-done | bytes 3145752
  7.9 1.2 copy-done.7
  9.1 1.1 copy-done.9
  10.1 0.7 copy-done.10
  10.8 0.7 copy-done.12
  11.5 9.1 %shard_map.91 = (bf16[576,512]{1,0:T(8,128)(2,1)S(1)}, f32[576,1]{1,0:T(8,128)S(1)}, bf16[192,512]{1,0:T(8,128)(2,1)S(1)}, bf16[192,512]{1,0:T(8,128)(2,1)S(1)},...) custom-call(s32[1,1]{1,0:T(1,128)} %bitcast.seam_ref, f32[2,16]{1,0:T(2,128)S(1)} %copy-done.12, ...), custom_call_target="tpu_custom_call" | custom-call | flops 4000000000 | bytes 4832132 | tf_op jit(solution)/shard_map/pallas_call | solution.py:242
  20.6 0.8 copy-done.14
  21.4 3.0 %collective-permute-start = (bf16[192,512]{1,0:T(8,128)(2,1)S(1)}, bf16[192,512]{1,0:T(8,128)(2,1)S(1)}, u32[]{:S(2)}, u32[]{:S(2)}) collective-permute-start(bf16[192,512]{1,0:T(8,128)(2,1)S(1)} %get-tuple-element.32), channel_id=1, source_target_pairs={{0,2},{1,3},{2,0},{3,1},{4,6},{5,7},{6,4},{7,5},{8,10},{9,11},{10,... | collective-permute-start | bytes 589832 | tf_op jit(solution)/shard_map/ppermute | solution.py:295
  24.5 2.6 %collective-permute-start.4 = (bf16[192,512]{1,0:T(8,128)(2,1)S(1)}, bf16[192,512]{1,0:T(8,128)(2,1)S(1)}, u32[]{:S(2)}, u32[]{:S(2)}) collective-permute-start(bf16[192,512]{1,0:T(8,128)(2,1)S(1)} %get-tuple-element.35), channel_id=1, source_target_pairs={{0,4},{1,5},{2,6},{3,7},{4,0},{5,1},{6,2},{7,3},{8,12},{9,13},{10,... | collective-permute-start | bytes 589832 | tf_op jit(solution)/shard_map/ppermute | solution.py:295
  27.0 6.0 %collective-permute-done.refs_1_ = bf16[192,512]{1,0:T(8,128)(2,1)S(1)} collective-permute-done((bf16[192,512]{1,0:T(8,128)(2,1)S(1)}, bf16[192,512]{1,0:T(8,128)(2,1)S(1)}, u32[]{:S(2)}, u32[]{:S(2)}) %collective-permute-start) | collective-permute-done | bytes 196640 | tf_op jit(solution)/shard_map/ppermute | solution.py:295
  33.1 3.4 %copy-done = bf16[2,4,512,1024]{3,2,1,0:T(8,128)(2,1)S(1)} copy-done((bf16[2,4,512,1024]{3,2,1,0:T(8,128)(2,1)S(1)}, bf16[2,4,512,1024]{3,2,1,0:T(8,128)(2,1)}, u32[]{:S(2)}) %copy-start) | copy-done | bytes 8388632
  36.5 3.4 %copy-done.2 = bf16[2,4,1024,512]{3,2,1,0:T(8,128)(2,1)S(1)} copy-done((bf16[2,4,1024,512]{3,2,1,0:T(8,128)(2,1)S(1)}, bf16[2,4,1024,512]{3,2,1,0:T(8,128)(2,1)}, u32[]{:S(2)}) %copy-start.2) | copy-done | bytes 8388632
  39.8 9.1 %shard_map.92 = (bf16[192,512]{1,0:T(8,128)(2,1)S(1)}, bf16[192,512]{1,0:T(8,128)(2,1)S(1)}) custom-call(bf16[192,512]{1,0:T(8,128)(2,1)S(1)} %get-tuple-element.31.refs_0_, bf16[192,512]{1,0:T(8,128)(2,1)S(1)} %collective-permute-done.refs_1_, bf16[2,4,512,1024]{3,2,1,0:T(8,128)(2,1)S(1)} %copy-done, bf16[2,4,1024,512]{3,2,1,0:T(8,128)(2,1)S(1)} %copy-done.2, ...), custom_call_target="tpu_custom_call" | custom-call | flops 1610612736 | bytes 16777216 | tf_op jit(solution)/shard_map/pallas_call | solution.py:264
  49.1 3.4 %copy-done.3 = bf16[2,4,1024,512]{3,2,1,0:T(8,128)(2,1)S(1)} copy-done((bf16[2,4,1024,512]{3,2,1,0:T(8,128)(2,1)S(1)}, bf16[2,4,1024,512]{3,2,1,0:T(8,128)(2,1)}, u32[]{:S(2)}) %copy-start.3) | copy-done | bytes 8388632
  52.4 8.7 %shard_map.93 = bf16[192,512]{1,0:T(8,128)(2,1)S(1)} custom-call(bf16[192,512]{1,0:T(8,128)(2,1)S(1)} %collective-permute-done.4.refs_0_, bf16[2,4,512,1024]{3,2,1,0:T(8,128)(2,1)S(1)} %bitcast.15, bf16[2,4,1024,512]{3,2,1,0:T(8,128)(2,1)S(1)} %copy-done.3, bf16[2,4,512,1024]{3,2,1,0:T(8,128)(2,1)} %collective-permute-done.1.refs_4_.refs_3_, ...), custom_call_target="tpu_custom_call" | custom-call | flops 805306368 | bytes 16777216 | tf_op jit(solution)/shard_map/pallas_call | solution.py:264
  61.1 3.8 %collective-permute-start.5 = (bf16[192,512]{1,0:T(8,128)(2,1)S(1)}, bf16[192,512]{1,0:T(8,128)(2,1)S(1)}, u32[]{:S(2)}, u32[]{:S(2)}) collective-permute-start(bf16[192,512]{1,0:T(8,128)(2,1)S(1)} %shard_map.93), channel_id=1, source_target_pairs={{0,4},{1,5},{2,6},{3,7},{4,0},{5,1},{6,2},{7,3},{8,12},{9,13},{10,... | collective-permute-start | bytes 589832 | tf_op jit(solution)/shard_map/ppermute | solution.py:295
  65.0 8.7 %shard_map.94 = bf16[192,512]{1,0:T(8,128)(2,1)S(1)} custom-call(bf16[192,512]{1,0:T(8,128)(2,1)S(1)} %collective-permute-done.6.refs_0_, bf16[2,4,512,1024]{3,2,1,0:T(8,128)(2,1)S(1)} %bitcast.15, bf16[2,4,1024,512]{3,2,1,0:T(8,128)(2,1)S(1)} %copy-done.3, bf16[2,4,512,1024]{3,2,1,0:T(8,128)(2,1)} %collective-permute-done.1.refs_4_.refs_3_, ...), custom_call_target="tpu_custom_call" | custom-call | flops 805306368 | bytes 16777216 | tf_op jit(solution)/shard_map/pallas_call | solution.py:264
  73.7 0.7 collective-permute-start.7
  74.4 0.1 broadcast_in_dim_reshape.14.target_ref
  74.5 0.1 reshape_squeeze.15
  74.7 6.6 %collective-permute-done.7.refs_3_ = bf16[192,512]{1,0:T(8,128)(2,1)S(1)} collective-permute-done((bf16[192,512]{1,0:T(8,128)(2,1)S(1)}, bf16[192,512]{1,0:T(8,128)(2,1)S(1)}, u32[]{:S(2)}, u32[]{:S(2)}) %collective-permute-start.7) | collective-permute-done | bytes 196640 | tf_op jit(solution)/shard_map/ppermute | solution.py:295
  81.3 1.1 copy-done.15
  82.4 0.7 shard_map.95
  83.1 0.7 copy-done.16
  83.8 2.5 %collective-permute-start.8 = (bf16[288,512]{1,0:T(8,128)(2,1)S(1)}, bf16[288,512]{1,0:T(8,128)(2,1)S(1)}, u32[]{:S(2)}, u32[]{:S(2)}) collective-permute-start(bf16[288,512]{1,0:T(8,128)(2,1)S(1)} %get-tuple-element.38), channel_id=1, source_target_pairs={{0,24},{1,25},{2,26},{3,27},{4,28},{5,29},{6,30},{7,31},{8,0},{9,1... | collective-permute-start | bytes 884744 | tf_op jit(solution)/shard_map/ppermute | solution.py:290
  86.3 1.0 collective-permute-start.9
  87.3 0.1 reshape_squeeze.14
  87.4 3.4 %collective-permute-done.10.corner_ref = bf16[48,512]{1,0:T(8,128)(2,1)S(1)} collective-permute-done((bf16[48,512]{1,0:T(8,128)(2,1)S(1)}, bf16[48,512]{1,0:T(8,128)(2,1)S(1)}, u32[]{:S(2)}, u32[]{:S(2)}) %collective-permute-start.10) | collective-permute-done | bytes 49184 | tf_op jit(solution)/shard_map/ppermute | solution.py:290
  90.9 0.7 collective-permute-done.8.north_ref
  91.6 1.9 %copy-done.6 = bf16[2,512,1536]{2,1,0:T(8,128)(2,1)S(1)} copy-done((bf16[2,512,1536]{2,1,0:T(8,128)(2,1)S(1)}, bf16[2,512,1536]{2,1,0:T(8,128)(2,1)}, u32[]{:S(2)}) %copy-start.6) | copy-done | bytes 3145752
  93.5 1.0 copy-done.17
  94.4 7.4 %shard_map.96 = (bf16[288,512]{1,0:T(8,128)(2,1)S(1)}, bf16[288,512]{1,0:T(8,128)(2,1)S(1)}, bf16[48,512]{1,0:T(8,128)(2,1)S(1)}, bf16[48,512]{1,0:T(8,128)(2,1)S(1)}) custom-call(s32[1,1]{1,0:T(1,128)} %bitcast.seam_ref, f32[2,16]{1,0:T(2,128)S(1)} %copy-done.13, bf16[288,512]{1,0:T(8,128)(2,1)S(1)} %copy-done.17, ...), custom_call_target="tpu_custom_call" | custom-call | flops 3000000000 | bytes 4890756 | tf_op jit(solution)/shard_map/pallas_call | solution.py:242
  101.9 2.4 %collective-permute-start.11 = (bf16[288,512]{1,0:T(8,128)(2,1)S(1)}, bf16[288,512]{1,0:T(8,128)(2,1)S(1)}, u32[]{:S(2)}, u32[]{:S(2)}) collective-permute-start(bf16[288,512]{1,0:T(8,128)(2,1)S(1)} %get-tuple-element.42), channel_id=1, source_target_pairs={{0,8},{1,9},{2,10},{3,11},{4,12},{5,13},{6,14},{7,15},{8,16},{9,17... | collective-permute-start | bytes 884744 | tf_op jit(solution)/shard_map/ppermute | solution.py:290
  104.3 2.8 %collective-permute-start.13 = (bf16[48,512]{1,0:T(8,128)(2,1)S(1)}, bf16[48,512]{1,0:T(8,128)(2,1)S(1)}, u32[]{:S(2)}, u32[]{:S(2)}) collective-permute-start(bf16[48,512]{1,0:T(8,128)(2,1)S(1)} %get-tuple-element.44), channel_id=1, source_target_pairs={{0,9},{1,10},{2,11},{3,12},{4,13},{5,14},{6,15},{7,8},{8,17},{9,18... | collective-permute-start | bytes 147464 | tf_op jit(solution)/shard_map/ppermute | solution.py:290
  108.1 0.2 broadcast_in_dim.29.experts_ref
  108.3 1.3 collective-permute-done.12.west_ref
  109.6 2.0 %collective-permute-done.13.corner_ref = bf16[48,512]{1,0:T(8,128)(2,1)S(1)} collective-permute-done((bf16[48,512]{1,0:T(8,128)(2,1)S(1)}, bf16[48,512]{1,0:T(8,128)(2,1)S(1)}, u32[]{:S(2)}, u32[]{:S(2)}) %collective-permute-start.13) | collective-permute-done | bytes 49184 | tf_op jit(solution)/shard_map/ppermute | solution.py:290
  111.6 0.5 collective-permute-done.11.south_ref
  112.1 1.4 shard_map.97
  113.5 1.7 collective-permute-start.18
  115.2 1.6 collective-permute-start.16
  116.8 1.2 collective-permute-start.14
  117.9 0.1 broadcast_in_dim.30.target_ref
  118.1 0.1 slice.125
  118.3 4.9 %collective-permute-done.18.refs_0_ = bf16[192,512]{1,0:T(8,128)(2,1)S(1)} collective-permute-done((bf16[192,512]{1,0:T(8,128)(2,1)S(1)}, bf16[192,512]{1,0:T(8,128)(2,1)S(1)}, u32[]{:S(2)}, u32[]{:S(2)}) %collective-permute-start.18) | collective-permute-done | bytes 196640 | tf_op jit(solution)/shard_map/ppermute | solution.py:295
  123.2 3.4 %copy-done.1 = bf16[2,4,512,1024]{3,2,1,0:T(8,128)(2,1)S(1)} copy-done((bf16[2,4,512,1024]{3,2,1,0:T(8,128)(2,1)S(1)}, bf16[2,4,512,1024]{3,2,1,0:T(8,128)(2,1)}, u32[]{:S(2)}) %copy-start.1) | copy-done | bytes 8388632
  126.6 3.4 %copy-done.4 = bf16[2,4,1024,512]{3,2,1,0:T(8,128)(2,1)S(1)} copy-done((bf16[2,4,1024,512]{3,2,1,0:T(8,128)(2,1)S(1)}, bf16[2,4,1024,512]{3,2,1,0:T(8,128)(2,1)}, u32[]{:S(2)}) %copy-start.4) | copy-done | bytes 8388632
  130.0 8.7 %shard_map.100 = bf16[192,512]{1,0:T(8,128)(2,1)S(1)} custom-call(bf16[192,512]{1,0:T(8,128)(2,1)S(1)} %collective-permute-done.18.refs_0_, bf16[2,4,512,1024]{3,2,1,0:T(8,128)(2,1)S(1)} %copy-done.1, bf16[2,4,1024,512]{3,2,1,0:T(8,128)(2,1)S(1)} %copy-done.4, bf16[2,4,512,1024]{3,2,1,0:T(8,128)(2,1)} %collective-permute-done.1.refs_4_.refs_3_, ...), custom_call_target="tpu_custom_call" | custom-call | flops 805306368 | bytes 16777216 | tf_op jit(solution)/shard_map/pallas_call | solution.py:264
  138.7 1.7 collective-permute-start.19
  140.4 8.7 %shard_map.99 = bf16[192,512]{1,0:T(8,128)(2,1)S(1)} custom-call(bf16[192,512]{1,0:T(8,128)(2,1)S(1)} %collective-permute-done.16.refs_0_, bf16[2,4,512,1024]{3,2,1,0:T(8,128)(2,1)S(1)} %copy-done.1, bf16[2,4,1024,512]{3,2,1,0:T(8,128)(2,1)S(1)} %copy-done.4, bf16[2,4,512,1024]{3,2,1,0:T(8,128)(2,1)} %collective-permute-done.1.refs_4_.refs_3_, ...), custom_call_target="tpu_custom_call" | custom-call | flops 805306368 | bytes 16777216 | tf_op jit(solution)/shard_map/pallas_call | solution.py:264
  149.1 8.1 %collective-permute-start.17 = (bf16[192,512]{1,0:T(8,128)(2,1)S(1)}, bf16[192,512]{1,0:T(8,128)(2,1)S(1)}, u32[]{:S(2)}, u32[]{:S(2)}) collective-permute-start(bf16[192,512]{1,0:T(8,128)(2,1)S(1)} %shard_map.99), channel_id=1, source_target_pairs={{0,4},{1,5},{2,6},{3,7},{4,0},{5,1},{6,2},{7,3},{8,12},{9,13},{10,... | collective-permute-start | bytes 589832 | tf_op jit(solution)/shard_map/ppermute | solution.py:295
  157.2 9.0 %shard_map.98 = (bf16[192,512]{1,0:T(8,128)(2,1)S(1)}, bf16[192,512]{1,0:T(8,128)(2,1)S(1)}) custom-call(bf16[192,512]{1,0:T(8,128)(2,1)S(1)} %get-tuple-element.47.refs_0_, bf16[192,512]{1,0:T(8,128)(2,1)S(1)} %collective-permute-done.14.refs_1_, bf16[2,4,512,1024]{3,2,1,0:T(8,128)(2,1)S(1)} %copy-done.1, bf16[2,4,1024,512]{3,2,1,0:T(8,128)(2,1)S(1)} %copy-done.4, ...), custom_call_target="tpu_custom_call" | custom-call | flops 1610612736 | bytes 16777216 | tf_op jit(solution)/shard_map/pallas_call | solution.py:264
  166.5 5.4 %collective-permute-done.15.refs_1_ = bf16[192,512]{1,0:T(8,128)(2,1)S(1)} collective-permute-done((bf16[192,512]{1,0:T(8,128)(2,1)S(1)}, bf16[192,512]{1,0:T(8,128)(2,1)S(1)}, u32[]{:S(2)}, u32[]{:S(2)}) %collective-permute-start.15) | collective-permute-done | bytes 196640 | tf_op jit(solution)/shard_map/ppermute | solution.py:295
  171.9 2.0 %shard_map.101 = bf16[576,512]{1,0:T(8,128)(2,1)} custom-call(bf16[672,512]{1,0:T(8,128)(2,1)S(1)} %get-tuple-element.45.mixed_ref, f32[672,1]{1,0:T(8,128)S(1)} %get-tuple-element.46.gate_ref, s32[672,1]{1,0:T(8,128)S(1)} %broadcast_in_dim.30.target_ref, s32[1,672]{1,0:T(1,128)S(1)} %broadcast_in_dim.28.order_ref, ...), custom_call_target="tpu_custom_call" | custom-call | flops 1000000000 | bytes 1482624 | tf_op jit(solution)/shard_map/pallas_call | solution.py:242
  (84 shorter events, 2.2 us)
Async XLA Ops:
  0.0 33.1 %collective-permute-start.1 = (bf16[2,4,512,1024]{3,2,1,0:T(8,128)(2,1)}, bf16[2,4,512,1024]{3,2,1,0:T(8,128)(2,1)}, u32[]{:S(2)}, u32[]{:S(2)}) collective-permute-start(bf16[2,4,512,1024]{3,2,1,0:T(8,128)(2,1)} %refs_1_.7), channel_id=1, source_target_pairs={{0,1},{1,0},{2,3},{3,2},{4,5},{5,4},{6,7},{7,6},{8,9},{9,8},{10,11... | collective-permute-start | bytes 25165832 | tf_op jit(solution)/shard_map/ppermute | solution.py:295
  0.5 32.6 %collective-permute-start.2 = (bf16[2,4,1024,512]{3,2,1,0:T(8,128)(2,1)}, bf16[2,4,1024,512]{3,2,1,0:T(8,128)(2,1)}, u32[]{:S(2)}, u32[]{:S(2)}) collective-permute-start(bf16[2,4,1024,512]{3,2,1,0:T(8,128)(2,1)} %refs_2_.11), channel_id=1, source_target_pairs={{0,1},{1,0},{2,3},{3,2},{4,5},{5,4},{6,7},{7,6},{8,9},{9,8},{10,11... | collective-permute-start | bytes 25165832 | tf_op jit(solution)/shard_map/ppermute | solution.py:295
  6.0 1.9 %copy-start.5 = (bf16[2,512,1536]{2,1,0:T(8,128)(2,1)S(1)}, bf16[2,512,1536]{2,1,0:T(8,128)(2,1)}, u32[]{:S(2)}) copy-start(bf16[2,512,1536]{2,1,0:T(8,128)(2,1)} %wqkv_ref.3) | copy-start | bytes 9437188
  7.8 1.2 copy-start.7
  9.1 1.1 copy-start.9
  10.1 0.7 copy-start.10
  10.8 0.7 copy-start.12
  11.5 37.5 %slice-start = ((s8[8388608]{0:T(1024)(128)(4,1)}), s8[4194304]{0:T(1024)(128)(4,1)S(1)}, s32[]{:S(2)}) async-start(s8[8388608]{0:T(1024)(128)(4,1)} %bitcast.14), calls=%async_computation | async-start | bytes 8388608
  20.6 0.8 copy-start.14
  21.4 11.6 %collective-permute-start = (bf16[192,512]{1,0:T(8,128)(2,1)S(1)}, bf16[192,512]{1,0:T(8,128)(2,1)S(1)}, u32[]{:S(2)}, u32[]{:S(2)}) collective-permute-start(bf16[192,512]{1,0:T(8,128)(2,1)S(1)} %get-tuple-element.32), channel_id=1, source_target_pairs={{0,2},{1,3},{2,0},{3,1},{4,6},{5,7},{6,4},{7,5},{8,10},{9,11},{10,... | collective-permute-start | bytes 589832 | tf_op jit(solution)/shard_map/ppermute | solution.py:295
  24.5 24.6 %collective-permute-start.4 = (bf16[192,512]{1,0:T(8,128)(2,1)S(1)}, bf16[192,512]{1,0:T(8,128)(2,1)S(1)}, u32[]{:S(2)}, u32[]{:S(2)}) collective-permute-start(bf16[192,512]{1,0:T(8,128)(2,1)S(1)} %get-tuple-element.35), channel_id=1, source_target_pairs={{0,4},{1,5},{2,6},{3,7},{4,0},{5,1},{6,2},{7,3},{8,12},{9,13},{10,... | collective-permute-start | bytes 589832 | tf_op jit(solution)/shard_map/ppermute | solution.py:295
  27.0 37.9 %collective-permute-start.6 = (bf16[192,512]{1,0:T(8,128)(2,1)S(1)}, bf16[192,512]{1,0:T(8,128)(2,1)S(1)}, u32[]{:S(2)}, u32[]{:S(2)}) collective-permute-start(bf16[192,512]{1,0:T(8,128)(2,1)S(1)} %get-tuple-element.36), channel_id=1, source_target_pairs={{0,6},{1,7},{2,4},{3,5},{4,2},{5,3},{6,0},{7,1},{8,14},{9,15},{10,... | collective-permute-start | bytes 589832 | tf_op jit(solution)/shard_map/ppermute | solution.py:295
  33.1 3.4 %copy-start = (bf16[2,4,512,1024]{3,2,1,0:T(8,128)(2,1)S(1)}, bf16[2,4,512,1024]{3,2,1,0:T(8,128)(2,1)}, u32[]{:S(2)}) copy-start(bf16[2,4,512,1024]{3,2,1,0:T(8,128)(2,1)} %refs_1_.7) | copy-start | bytes 25165828
  36.5 3.4 %copy-start.2 = (bf16[2,4,1024,512]{3,2,1,0:T(8,128)(2,1)S(1)}, bf16[2,4,1024,512]{3,2,1,0:T(8,128)(2,1)}, u32[]{:S(2)}) copy-start(bf16[2,4,1024,512]{3,2,1,0:T(8,128)(2,1)} %refs_2_.11) | copy-start | bytes 25165828
  39.8 9.2 %slice-start.1 = ((s8[8388608]{0:T(1024)(128)(4,1)}), s8[4194304]{0:T(1024)(128)(4,1)S(1)}, s32[]{:S(2)}) async-start(s8[8388608]{0:T(1024)(128)(4,1)} %bitcast.14), calls=%async_computation.1 | async-start | bytes 8388608
  48.9 25.8 %collective-permute-start.3 = (bf16[192,512]{1,0:T(8,128)(2,1)S(1)}, bf16[192,512]{1,0:T(8,128)(2,1)S(1)}, u32[]{:S(2)}, u32[]{:S(2)}) collective-permute-start(bf16[192,512]{1,0:T(8,128)(2,1)S(1)} %get-tuple-element.34), channel_id=1, source_target_pairs={{0,2},{1,3},{2,0},{3,1},{4,6},{5,7},{6,4},{7,5},{8,10},{9,11},{10,... | collective-permute-start | bytes 589832 | tf_op jit(solution)/shard_map/ppermute | solution.py:295
  49.0 3.4 %copy-start.3 = (bf16[2,4,1024,512]{3,2,1,0:T(8,128)(2,1)S(1)}, bf16[2,4,1024,512]{3,2,1,0:T(8,128)(2,1)}, u32[]{:S(2)}) copy-start(bf16[2,4,1024,512]{3,2,1,0:T(8,128)(2,1)} %refs_2_.11) | copy-start | bytes 25165828
  61.1 13.6 %collective-permute-start.5 = (bf16[192,512]{1,0:T(8,128)(2,1)S(1)}, bf16[192,512]{1,0:T(8,128)(2,1)S(1)}, u32[]{:S(2)}, u32[]{:S(2)}) collective-permute-start(bf16[192,512]{1,0:T(8,128)(2,1)S(1)} %shard_map.93), channel_id=1, source_target_pairs={{0,4},{1,5},{2,6},{3,7},{4,0},{5,1},{6,2},{7,3},{8,12},{9,13},{10,... | collective-permute-start | bytes 589832 | tf_op jit(solution)/shard_map/ppermute | solution.py:295
  73.7 17.9 %copy-start.8 = (bf16[2,512,512]{2,1,0:T(8,128)(2,1)S(1)}, bf16[2,512,512]{2,1,0:T(8,128)(2,1)}, u32[]{:S(2)}) copy-start(bf16[2,512,512]{2,1,0:T(8,128)(2,1)} %wproj_ref.3) | copy-start | bytes 3145732
  73.7 17.9 %copy-start.11 = (f32[2,2,512]{2,1,0:T(2,128)S(1)}, f32[2,2,512]{2,1,0:T(2,128)}, u32[]{:S(2)}) copy-start(f32[2,2,512]{2,1,0:T(2,128)} %gain_ref.5) | copy-start | bytes 24580
  73.7 17.9 %copy-start.13 = (f32[2,16]{1,0:T(2,128)S(1)}, f32[2,16]{1,0:T(2,128)}, u32[]{:S(2)}) copy-start(f32[2,16]{1,0:T(2,128)} %temper_ref.3) | copy-start | bytes 388
  73.7 7.6 %collective-permute-start.7 = (bf16[192,512]{1,0:T(8,128)(2,1)S(1)}, bf16[192,512]{1,0:T(8,128)(2,1)S(1)}, u32[]{:S(2)}, u32[]{:S(2)}) collective-permute-start(bf16[192,512]{1,0:T(8,128)(2,1)S(1)} %shard_map.94), channel_id=1, source_target_pairs={{0,6},{1,7},{2,4},{3,5},{4,2},{5,3},{6,0},{7,1},{8,14},{9,15},{10,... | collective-permute-start | bytes 589832 | tf_op jit(solution)/shard_map/ppermute | solution.py:295
  81.3 1.1 copy-start.15
  83.1 0.7 copy-start.16
  83.8 7.8 %collective-permute-start.8 = (bf16[288,512]{1,0:T(8,128)(2,1)S(1)}, bf16[288,512]{1,0:T(8,128)(2,1)S(1)}, u32[]{:S(2)}, u32[]{:S(2)}) collective-permute-start(bf16[288,512]{1,0:T(8,128)(2,1)S(1)} %get-tuple-element.38), channel_id=1, source_target_pairs={{0,24},{1,25},{2,26},{3,27},{4,28},{5,29},{6,30},{7,31},{8,0},{9,1... | collective-permute-start | bytes 884744 | tf_op jit(solution)/shard_map/ppermute | solution.py:290
  86.2 4.6 %collective-permute-start.10 = (bf16[48,512]{1,0:T(8,128)(2,1)S(1)}, bf16[48,512]{1,0:T(8,128)(2,1)S(1)}, u32[]{:S(2)}, u32[]{:S(2)}) collective-permute-start(bf16[48,512]{1,0:T(8,128)(2,1)S(1)} %get-tuple-element.40), channel_id=1, source_target_pairs={{0,31},{1,24},{2,25},{3,26},{4,27},{5,28},{6,29},{7,30},{8,7},{9,0... | collective-permute-start | bytes 147464 | tf_op jit(solution)/shard_map/ppermute | solution.py:290
  86.3 4.6 %collective-permute-start.9 = (bf16[48,512]{1,0:T(8,128)(2,1)S(1)}, bf16[48,512]{1,0:T(8,128)(2,1)S(1)}, u32[]{:S(2)}, u32[]{:S(2)}) collective-permute-start(bf16[48,512]{1,0:T(8,128)(2,1)S(1)} %get-tuple-element.39), channel_id=1, source_target_pairs={{0,7},{1,0},{2,1},{3,2},{4,3},{5,4},{6,5},{7,6},{8,15},{9,8},{10,9... | collective-permute-start | bytes 147464 | tf_op jit(solution)/shard_map/ppermute | solution.py:290
  91.6 1.9 %copy-start.6 = (bf16[2,512,1536]{2,1,0:T(8,128)(2,1)S(1)}, bf16[2,512,1536]{2,1,0:T(8,128)(2,1)}, u32[]{:S(2)}) copy-start(bf16[2,512,1536]{2,1,0:T(8,128)(2,1)} %wqkv_ref.3) | copy-start | bytes 9437188
  93.5 1.0 copy-start.17
  101.9 10.2 %collective-permute-start.11 = (bf16[288,512]{1,0:T(8,128)(2,1)S(1)}, bf16[288,512]{1,0:T(8,128)(2,1)S(1)}, u32[]{:S(2)}, u32[]{:S(2)}) collective-permute-start(bf16[288,512]{1,0:T(8,128)(2,1)S(1)} %get-tuple-element.42), channel_id=1, source_target_pairs={{0,8},{1,9},{2,10},{3,11},{4,12},{5,13},{6,14},{7,15},{8,16},{9,17... | collective-permute-start | bytes 884744 | tf_op jit(solution)/shard_map/ppermute | solution.py:290
  104.3 5.3 %collective-permute-start.12 = (bf16[48,512]{1,0:T(8,128)(2,1)S(1)}, bf16[48,512]{1,0:T(8,128)(2,1)S(1)}, u32[]{:S(2)}, u32[]{:S(2)}) collective-permute-start(bf16[48,512]{1,0:T(8,128)(2,1)S(1)} %get-tuple-element.43), channel_id=1, source_target_pairs={{0,1},{1,2},{2,3},{3,4},{4,5},{5,6},{6,7},{7,0},{8,9},{9,10},{10,1... | collective-permute-start | bytes 147464 | tf_op jit(solution)/shard_map/ppermute | solution.py:290
  104.3 7.3 %collective-permute-start.13 = (bf16[48,512]{1,0:T(8,128)(2,1)S(1)}, bf16[48,512]{1,0:T(8,128)(2,1)S(1)}, u32[]{:S(2)}, u32[]{:S(2)}) collective-permute-start(bf16[48,512]{1,0:T(8,128)(2,1)S(1)} %get-tuple-element.44), channel_id=1, source_target_pairs={{0,9},{1,10},{2,11},{3,12},{4,13},{5,14},{6,15},{7,8},{8,17},{9,18... | collective-permute-start | bytes 147464 | tf_op jit(solution)/shard_map/ppermute | solution.py:290
  113.5 9.7 %collective-permute-start.18 = (bf16[192,512]{1,0:T(8,128)(2,1)S(1)}, bf16[192,512]{1,0:T(8,128)(2,1)S(1)}, u32[]{:S(2)}, u32[]{:S(2)}) collective-permute-start(bf16[192,512]{1,0:T(8,128)(2,1)S(1)} %get-tuple-element.52), channel_id=1, source_target_pairs={{0,6},{1,7},{2,4},{3,5},{4,2},{5,3},{6,0},{7,1},{8,14},{9,15},{10,... | collective-permute-start | bytes 589832 | tf_op jit(solution)/shard_map/ppermute | solution.py:295
  115.2 25.2 %collective-permute-start.16 = (bf16[192,512]{1,0:T(8,128)(2,1)S(1)}, bf16[192,512]{1,0:T(8,128)(2,1)S(1)}, u32[]{:S(2)}, u32[]{:S(2)}) collective-permute-start(bf16[192,512]{1,0:T(8,128)(2,1)S(1)} %get-tuple-element.51), channel_id=1, source_target_pairs={{0,4},{1,5},{2,6},{3,7},{4,0},{5,1},{6,2},{7,3},{8,12},{9,13},{10,... | collective-permute-start | bytes 589832 | tf_op jit(solution)/shard_map/ppermute | solution.py:295
  116.8 40.5 %collective-permute-start.14 = (bf16[192,512]{1,0:T(8,128)(2,1)S(1)}, bf16[192,512]{1,0:T(8,128)(2,1)S(1)}, u32[]{:S(2)}, u32[]{:S(2)}) collective-permute-start(bf16[192,512]{1,0:T(8,128)(2,1)S(1)} %get-tuple-element.48), channel_id=1, source_target_pairs={{0,2},{1,3},{2,0},{3,1},{4,6},{5,7},{6,4},{7,5},{8,10},{9,11},{10,... | collective-permute-start | bytes 589832 | tf_op jit(solution)/shard_map/ppermute | solution.py:295
  123.2 3.4 %copy-start.1 = (bf16[2,4,512,1024]{3,2,1,0:T(8,128)(2,1)S(1)}, bf16[2,4,512,1024]{3,2,1,0:T(8,128)(2,1)}, u32[]{:S(2)}) copy-start(bf16[2,4,512,1024]{3,2,1,0:T(8,128)(2,1)} %refs_1_.7) | copy-start | bytes 25165828
  126.6 3.4 %copy-start.4 = (bf16[2,4,1024,512]{3,2,1,0:T(8,128)(2,1)S(1)}, bf16[2,4,1024,512]{3,2,1,0:T(8,128)(2,1)}, u32[]{:S(2)}) copy-start(bf16[2,4,1024,512]{3,2,1,0:T(8,128)(2,1)} %refs_2_.11) | copy-start | bytes 25165828
  138.7 27.9 %collective-permute-start.19 = (bf16[192,512]{1,0:T(8,128)(2,1)S(1)}, bf16[192,512]{1,0:T(8,128)(2,1)S(1)}, u32[]{:S(2)}, u32[]{:S(2)}) collective-permute-start(bf16[192,512]{1,0:T(8,128)(2,1)S(1)} %shard_map.100), channel_id=1, source_target_pairs={{0,6},{1,7},{2,4},{3,5},{4,2},{5,3},{6,0},{7,1},{8,14},{9,15},{10,... | collective-permute-start | bytes 589832 | tf_op jit(solution)/shard_map/ppermute | solution.py:295
  149.1 17.5 %collective-permute-start.17 = (bf16[192,512]{1,0:T(8,128)(2,1)S(1)}, bf16[192,512]{1,0:T(8,128)(2,1)S(1)}, u32[]{:S(2)}, u32[]{:S(2)}) collective-permute-start(bf16[192,512]{1,0:T(8,128)(2,1)S(1)} %shard_map.99), channel_id=1, source_target_pairs={{0,4},{1,5},{2,6},{3,7},{4,0},{5,1},{6,2},{7,3},{8,12},{9,13},{10,... | collective-permute-start | bytes 589832 | tf_op jit(solution)/shard_map/ppermute | solution.py:295
  166.2 5.7 %collective-permute-start.15 = (bf16[192,512]{1,0:T(8,128)(2,1)S(1)}, bf16[192,512]{1,0:T(8,128)(2,1)S(1)}, u32[]{:S(2)}, u32[]{:S(2)}) collective-permute-start(bf16[192,512]{1,0:T(8,128)(2,1)S(1)} %get-tuple-element.50), channel_id=1, source_target_pairs={{0,2},{1,3},{2,0},{3,1},{4,6},{5,7},{6,4},{7,5},{8,10},{9,11},{10,... | collective-permute-start | bytes 589832 | tf_op jit(solution)/shard_map/ppermute | solution.py:295
where the time goes:
time: 176 us; the launch traced here: 174 us
  Pallas kernels  73.5 us (42%)
  starting transfers between devices  33.7 us (19%)
  local copies, waits for them, and re-layouts  33.4 us (19%)
  waiting for transfers between devices  30.8 us (18%)
  other arithmetic  2.06 us (1%)
    pallas_call x6, Pallas kernels, run_experts(): pl.pallas_call(functools.partial(expert_kernel, sources=sources, steps=st...  52.9 us
    unnamed x42, local copies, waits for them, and re-layouts  29.5 us
    ppermute x14, starting transfers between devices, between(): lax.ppermute(value, 'lon', [(s, s ^ distance) for s in range(sectors)])  25 us
    ppermute x14, waiting for transfers between devices, between(): lax.ppermute(value, 'lon', [(s, s ^ distance) for s in range(sectors)])  22.9 us
    pallas_call x5, Pallas kernels, call(): pl.pallas_call(kernel, grid=(1,), in_specs=[spec if spec is not None else...  20.6 us
    ppermute x6, starting transfers between devices, shift(): lax.ppermute(value, ('lat', 'lon'), lat_lon_pairs(lat_step, lon_step))  8.68 us
    ppermute x6, waiting for transfers between devices, shift(): lax.ppermute(value, ('lat', 'lon'), lat_lon_pairs(lat_step, lon_step))  7.93 us
  transfers between devices with their start and end apart: 20, of which 9 were waited for; matrix products, arithmetic and copies ran while one was open for 4% of the time, Pallas kernels for 36%

commit v1 on v0

v1 whole, which is shorter than its diff:
```python
import functools
import math

import jax
import jax.numpy as jnp
import numpy as np
from jax import lax
from jax.experimental import pallas as pl
from jax.experimental.pallas import tpu as pltpu
from jax.sharding import PartitionSpec as P

WIN = 12
HALF = WIN // 2
EXPERTS = 16
LAYERS = 2
CAP = 48
EPSILON = 1e-05
LANES = 128
MIB = 1 << 20

F32 = jnp.float32
BF16 = jnp.bfloat16


def norm_rows(values, gain_row):
    centered = values - jnp.mean(values, axis=-1, keepdims=True)
    variance = jnp.mean(centered * centered, axis=-1, keepdims=True)
    return (centered * lax.rsqrt(variance + EPSILON) * gain_row).astype(BF16)


def dot(left, right, dims=((1,), (0,))):
    return lax.dot_general(left, right, (dims, ((), ())), preferred_element_type=F32)


def one_hot_columns(column, count):
    spread = lax.broadcasted_iota(jnp.int32, (column.shape[0], count), 1)
    return jnp.where(spread == column, 1.0, 0.0).astype(BF16)


def one_hot_rows(row, count):
    spread = lax.broadcasted_iota(jnp.int32, (count, row.shape[1]), 0)
    return jnp.where(spread == row, 1.0, 0.0).astype(BF16)


def slots_of(ids, order, place_ref, pair_experts):
    count = ids.shape[0]
    chosen = lax.broadcasted_iota(jnp.int32, (count, LANES), 1) == ids
    earlier = lax.broadcasted_iota(jnp.int32, (count, count), 0) > lax.broadcasted_iota(jnp.int32, (count, count), 1)
    before = dot(jnp.where(earlier, 1.0, 0.0).astype(BF16), jnp.where(chosen, 1.0, 0.0).astype(BF16))
    place = jnp.sum(jnp.where(chosen, before, 0.0), axis=1, keepdims=True).astype(jnp.int32)
    piece = lax.div(ids, pair_experts) ^ place_ref[0, 1]
    inner = lax.rem(ids, pair_experts) ^ (place_ref[0, 2] * (pair_experts // 2))
    target = (piece * pair_experts + inner) * CAP + place
    lane = lax.broadcasted_iota(jnp.int32, (count, LANES), 1)
    parts = jnp.where(lane == 0, target // 256, jnp.where(lane == 1, target % 256, jnp.where(lane == 2, ids, 1)))
    moved = dot(one_hot_columns(order, count), parts.astype(F32).astype(BF16))
    slot = jnp.where(moved[:, 3:4] > 0.5, moved[:, 0:1] * 256.0 + moved[:, 1:2], -1.0)
    row = jnp.transpose(jnp.broadcast_to(slot, (slot.shape[0], LANES)))[0:1, :]
    return moved[:, 2:3], slot, row


def route(ynorm, router, experts, target_row, piece_refs):
    logits = dot(ynorm, router, ((1,), (1,)))
    chosen = lax.broadcasted_iota(jnp.int32, logits.shape, 1) == experts.astype(jnp.int32)
    picked = jnp.sum(jnp.where(chosen, logits, 0.0), axis=1, keepdims=True)
    target = target_row.astype(jnp.int32)
    slots = piece_refs[0].shape[0]
    for index, piece_ref in enumerate(piece_refs):
        spread = one_hot_rows(target - index * slots, slots)
        piece_ref[...] = dot(spread, ynorm).astype(BF16)
    return jax.nn.sigmoid(picked)


def fetch(layer, sources, targets, arrived):
    copies = []
    for index, (source, target) in enumerate(zip(sources, targets)):
        copy = pltpu.make_async_copy(source.at[layer], target, arrived.at[index])
        copy.start()
        copies.append(copy)
    return copies


def attend(frame, layer, place_ref, temper_ref, gain_ref, wqkv_ref, wproj_ref, qkv_ref, context_ref, copies):
    total, channels = frame.shape
    heads = temper_ref.shape[1]
    width = channels // heads
    area = WIN * WIN
    windows = total // area
    group = LANES // width
    main = LANES
    rest = area - main
    lanes = group * area
    normed = norm_rows(frame, gain_ref[0, 0:1, :])
    copies[0].wait()
    qkv_ref[...] = dot(normed, wqkv_ref[...]).astype(BF16)

    lane = lax.broadcasted_iota(jnp.int32, (1, lanes), 1)
    leftover = lane >= group * main
    head_of = jnp.where(leftover, (lane - group * main) // rest, lane // main)
    query_of = jnp.where(leftover, main + (lane - group * main) % rest, lane % main)
    late = query_of >= area // 2
    seam = place_ref[0, 0] > 0
    bias_early = jnp.where(jnp.logical_and(seam, late), -1e30, 0.0)
    bias_late = jnp.where(jnp.logical_and(seam, jnp.logical_not(late)), -1e30, 0.0)
    channel_head = lax.broadcasted_iota(jnp.int32, (1, LANES), 1) // width
    keep = [jnp.where(channel_head == h, 1.0, 0.0).astype(BF16) for h in range(group)]
    keep_f = [jnp.where(channel_head == h, 1.0, 0.0) for h in range(group)]

    def one_window(window):
        rows = pl.ds(window * area, area)
        for g in range(channels // LANES):
            q = qkv_ref[rows, g * LANES : (g + 1) * LANES]
            k = qkv_ref[rows, channels + g * LANES : channels + (g + 1) * LANES]
            v = qkv_ref[rows, 2 * channels + g * LANES : 2 * channels + (g + 1) * LANES]
            stacked = jnp.concatenate(
                [q[:main] * keep[h] for h in range(group)] + [q[main:] * keep[h] for h in range(group)], axis=0
            )
            scores = dot(k, stacked, ((1,), (1,)))
            scale = jnp.zeros((1, lanes), F32)
            for h in range(group):
                factor = temper_ref[layer, g * group + h] * (math.log2(math.e) / math.sqrt(width))
                scale = jnp.where(head_of == h, factor, scale)
            if layer % 2 == 1:
                scores = jnp.concatenate(
                    [scores[: area // 2] + bias_early, scores[area // 2 :] + bias_late], axis=0
                )
            peak = jnp.max(scores, axis=0, keepdims=True)
            weights = jnp.exp2((scores - peak) * scale)
            shares = (weights * (1.0 / jnp.sum(weights, axis=0, keepdims=True))).astype(BF16)
            mixed_t = dot(v, shares, ((0,), (0,)))
            picked = jnp.concatenate(
                [mixed_t[h * width : (h + 1) * width, h * main : (h + 1) * main] for h in range(group)], axis=0
            )
            first = jnp.transpose(picked)
            tail = jnp.transpose(mixed_t[:, group * main :])
            second = tail[:rest] * keep_f[0]
            for h in range(1, group):
                second = second + tail[h * rest : (h + 1) * rest] * keep_f[h]
            context = jnp.concatenate([first, second], axis=0).astype(BF16)
            context_ref[rows, g * LANES : (g + 1) * LANES] = context

    for window in range(windows):
        one_window(window)
    copies[1].wait()
    attended = dot(context_ref[...], wproj_ref[...])
    return (frame + attended).astype(BF16)


def first_kernel(
    place_ref, temper_ref, tokens_ref, order_ref, ids_ref, gain_ref, wqkv_hbm, wproj_hbm, router_ref,
    mixed_ref, info_ref, *refs, layer, pair_experts
):
    *piece_refs, wqkv_ref, wproj_ref, qkv_ref, context_ref, arrived = refs
    copies = fetch(layer, (wqkv_hbm, wproj_hbm), (wqkv_ref, wproj_ref), arrived)
    tokens = tokens_ref[...]
    frame = dot(one_hot_columns(order_ref[...], tokens.shape[0]), tokens)
    mixed = attend(frame, layer, place_ref, temper_ref, gain_ref, wqkv_ref, wproj_ref, qkv_ref, context_ref, copies)
    mixed_ref[...] = mixed
    ynorm = norm_rows(mixed.astype(F32), gain_ref[0, 1:2, :])
    experts, slot, slot_row = slots_of(ids_ref[0], order_ref[...], place_ref, pair_experts)
    gate = route(ynorm, router_ref[0], experts, slot_row, piece_refs)
    info_ref[...] = jnp.concatenate([gate, slot], axis=1)


def slots_kernel(place_ref, ids_ref, order_ref, _, columns_ref, row_ref, *, pair_experts):
    experts, slot, slot_row = slots_of(ids_ref[0], order_ref[...], place_ref, pair_experts)
    columns_ref[...] = jnp.concatenate([experts, slot], axis=1)
    row_ref[...] = slot_row


def shifted_kernel(
    place_ref, temper_ref, own_ref, north_ref, east_ref, corner_ref, gain_ref, wqkv_hbm, wproj_hbm,
    low_ref, high_ref, low_edge_ref, high_edge_ref,
    low_scratch, high_scratch, wqkv_ref, wproj_ref, qkv_ref, context_ref, arrived, *, layer
):
    copies = fetch(layer, (wqkv_hbm, wproj_hbm), (wqkv_ref, wproj_ref), arrived)
    half, channels = own_ref.shape
    strip = HALF * HALF
    part = WIN * HALF
    edge = east_ref.shape[0]
    low_scratch[0:half] = own_ref[...].astype(F32)
    low_scratch[half : half + edge] = east_ref[...].astype(F32)
    high_scratch[0:half] = north_ref[...].astype(F32)
    high_scratch[half : half + edge] = corner_ref[...].astype(F32)
    pieces = []
    for window in range(half // part):
        start = strip + window * part
        pieces += [low_scratch[start : start + part], high_scratch[start : start + part]]
    frame = jnp.concatenate(pieces, axis=0)
    mixed = attend(frame, layer, place_ref, temper_ref, gain_ref, wqkv_ref, wproj_ref, qkv_ref, context_ref, copies)
    mixed = mixed.astype(F32)
    low, high = split_halves(mixed)
    low_ref[...] = low.astype(BF16)
    high_ref[...] = high.astype(BF16)
    low_edge_ref[...] = low[half - edge :].astype(BF16)
    high_edge_ref[...] = high[half - edge :].astype(BF16)


def split_halves(rows):
    part = WIN * HALF
    pieces = [rows[start : start + part] for start in range(0, rows.shape[0], part)]
    return jnp.concatenate(pieces[0::2], axis=0), jnp.concatenate(pieces[1::2], axis=0)


def route_kernel(own_ref, south_ref, west_ref, corner_ref, columns_ref, row_ref, gain_ref, router_ref,
                 rows_ref, info_ref, *piece_refs):
    mixed = jnp.concatenate([own_ref[...], south_ref[...], west_ref[...], corner_ref[...]], axis=0)
    rows_ref[...] = mixed
    ynorm = norm_rows(mixed.astype(F32), gain_ref[0, 1:2, :])
    gate = route(ynorm, router_ref[0], columns_ref[:, 0:1], row_ref[...], piece_refs)
    info_ref[...] = jnp.concatenate([gate, columns_ref[:, 1:2]], axis=1)


def expert_rows(piece_refs, out_refs, block, first, second, carried, last):
    rows = jnp.concatenate([ref[block, :] for ref in piece_refs], axis=0)
    hidden = jax.nn.gelu(dot(rows, first())).astype(BF16)
    part = dot(hidden, second())
    total = part if carried is None else carried + part
    if last:
        for index, ref in enumerate(out_refs):
            ref[block, :] = total[index * CAP : (index + 1) * CAP].astype(BF16)
    return total


def near_kernel(*refs, sources, plan, layer):
    piece_hbm = refs[:sources]
    weights = refs[sources : sources + 4]
    out_refs = refs[sources + 4 : 2 * sources + 4]
    first_ref, second_ref, piece_ref, arrived, here = refs[2 * sources + 4 :]
    moves = []
    for index, ref in enumerate(piece_hbm):
        move = pltpu.make_async_copy(ref, piece_ref.at[index], here.at[index])
        move.start()
        moves.append(move)
    copies = []
    for unit, (which, entry, _) in enumerate(plan):
        pair = []
        for side, target in enumerate((first_ref, second_ref)):
            copy = pltpu.make_async_copy(
                weights[2 * which + side].at[layer, entry], target.at[unit], arrived.at[side, unit]
            )
            copy.start()
            pair.append(copy)
        copies.append(pair)
    for move in moves:
        move.wait()
    totals = {}
    last = {place: unit for unit, (_, _, place) in enumerate(plan)}
    pieces = [piece_ref.at[index] for index in range(sources)]

    def wait_for(unit, side, ref):
        copies[unit][side].wait()
        return ref[unit]

    for unit, (_, _, place) in enumerate(plan):
        block = slice(place * CAP, (place + 1) * CAP)
        totals[place] = expert_rows(
            pieces, out_refs, block,
            functools.partial(wait_for, unit, 0, first_ref), functools.partial(wait_for, unit, 1, second_ref),
            totals.get(place), last[place] == unit,
        )


def away_kernel(*refs, sources, plan, base):
    piece_hbm = refs[:sources]
    first_ref, second_ref = refs[sources : sources + 2]
    out_refs = refs[sources + 2 : 2 * sources + 2]
    piece_ref, here = refs[2 * sources + 2 :]
    size = out_refs[0].shape[0]
    moves = []
    for index, ref in enumerate(piece_hbm):
        move = pltpu.make_async_copy(ref.at[pl.ds(base * CAP, size)], piece_ref.at[index], here.at[index])
        move.start()
        moves.append(move)
    for move in moves:
        move.wait()
    totals = {}
    last = {place: unit for unit, place in plan}
    pieces = [piece_ref.at[index] for index in range(sources)]
    for unit, place in plan:
        block = slice((place - base) * CAP, (place - base + 1) * CAP)
        totals[place] = expert_rows(
            pieces, out_refs, block, lambda unit=unit: first_ref[unit], lambda unit=unit: second_ref[unit],
            totals.get(place), last[place] == unit,
        )


def gathered_state(mixed_ref, info_ref, piece_refs):
    produced = jnp.concatenate([ref[...] for ref in piece_refs], axis=0)
    spread = one_hot_columns(info_ref[:, 1:2].astype(jnp.int32), produced.shape[0])
    combined = dot(spread, produced)
    return (mixed_ref[...].astype(F32) + info_ref[:, 0:1] * combined).astype(BF16)


def combine_kernel(mixed_ref, info_ref, *refs):
    *piece_refs, north_ref, own_ref, corner_ref, east_ref = refs
    state = gathered_state(mixed_ref, info_ref, piece_refs).astype(F32)
    low, high = split_halves(state)
    edge = east_ref.shape[0]
    north_ref[...] = low.astype(BF16)
    own_ref[...] = high.astype(BF16)
    corner_ref[...] = low[:edge].astype(BF16)
    east_ref[...] = high[:edge].astype(BF16)


def last_kernel(mixed_ref, info_ref, order_ref, *refs):
    *piece_refs, out_ref = refs
    state = gathered_state(mixed_ref, info_ref, piece_refs)
    out_ref[...] = dot(one_hot_rows(order_ref[...], out_ref.shape[0]), state).astype(BF16)


def whole(shape):
    return pl.BlockSpec(shape, lambda *_: (0,) * len(shape))


def of_layer(array, layer):
    rest = array.shape[1:]
    return pl.BlockSpec((1,) + rest, lambda *_: (layer,) + (0,) * len(rest))


SCALARS = pl.BlockSpec(memory_space=pltpu.SMEM)
IN_HBM = pl.BlockSpec(memory_space=pltpu.HBM)
IN_VMEM = pl.BlockSpec(memory_space=pltpu.VMEM)
SMALL = 1 << 14


def keep_out(array):
    if array.size < SMALL:
        return array
    return pltpu.with_memory_space_constraint(array, pltpu.HBM)


def call(kernel, ins, outs, scratch=(), limit=40, flops=0):
    arrays = [array for array, _ in ins]
    size = sum(a.size * a.dtype.itemsize for a in arrays)
    return pl.pallas_call(
        kernel,
        grid=(1,),
        in_specs=[spec if spec is not None else whole(array.shape) for array, spec in ins],
        out_specs=[whole(o.shape) for o in outs],
        out_shape=outs,
        scratch_shapes=list(scratch),
        compiler_params=pltpu.CompilerParams(vmem_limit_bytes=limit * MIB),
        cost_estimate=pl.CostEstimate(flops=flops, bytes_accessed=size, transcendentals=0),
    )(*[keep_out(array) if spec is not SCALARS else array for array, spec in ins])


def run_near(pieces, weights, plan, layer):
    sources = len(pieces)
    slots, channels = pieces[0].shape
    units = weights[0].shape[3]
    held = [pltpu.VMEM((len(plan), channels, units), BF16), pltpu.VMEM((len(plan), units, channels), BF16)]
    outs = pl.pallas_call(
        functools.partial(near_kernel, sources=sources, plan=plan, layer=layer),
        in_specs=[IN_HBM] * (sources + 4),
        out_specs=[IN_VMEM] * (sources + 2),
        out_shape=[jax.ShapeDtypeStruct(p.shape, BF16) for p in pieces] + held,
        scratch_shapes=[
            pltpu.VMEM((sources, slots, channels), BF16),
            pltpu.SemaphoreType.DMA((2, len(plan))),
            pltpu.SemaphoreType.DMA((sources,)),
        ],
        compiler_params=pltpu.CompilerParams(vmem_limit_bytes=24 * MIB),
        cost_estimate=pl.CostEstimate(
            flops=4_000_000_000, bytes_accessed=len(plan) * 4 * channels * units, transcendentals=0
        ),
    )(*[keep_out(p) for p in pieces], *[keep_out(w) for w in weights])
    return outs[:sources], outs[sources:]


def run_away(pieces, held, plan, layer):
    sources = len(pieces)
    channels = pieces[0].shape[1]
    places = [place for _, place in plan]
    base = min(places)
    size = (max(places) - base + 1) * CAP
    return pl.pallas_call(
        functools.partial(away_kernel, sources=sources, plan=plan, base=base),
        in_specs=[IN_HBM] * sources + [IN_VMEM] * 2,
        out_specs=[IN_VMEM] * sources,
        out_shape=[jax.ShapeDtypeStruct((size, channels), BF16)] * sources,
        scratch_shapes=[pltpu.VMEM((sources, size, channels), BF16), pltpu.SemaphoreType.DMA((sources,))],
        compiler_params=pltpu.CompilerParams(vmem_limit_bytes=24 * MIB),
        cost_estimate=pl.CostEstimate(flops=3_000_000_000, bytes_accessed=1 << 20, transcendentals=0),
    )(*[keep_out(p) for p in pieces], *held)


def lat_lon_pairs(lat_step, lon_step):
    bands, sectors = lax.axis_size("lat"), lax.axis_size("lon")
    pairs = []
    for i in range(bands):
        for j in range(sectors):
            target = (i + lat_step) % bands * sectors + (j + lon_step) % sectors
            pairs.append((i * sectors + j, target))
    return pairs


def shift(value, lat_step, lon_step):
    return lax.ppermute(value, ("lat", "lon"), lat_lon_pairs(lat_step, lon_step))


def between(value, distance):
    sectors = lax.axis_size("lon")
    return lax.ppermute(value, "lon", [(s, s ^ distance) for s in range(sectors)])


def per_device(tokens, expert_ids, norm_gain, weight_qkv, weight_proj, temper, router, weight_in, weight_out):
    row_count, col_count, channels = tokens.shape
    token_count = row_count * col_count
    half = token_count // 2
    strip = HALF * HALF
    part = WIN * HALF
    edge = 48
    sectors = lax.axis_size("lon")
    local = weight_in.shape[1]
    pieces_count = sectors // 2
    pair_experts = EXPERTS // pieces_count
    slots = pair_experts * CAP
    lon = lax.axis_index("lon")
    lat = lax.axis_index("lat")

    far_in = between(weight_in, 1)
    far_out = between(weight_out, 1)

    router = router.transpose(0, 2, 1)
    ids = expert_ids.reshape(LAYERS, token_count, 1)
    seam = jnp.where(lat == lax.axis_size("lat") - 1, 1, 0)
    place = jnp.stack([seam, lon // 2, lon % 2]).astype(jnp.int32).reshape(1, 3)

    grid = np.arange(token_count, dtype=np.int32).reshape(row_count // HALF, HALF, col_count // HALF, HALF)
    halves = grid.transpose(0, 2, 1, 3).reshape(2, half)
    order0 = halves.reshape(2, half // part, part).transpose(1, 0, 2).reshape(token_count)
    gap = np.full(strip, -1, np.int32)
    lead = np.full(edge - strip, -1, np.int32)
    low, high = halves
    order1 = np.concatenate([high[strip:], gap, low[strip:], gap, lead, high[:strip], lead, low[:strip]])
    rows1 = order1.shape[0]
    order0, order1 = jnp.asarray(order0), jnp.asarray(order1)

    shape = jax.ShapeDtypeStruct
    piece_shapes = [shape((slots, channels), BF16)] * pieces_count
    attention_scratch = [
        pltpu.VMEM((channels, 3 * channels), BF16), pltpu.VMEM((channels, channels), BF16),
        pltpu.VMEM((token_count, 3 * channels), BF16), pltpu.VMEM((token_count, channels), BF16),
        pltpu.SemaphoreType.DMA((2,)),
    ]

    layer = 0
    mixed, info, *pieces = call(
        functools.partial(first_kernel, layer=layer, pair_experts=pair_experts),
        [(place, SCALARS), (temper, SCALARS), (tokens.reshape(token_count, channels), None),
         (order0[:, None], None), (ids, of_layer(ids, layer)),
         (norm_gain, of_layer(norm_gain, layer)), (weight_qkv, IN_HBM), (weight_proj, IN_HBM),
         (router, of_layer(router, layer))],
        [shape((token_count, channels), BF16), shape((token_count, 2), F32)] + piece_shapes,
        attention_scratch,
        flops=4_000_000_000,
    )
    columns1, row1 = call(
        functools.partial(slots_kernel, pair_experts=pair_experts),
        [(place, SCALARS), (ids, of_layer(ids, 1)), (order1[:, None], None), (info, IN_HBM)],
        [shape((rows1, 2), F32), shape((1, rows1), F32)],
        flops=500_000_000,
    )
    produced = moe(pieces, weight_in, weight_out, far_in, far_out, layer)
    north, own, corner, east = call(
        combine_kernel,
        [(mixed, None), (info, None)] + [(p, None) for p in produced],
        [shape((half, channels), BF16)] * 2 + [shape((edge, channels), BF16)] * 2,
        flops=1_000_000_000,
    )

    layer = 1
    north = shift(north, -1, 0)
    east = shift(east, 0, -1)
    corner = shift(corner, -1, -1)
    low, high, low_edge, high_edge = call(
        functools.partial(shifted_kernel, layer=layer),
        [(place, SCALARS), (temper, SCALARS), (own, None), (north, None), (east, None), (corner, None),
         (norm_gain, of_layer(norm_gain, layer)), (weight_qkv, IN_HBM), (weight_proj, IN_HBM)],
        [shape((half, channels), BF16)] * 2 + [shape((edge, channels), BF16)] * 2,
        [pltpu.VMEM((half + edge, channels), F32)] * 2 + attention_scratch,
        flops=3_000_000_000,
    )
    high = shift(high, 1, 0)
    low_edge = shift(low_edge, 0, 1)
    high_edge = shift(high_edge, 1, 1)
    mixed, info, *pieces = call(
        route_kernel,
        [(low, None), (high, None), (low_edge, None), (high_edge, None), (columns1, None), (row1, None),
         (norm_gain, of_layer(norm_gain, layer)), (router, of_layer(router, layer))],
        [shape((rows1, channels), BF16), shape((rows1, 2), F32)] + piece_shapes,
        flops=1_000_000_000,
    )
    produced = moe(pieces, weight_in, weight_out, far_in, far_out, layer)
    (out,) = call(
        last_kernel,
        [(mixed, None), (info, None), (order1[None, :], None)] + [(p, None) for p in produced],
        [shape((token_count, channels), BF16)],
        flops=1_000_000_000,
    )
    return out.reshape(row_count, col_count, channels)


def moe(pieces, own_in, own_out, far_in, far_out, layer):
    local = own_in.shape[1]
    count = len(pieces)
    if local > 1:
        plan = [(0, entry, entry // 2) for entry in range(local)]
        plan += [(1, entry, local // 2 + entry // 2) for entry in range(local)]
    else:
        plan = [(0, 0, 0), (1, 0, 0)]
    places = sorted({place for _, _, place in plan})
    groups = [places[: len(places) // 2], places[len(places) // 2 :]] if len(places) > 1 else [places]
    near, away = range(count // 2), range(count // 2, count)
    arrived = {k: between(pieces[k], 2 * k) for k in away}
    arrived.update({k: between(pieces[k], 2 * k) if k else pieces[k] for k in near})
    back = {k: [] for k in range(count)}
    outs, held = run_near([arrived[k] for k in near], [own_in, own_out, far_in, far_out], plan, layer)
    for k, value in zip(near, outs):
        back[k].append(between(value, 2 * k) if k else value)
    for group in groups:
        units = [(unit, place) for unit, (_, _, place) in enumerate(plan) if place in group]
        outs = run_away([arrived[k] for k in away], held, units, layer)
        for k, value in zip(away, outs):
            back[k].append(between(value, 2 * k))
    return [value for k in range(count) for value in back[k]]


def solution(mesh):
    in_specs = (
        P("lat", "lon", None),
        P(None, "lat", "lon", None, None),
        P(),
        P(),
        P(),
        P(),
        P(),
        P(None, "lon", None, None),
        P(None, "lon", None, None),
    )
    out_specs = P("lat", "lon", None)
    return jax.shard_map(per_device, mesh=mesh, in_specs=in_specs, out_specs=out_specs, check_vma=False)
```

time: 176 us -> 149 us (0.85)
  local copies, waits for them, and re-layouts: 33.4 us -> 11.4 us
  Pallas kernels: 73.5 us -> 64.5 us
  waiting for transfers between devices: 30.8 us -> 35.3 us
  starting transfers between devices: 33.7 us -> 35.8 us
    pallas_call x6, Pallas kernels: 52.9 us -> 32.1 us  [the longest x2 21.7 us: run_near(): pl.pallas_call(functools.partial(near_kernel, sources=sources, plan=plan,...]
    unnamed x42 -> x74, local copies, waits for them, and re-layouts: 29.5 us -> 11.2 us
    pallas_call x5 -> x6, Pallas kernels: 20.6 us -> 32.4 us  [call(): pl.pallas_call(kernel, grid=(1,), in_specs=[spec if spec is not None else...]
    ppermute x14 -> x18, waiting for transfers between devices: 22.9 us -> 29.6 us  [between(): lax.ppermute(value, 'lon', [(s, s ^ distance) for s in range(sectors)])]
    ppermute x6, waiting for transfers between devices: 7.93 us -> 5.7 us  [shift(): lax.ppermute(value, ('lat', 'lon'), lat_lon_pairs(lat_step, lon_step))]
    slice x24 -> x0, local copies, waits for them, and re-layouts: 1.98 us -> none  [the longest x2 0.74 us: per_device(): target1, experts1 = (split_order(target[1], -1), split_order(ids[1], -1))]
    ppermute x14 -> x18, starting transfers between devices: 25 us -> 26.1 us  [between(): lax.ppermute(value, 'lon', [(s, s ^ distance) for s in range(sectors)])]
  transfers between devices with their start and end apart: 20 -> 24, of which waited for: 9 -> 9; matrix products, arithmetic and copies ran while one was open for 4% -> 1% of each run, Pallas kernels for 36% -> 30%
where the time goes in v1:
time: 149 us; the launch traced here: 148 us
  Pallas kernels  64.5 us (43%)
  starting transfers between devices  35.8 us (24%)
  waiting for transfers between devices  35.3 us (24%)
  local copies, waits for them, and re-layouts  11.4 us (8%)
    pallas_call x6, Pallas kernels, call(): pl.pallas_call(kernel, grid=(1,), in_specs=[spec if spec is not None else...  32.4 us
    ppermute x18, waiting for transfers between devices, between(): lax.ppermute(value, 'lon', [(s, s ^ distance) for s in range(sectors)])  29.6 us
    ppermute x18, starting transfers between devices, between(): lax.ppermute(value, 'lon', [(s, s ^ distance) for s in range(sectors)])  26.1 us
    pallas_call x2, Pallas kernels, run_near(): pl.pallas_call(functools.partial(near_kernel, sources=sources, plan=plan,...  21.7 us
    unnamed x74, local copies, waits for them, and re-layouts  11.2 us
    pallas_call x4, Pallas kernels, run_away(): pl.pallas_call(functools.partial(away_kernel, sources=sources, plan=plan,...  10.5 us
    ppermute x6, starting transfers between devices, shift(): lax.ppermute(value, ('lat', 'lon'), lat_lon_pairs(lat_step, lon_step))  9.68 us
    ppermute x6, waiting for transfers between devices, shift(): lax.ppermute(value, ('lat', 'lon'), lat_lon_pairs(lat_step, lon_step))  5.7 us
  transfers between devices with their start and end apart: 24, of which 9 were waited for; matrix products, arithmetic and copies ran while one was open for 1% of the time, Pallas kernels for 30%

profile of v1, /device:TPU:0, one launch (start us, length us, event | category | flops | bytes accessed | tf_op | source)
XLA Modules:
  0.0 148.2 jit_solution(11767779494523636568)
XLA Ops:
  0.0 0.5 collective-permute-start.1
  0.5 0.1 collective-permute-start.2
  0.5 0.7 reduce
  1.2 0.2 reshape.16.ids_ref
  1.5 0.1 add_bitcast_fusion.place_ref
  1.5 0.7 copy-done.4
  2.2 0.7 copy-done.6
  2.9 1.0 copy-done.9
  3.9 12.6 %shard_map.109 = (bf16[576,512]{1,0:T(8,128)(2,1)S(1)}, f32[576,2]{1,0:T(8,128)S(1)}, bf16[192,512]{1,0:T(8,128)(2,1)S(1)}, bf16[192,512]{1,0:T(8,128)(2,1)S(1)}...) custom-call(s32[1,3]{1,0:T(1,128)S(1)} %add_bitcast_fusion.place_ref, f32[2,16]{1,0:T(2,128)S(1)} %copy-done.6, ...), custom_call_target="tpu_custom_call" | custom-call | flops 4000000000 | bytes 4832140 | tf_op jit(solution)/shard_map/pallas_call | solution.py:336
  16.5 0.7 copy-done.1
  17.2 3.0 %collective-permute-start = (bf16[192,512]{1,0:T(8,128)(2,1)S(1)}, bf16[192,512]{1,0:T(8,128)(2,1)S(1)}, u32[]{:S(2)}, u32[]{:S(2)}) collective-permute-start(bf16[192,512]{1,0:T(8,128)(2,1)S(1)} %get-tuple-element.46), channel_id=1, source_target_pairs={{0,2},{1,3},{2,0},{3,1},{4,6},{5,7},{6,4},{7,5},{8,10},{9,11},{10,... | collective-permute-start | bytes 589832 | tf_op jit(solution)/shard_map/ppermute | solution.py:404
  20.2 2.6 %collective-permute-start.4 = (bf16[192,512]{1,0:T(8,128)(2,1)S(1)}, bf16[192,512]{1,0:T(8,128)(2,1)S(1)}, u32[]{:S(2)}, u32[]{:S(2)}) collective-permute-start(bf16[192,512]{1,0:T(8,128)(2,1)S(1)} %get-tuple-element.49), channel_id=1, source_target_pairs={{0,4},{1,5},{2,6},{3,7},{4,0},{5,1},{6,2},{7,3},{8,12},{9,13},{10,... | collective-permute-start | bytes 589832 | tf_op jit(solution)/shard_map/ppermute | solution.py:404
  22.8 6.0 %collective-permute-done.refs_1_ = bf16[192,512]{1,0:T(8,128)(2,1)S(1)} collective-permute-done((bf16[192,512]{1,0:T(8,128)(2,1)S(1)}, bf16[192,512]{1,0:T(8,128)(2,1)S(1)}, u32[]{:S(2)}, u32[]{:S(2)}) %collective-permute-start) | collective-permute-done | bytes 196640 | tf_op jit(solution)/shard_map/ppermute | solution.py:404
  28.8 0.7 copy-done.19
  29.5 10.9 %shard_map.110 = (bf16[192,512]{1,0:T(8,128)(2,1)S(1)}, bf16[192,512]{1,0:T(8,128)(2,1)S(1)}, bf16[8,512,1024]{2,1,0:T(8,128)(2,1)S(1)}, bf16[8,1024,512]{2,1,0:T(8,128)(2,1)S(1)}) custom-call(bf16[192,512]{1,0:T(8,128)(2,1)} %copy-done.1, bf16[192,512]{1,0:T(8,128)(2,1)} %copy-done.19, bf16[2,4,512,1024]{3,2,1,0:T(8,128)(2,1)} %refs_2_.3, ...), custom_call_target="tpu_custom_call" | custom-call | flops 4000000000 | bytes 16777216 | tf_op jit(solution)/shard_map/pallas_call | solution.py:353
  40.5 0.7 copy-done.15
  41.2 0.1 copy-done.16
  41.3 2.6 %shard_map.112 = (bf16[96,512]{1,0:T(8,128)(2,1)S(1)}, bf16[96,512]{1,0:T(8,128)(2,1)S(1)}) custom-call(bf16[192,512]{1,0:T(8,128)(2,1)} %copy-done.15, bf16[192,512]{1,0:T(8,128)(2,1)} %copy-done.16, bf16[8,512,1024]{2,1,0:T(8,128)(2,1)S(1)} %get-tuple-element.51.refs_2_, bf16[8,1024,512]{2,1,0:T(8,128)(2,1)S(1)} %get-tuple-element.52.refs_3_), custom_call_target="tpu_custom_call" | custom-call | flops 3000000000 | bytes 1048576 | tf_op jit(solution)/shard_map/pallas_call | solution.py:377
  43.9 1.4 collective-permute-start.7
  45.3 2.0 %collective-permute-start.9 = (bf16[96,512]{1,0:T(8,128)(2,1)S(1)}, bf16[96,512]{1,0:T(8,128)(2,1)S(1)}, u32[]{:S(2)}, u32[]{:S(2)}) collective-permute-start(bf16[96,512]{1,0:T(8,128)(2,1)S(1)} %get-tuple-element.56), channel_id=1, source_target_pairs={{0,6},{1,7},{2,4},{3,5},{4,2},{5,3},{6,0},{7,1},{8,14},{9,15},{10,... | collective-permute-start | bytes 294920 | tf_op jit(solution)/shard_map/ppermute | solution.py:404
  47.3 0.5 collective-permute-start.3
  47.8 2.6 %shard_map.111 = (bf16[96,512]{1,0:T(8,128)(2,1)S(1)}, bf16[96,512]{1,0:T(8,128)(2,1)S(1)}) custom-call(bf16[192,512]{1,0:T(8,128)(2,1)} %copy-done.15, bf16[192,512]{1,0:T(8,128)(2,1)} %copy-done.16, bf16[8,512,1024]{2,1,0:T(8,128)(2,1)S(1)} %get-tuple-element.51.refs_2_, bf16[8,1024,512]{2,1,0:T(8,128)(2,1)S(1)} %get-tuple-element.52.refs_3_), custom_call_target="tpu_custom_call" | custom-call | flops 3000000000 | bytes 1048576 | tf_op jit(solution)/shard_map/pallas_call | solution.py:377
  50.4 2.0 %collective-permute-start.6 = (bf16[96,512]{1,0:T(8,128)(2,1)S(1)}, bf16[96,512]{1,0:T(8,128)(2,1)S(1)}, u32[]{:S(2)}, u32[]{:S(2)}) collective-permute-start(bf16[96,512]{1,0:T(8,128)(2,1)S(1)} %get-tuple-element.53), channel_id=1, source_target_pairs={{0,4},{1,5},{2,6},{3,7},{4,0},{5,1},{6,2},{7,3},{8,12},{9,13},{10,... | collective-permute-start | bytes 294920 | tf_op jit(solution)/shard_map/ppermute | solution.py:404
  52.4 2.0 %collective-permute-start.8 = (bf16[96,512]{1,0:T(8,128)(2,1)S(1)}, bf16[96,512]{1,0:T(8,128)(2,1)S(1)}, u32[]{:S(2)}, u32[]{:S(2)}) collective-permute-start(bf16[96,512]{1,0:T(8,128)(2,1)S(1)} %get-tuple-element.55), channel_id=1, source_target_pairs={{0,6},{1,7},{2,4},{3,5},{4,2},{5,3},{6,0},{7,1},{8,14},{9,15},{10,... | collective-permute-start | bytes 294920 | tf_op jit(solution)/shard_map/ppermute | solution.py:404
  54.4 7.9 %collective-permute-done.6.refs_2_ = bf16[96,512]{1,0:T(8,128)(2,1)S(1)} collective-permute-done((bf16[96,512]{1,0:T(8,128)(2,1)S(1)}, bf16[96,512]{1,0:T(8,128)(2,1)S(1)}, u32[]{:S(2)}, u32[]{:S(2)}) %collective-permute-start.6) | collective-permute-done | bytes 98336 | tf_op jit(solution)/shard_map/ppermute | solution.py:404
  62.3 0.6 copy-done.29
  62.9 0.1 copy-done.24
  63.0 2.1 %shard_map.113 = (bf16[288,512]{1,0:T(8,128)(2,1)S(1)}, bf16[288,512]{1,0:T(8,128)(2,1)S(1)}, bf16[48,512]{1,0:T(8,128)(2,1)S(1)}, bf16[48,512]{1,0:T(8,128)(2,1)S(1)}) custom-call(bf16[576,512]{1,0:T(8,128)(2,1)} %copy-done.12, f32[576,2]{1,0:T(8,128)S(1)} %get-tuple-element.44.info_ref._, bf16[192,512]{1,0:T(8,128)(2,1)} %copy-done.2, ...), custom_call_target="tpu_custom_call" | custom-call | flops 1000000000 | bytes 1380864 | tf_op jit(solution)/shard_map/pallas_call | solution.py:336
  65.1 0.7 copy-done.13
  65.8 2.5 %collective-permute-start.10 = (bf16[288,512]{1,0:T(8,128)(2,1)S(1)}, bf16[288,512]{1,0:T(8,128)(2,1)S(1)}, u32[]{:S(2)}, u32[]{:S(2)}) collective-permute-start(bf16[288,512]{1,0:T(8,128)(2,1)S(1)} %get-tuple-element.58), channel_id=1, source_target_pairs={{0,24},{1,25},{2,26},{3,27},{4,28},{5,29},{6,30},{7,31},{8,0},{9,1... | collective-permute-start | bytes 884744 | tf_op jit(solution)/shard_map/ppermute | solution.py:399
  68.3 2.3 %collective-permute-start.12 = (bf16[48,512]{1,0:T(8,128)(2,1)S(1)}, bf16[48,512]{1,0:T(8,128)(2,1)S(1)}, u32[]{:S(2)}, u32[]{:S(2)}) collective-permute-start(bf16[48,512]{1,0:T(8,128)(2,1)S(1)} %get-tuple-element.60), channel_id=1, source_target_pairs={{0,31},{1,24},{2,25},{3,26},{4,27},{5,28},{6,29},{7,30},{8,7},{9,0... | collective-permute-start | bytes 147464 | tf_op jit(solution)/shard_map/ppermute | solution.py:399
  70.6 1.8 %collective-permute-done.12.corner_ref = bf16[48,512]{1,0:T(8,128)(2,1)S(1)} collective-permute-done((bf16[48,512]{1,0:T(8,128)(2,1)S(1)}, bf16[48,512]{1,0:T(8,128)(2,1)S(1)}, u32[]{:S(2)}, u32[]{:S(2)}) %collective-permute-start.12) | collective-permute-done | bytes 49184 | tf_op jit(solution)/shard_map/ppermute | solution.py:399
  72.4 2.1 %collective-permute-done.10.north_ref = bf16[288,512]{1,0:T(8,128)(2,1)S(1)} collective-permute-done((bf16[288,512]{1,0:T(8,128)(2,1)S(1)}, bf16[288,512]{1,0:T(8,128)(2,1)S(1)}, u32[]{:S(2)}, u32[]{:S(2)}) %collective-permute-start.10) | collective-permute-done | bytes 294944 | tf_op jit(solution)/shard_map/ppermute | solution.py:399
  74.5 0.7 copy-done.22
  75.3 9.3 %shard_map.114 = (bf16[288,512]{1,0:T(8,128)(2,1)S(1)}, bf16[288,512]{1,0:T(8,128)(2,1)S(1)}, bf16[48,512]{1,0:T(8,128)(2,1)S(1)}, bf16[48,512]{1,0:T(8,128)(2,1)S(1)}) custom-call(s32[1,3]{1,0:T(1,128)S(1)} %add_bitcast_fusion.place_ref, f32[2,16]{1,0:T(2,128)S(1)} %copy-done.7, bf16[288,512]{1,0:T(8,128)(2,1)} %copy-done.13, bf16[288,512]{1,0:T(8,128)(2,1)} %copy-done.22, ...), custom_call_target="tpu_custom_call" | custom-call | flops 3000000000 | bytes 4890764 | tf_op jit(solution)/shard_map/pallas_call | solution.py:336
  84.6 1.9 %collective-permute-start.13 = (bf16[288,512]{1,0:T(8,128)(2,1)S(1)}, bf16[288,512]{1,0:T(8,128)(2,1)S(1)}, u32[]{:S(2)}, u32[]{:S(2)}) collective-permute-start(bf16[288,512]{1,0:T(8,128)(2,1)S(1)} %get-tuple-element.62), channel_id=1, source_target_pairs={{0,8},{1,9},{2,10},{3,11},{4,12},{5,13},{6,14},{7,15},{8,16},{9,17... | collective-permute-start | bytes 884744 | tf_op jit(solution)/shard_map/ppermute | solution.py:399
  86.5 3.0 %collective-permute-start.15 = (bf16[48,512]{1,0:T(8,128)(2,1)S(1)}, bf16[48,512]{1,0:T(8,128)(2,1)S(1)}, u32[]{:S(2)}, u32[]{:S(2)}) collective-permute-start(bf16[48,512]{1,0:T(8,128)(2,1)S(1)} %get-tuple-element.64), channel_id=1, source_target_pairs={{0,9},{1,10},{2,11},{3,12},{4,13},{5,14},{6,15},{7,8},{8,17},{9,18... | collective-permute-start | bytes 147464 | tf_op jit(solution)/shard_map/ppermute | solution.py:399
  89.5 2.6 %shard_map.115 = (f32[672,2]{1,0:T(8,128)S(1)}, f32[1,672]{1,0:T(1,128)S(1)}) custom-call(s32[1,3]{1,0:T(1,128)S(1)} %add_bitcast_fusion.place_ref, s32[2,576,1]{2,1,0:T(8,128)S(1)} %reshape.16.ids_ref, s32[672,1]{1,0:T(8,128)S(1)} %copy-done.8, f32[576,2]{1,0:T(8,128)S(1)} %get-tuple-element.44.info_ref._), custom_call_target="tpu_custom_call" | custom-call | flops 500000000 | bytes 11916 | tf_op jit(solution)/shard_map/pallas_call | solution.py:336
  92.1 1.7 %collective-permute-done.15.corner_ref = bf16[48,512]{1,0:T(8,128)(2,1)S(1)} collective-permute-done((bf16[48,512]{1,0:T(8,128)(2,1)S(1)}, bf16[48,512]{1,0:T(8,128)(2,1)S(1)}, u32[]{:S(2)}, u32[]{:S(2)}) %collective-permute-start.15) | collective-permute-done | bytes 49184 | tf_op jit(solution)/shard_map/ppermute | solution.py:399
  93.7 0.1 collective-permute-done.13.south_ref
  93.8 0.5 copy-done.34
  94.4 0.2 copy-done.21
  94.5 2.4 %shard_map.116 = (bf16[672,512]{1,0:T(8,128)(2,1)S(1)}, f32[672,2]{1,0:T(8,128)S(1)}, bf16[192,512]{1,0:T(8,128)(2,1)S(1)}, bf16[192,512]{1,0:T(8,128)(2,1)S(1)}...) custom-call(bf16[288,512]{1,0:T(8,128)(2,1)} %copy-done.14, bf16[288,512]{1,0:T(8,128)(2,1)} %copy-done.21, ...), custom_call_target="tpu_custom_call" | custom-call | flops 1000000000 | bytes 737152 | tf_op jit(solution)/shard_map/pallas_call | solution.py:336
  97.0 0.7 copy-done
  97.6 0.9 copy-done.11
  98.5 2.1 %collective-permute-start.16 = (bf16[192,512]{1,0:T(8,128)(2,1)S(1)}, bf16[192,512]{1,0:T(8,128)(2,1)S(1)}, u32[]{:S(2)}, u32[]{:S(2)}) collective-permute-start(bf16[192,512]{1,0:T(8,128)(2,1)S(1)} %get-tuple-element.70), channel_id=1, source_target_pairs={{0,2},{1,3},{2,0},{3,1},{4,6},{5,7},{6,4},{7,5},{8,10},{9,11},{10,... | collective-permute-start | bytes 589832 | tf_op jit(solution)/shard_map/ppermute | solution.py:404
  100.6 2.4 %collective-permute-start.18 = (bf16[192,512]{1,0:T(8,128)(2,1)S(1)}, bf16[192,512]{1,0:T(8,128)(2,1)S(1)}, u32[]{:S(2)}, u32[]{:S(2)}) collective-permute-start(bf16[192,512]{1,0:T(8,128)(2,1)S(1)} %get-tuple-element.73), channel_id=1, source_target_pairs={{0,4},{1,5},{2,6},{3,7},{4,0},{5,1},{6,2},{7,3},{8,12},{9,13},{10,... | collective-permute-start | bytes 589832 | tf_op jit(solution)/shard_map/ppermute | solution.py:404
  103.0 6.6 %collective-permute-done.16.refs_1_ = bf16[192,512]{1,0:T(8,128)(2,1)S(1)} collective-permute-done((bf16[192,512]{1,0:T(8,128)(2,1)S(1)}, bf16[192,512]{1,0:T(8,128)(2,1)S(1)}, u32[]{:S(2)}, u32[]{:S(2)}) %collective-permute-start.16) | collective-permute-done | bytes 196640 | tf_op jit(solution)/shard_map/ppermute | solution.py:404
  109.6 0.7 copy-done.20
  110.3 10.7 %shard_map.117 = (bf16[192,512]{1,0:T(8,128)(2,1)S(1)}, bf16[192,512]{1,0:T(8,128)(2,1)S(1)}, bf16[8,512,1024]{2,1,0:T(8,128)(2,1)S(1)}, bf16[8,1024,512]{2,1,0:T(8,128)(2,1)S(1)}) custom-call(bf16[192,512]{1,0:T(8,128)(2,1)} %copy-done, bf16[192,512]{1,0:T(8,128)(2,1)} %copy-done.20, bf16[2,4,512,1024]{3,2,1,0:T(8,128)(2,1)} %refs_2_.3, ...), custom_call_target="tpu_custom_call" | custom-call | flops 4000000000 | bytes 16777216 | tf_op jit(solution)/shard_map/pallas_call | solution.py:353
  121.1 0.1 collective-permute-start.17
  121.2 0.6 copy-done.17
  121.8 0.1 copy-done.18
  121.9 2.6 %shard_map.119 = (bf16[96,512]{1,0:T(8,128)(2,1)S(1)}, bf16[96,512]{1,0:T(8,128)(2,1)S(1)}) custom-call(bf16[192,512]{1,0:T(8,128)(2,1)} %copy-done.17, bf16[192,512]{1,0:T(8,128)(2,1)} %copy-done.18, bf16[8,512,1024]{2,1,0:T(8,128)(2,1)S(1)} %get-tuple-element.75.refs_2_, bf16[8,1024,512]{2,1,0:T(8,128)(2,1)S(1)} %get-tuple-element.76.refs_3_), custom_call_target="tpu_custom_call" | custom-call | flops 3000000000 | bytes 1048576 | tf_op jit(solution)/shard_map/pallas_call | solution.py:377
  124.6 3.7 %collective-permute-start.21 = (bf16[96,512]{1,0:T(8,128)(2,1)S(1)}, bf16[96,512]{1,0:T(8,128)(2,1)S(1)}, u32[]{:S(2)}, u32[]{:S(2)}) collective-permute-start(bf16[96,512]{1,0:T(8,128)(2,1)S(1)} %get-tuple-element.78), channel_id=1, source_target_pairs={{0,4},{1,5},{2,6},{3,7},{4,0},{5,1},{6,2},{7,3},{8,12},{9,13},{10,... | collective-permute-start | bytes 294920 | tf_op jit(solution)/shard_map/ppermute | solution.py:404
  128.3 0.7 collective-permute-start.23
  129.0 2.6 %shard_map.118 = (bf16[96,512]{1,0:T(8,128)(2,1)S(1)}, bf16[96,512]{1,0:T(8,128)(2,1)S(1)}) custom-call(bf16[192,512]{1,0:T(8,128)(2,1)} %copy-done.17, bf16[192,512]{1,0:T(8,128)(2,1)} %copy-done.18, bf16[8,512,1024]{2,1,0:T(8,128)(2,1)S(1)} %get-tuple-element.75.refs_2_, bf16[8,1024,512]{2,1,0:T(8,128)(2,1)S(1)} %get-tuple-element.76.refs_3_), custom_call_target="tpu_custom_call" | custom-call | flops 3000000000 | bytes 1048576 | tf_op jit(solution)/shard_map/pallas_call | solution.py:377
  131.6 0.9 collective-permute-start.20
  132.5 2.4 %collective-permute-start.22 = (bf16[96,512]{1,0:T(8,128)(2,1)S(1)}, bf16[96,512]{1,0:T(8,128)(2,1)S(1)}, u32[]{:S(2)}, u32[]{:S(2)}) collective-permute-start(bf16[96,512]{1,0:T(8,128)(2,1)S(1)} %get-tuple-element.79), channel_id=1, source_target_pairs={{0,6},{1,7},{2,4},{3,5},{4,2},{5,3},{6,0},{7,1},{8,14},{9,15},{10,... | collective-permute-start | bytes 294920 | tf_op jit(solution)/shard_map/ppermute | solution.py:404
  134.9 4.8 %collective-permute-done.21.refs_3_ = bf16[96,512]{1,0:T(8,128)(2,1)S(1)} collective-permute-done((bf16[96,512]{1,0:T(8,128)(2,1)S(1)}, bf16[96,512]{1,0:T(8,128)(2,1)S(1)}, u32[]{:S(2)}, u32[]{:S(2)}) %collective-permute-start.21) | collective-permute-done | bytes 98336 | tf_op jit(solution)/shard_map/ppermute | solution.py:404
  139.8 4.2 %collective-permute-done.20.refs_2_ = bf16[96,512]{1,0:T(8,128)(2,1)S(1)} collective-permute-done((bf16[96,512]{1,0:T(8,128)(2,1)S(1)}, bf16[96,512]{1,0:T(8,128)(2,1)S(1)}, u32[]{:S(2)}, u32[]{:S(2)}) %collective-permute-start.20) | collective-permute-done | bytes 98336 | tf_op jit(solution)/shard_map/ppermute | solution.py:404
  144.0 0.6 copy-done.30
  144.6 0.1 copy-done.23
  144.8 3.4 %shard_map.120 = bf16[576,512]{1,0:T(8,128)(2,1)} custom-call(bf16[672,512]{1,0:T(8,128)(2,1)} %copy-done.11, f32[672,2]{1,0:T(8,128)S(1)} %get-tuple-element.68.info_ref, s32[1,672]{1,0:T(1,128)S(1)} %copy-done.10, bf16[192,512]{1,0:T(8,128)(2,1)} %copy-done.3, bf16[192,512]{1,0:T(8,128)(2,1)} %copy-done.23, bf16[96,512]{1,0:T(8,128)(2,1)} %copy-done.30, ...), custom_call_target="tpu_custom_call" | custom-call | flops 1000000000 | bytes 1482624 | tf_op jit(solution)/shard_map/pallas_call | solution.py:336
  (73 shorter events, 0.3 us)
Async XLA Ops:
  0.0 28.8 %collective-permute-start.1 = (bf16[2,4,512,1024]{3,2,1,0:T(8,128)(2,1)}, bf16[2,4,512,1024]{3,2,1,0:T(8,128)(2,1)}, u32[]{:S(2)}, u32[]{:S(2)}) collective-permute-start(bf16[2,4,512,1024]{3,2,1,0:T(8,128)(2,1)} %refs_2_.3), channel_id=1, source_target_pairs={{0,1},{1,0},{2,3},{3,2},{4,5},{5,4},{6,7},{7,6},{8,9},{9,8},{10,11... | collective-permute-start | bytes 25165832 | tf_op jit(solution)/shard_map/ppermute | solution.py:404
  0.5 28.4 %collective-permute-start.2 = (bf16[2,4,1024,512]{3,2,1,0:T(8,128)(2,1)}, bf16[2,4,1024,512]{3,2,1,0:T(8,128)(2,1)}, u32[]{:S(2)}, u32[]{:S(2)}) collective-permute-start(bf16[2,4,1024,512]{3,2,1,0:T(8,128)(2,1)} %refs_3_.3), channel_id=1, source_target_pairs={{0,1},{1,0},{2,3},{3,2},{4,5},{5,4},{6,7},{7,6},{8,9},{9,8},{10,11... | collective-permute-start | bytes 25165832 | tf_op jit(solution)/shard_map/ppermute | solution.py:404
  1.5 0.7 copy-start.4
  2.2 0.7 copy-start.6
  2.9 1.0 copy-start.9
  16.5 0.7 copy-start.1
  17.2 23.2 %copy-start.12 = (bf16[576,512]{1,0:T(8,128)(2,1)}, bf16[576,512]{1,0:T(8,128)(2,1)S(1)}, u32[]{:S(2)}) copy-start(bf16[576,512]{1,0:T(8,128)(2,1)S(1)} %get-tuple-element.43.mixed_ref) | copy-start | bytes 1769476
  17.2 11.6 %collective-permute-start = (bf16[192,512]{1,0:T(8,128)(2,1)S(1)}, bf16[192,512]{1,0:T(8,128)(2,1)S(1)}, u32[]{:S(2)}, u32[]{:S(2)}) collective-permute-start(bf16[192,512]{1,0:T(8,128)(2,1)S(1)} %get-tuple-element.46), channel_id=1, source_target_pairs={{0,2},{1,3},{2,0},{3,1},{4,6},{5,7},{6,4},{7,5},{8,10},{9,11},{10,... | collective-permute-start | bytes 589832 | tf_op jit(solution)/shard_map/ppermute | solution.py:404
  20.2 20.2 %collective-permute-start.4 = (bf16[192,512]{1,0:T(8,128)(2,1)S(1)}, bf16[192,512]{1,0:T(8,128)(2,1)S(1)}, u32[]{:S(2)}, u32[]{:S(2)}) collective-permute-start(bf16[192,512]{1,0:T(8,128)(2,1)S(1)} %get-tuple-element.49), channel_id=1, source_target_pairs={{0,4},{1,5},{2,6},{3,7},{4,0},{5,1},{6,2},{7,3},{8,12},{9,13},{10,... | collective-permute-start | bytes 589832 | tf_op jit(solution)/shard_map/ppermute | solution.py:404
  22.8 17.7 %collective-permute-start.5 = (bf16[192,512]{1,0:T(8,128)(2,1)S(1)}, bf16[192,512]{1,0:T(8,128)(2,1)S(1)}, u32[]{:S(2)}, u32[]{:S(2)}) collective-permute-start(bf16[192,512]{1,0:T(8,128)(2,1)S(1)} %get-tuple-element.50), channel_id=1, source_target_pairs={{0,6},{1,7},{2,4},{3,5},{4,2},{5,3},{6,0},{7,1},{8,14},{9,15},{10,... | collective-permute-start | bytes 589832 | tf_op jit(solution)/shard_map/ppermute | solution.py:404
  28.8 0.7 copy-start.19
  40.4 3.5 %copy-start.2 = (bf16[192,512]{1,0:T(8,128)(2,1)}, bf16[192,512]{1,0:T(8,128)(2,1)S(1)}, u32[]{:S(2)}) copy-start(bf16[192,512]{1,0:T(8,128)(2,1)S(1)} %get-tuple-element.47.refs_0_) | copy-start | bytes 589828
  40.5 0.7 copy-start.15
  40.5 0.8 copy-start.16
  43.9 10.5 %collective-permute-start.7 = (bf16[96,512]{1,0:T(8,128)(2,1)S(1)}, bf16[96,512]{1,0:T(8,128)(2,1)S(1)}, u32[]{:S(2)}, u32[]{:S(2)}) collective-permute-start(bf16[96,512]{1,0:T(8,128)(2,1)S(1)} %get-tuple-element.54), channel_id=1, source_target_pairs={{0,4},{1,5},{2,6},{3,7},{4,0},{5,1},{6,2},{7,3},{8,12},{9,13},{10,... | collective-permute-start | bytes 294920 | tf_op jit(solution)/shard_map/ppermute | solution.py:404
  45.3 9.1 %collective-permute-start.9 = (bf16[96,512]{1,0:T(8,128)(2,1)S(1)}, bf16[96,512]{1,0:T(8,128)(2,1)S(1)}, u32[]{:S(2)}, u32[]{:S(2)}) collective-permute-start(bf16[96,512]{1,0:T(8,128)(2,1)S(1)} %get-tuple-element.56), channel_id=1, source_target_pairs={{0,6},{1,7},{2,4},{3,5},{4,2},{5,3},{6,0},{7,1},{8,14},{9,15},{10,... | collective-permute-start | bytes 294920 | tf_op jit(solution)/shard_map/ppermute | solution.py:404
  47.3 28.0 %copy-start.5 = (f32[2,2,512]{2,1,0:T(2,128)S(1)}, f32[2,2,512]{2,1,0:T(2,128)}, u32[]{:S(2)}) copy-start(f32[2,2,512]{2,1,0:T(2,128)} %gain_ref.5) | copy-start | bytes 24580
  47.3 28.0 %copy-start.7 = (f32[2,16]{1,0:T(2,128)S(1)}, f32[2,16]{1,0:T(2,128)}, u32[]{:S(2)}) copy-start(f32[2,16]{1,0:T(2,128)} %temper_ref.3) | copy-start | bytes 388
  47.3 15.0 %collective-permute-start.3 = (bf16[192,512]{1,0:T(8,128)(2,1)S(1)}, bf16[192,512]{1,0:T(8,128)(2,1)S(1)}, u32[]{:S(2)}, u32[]{:S(2)}) collective-permute-start(bf16[192,512]{1,0:T(8,128)(2,1)S(1)} %get-tuple-element.48), channel_id=1, source_target_pairs={{0,2},{1,3},{2,0},{3,1},{4,6},{5,7},{6,4},{7,5},{8,10},{9,11},{10,... | collective-permute-start | bytes 589832 | tf_op jit(solution)/shard_map/ppermute | solution.py:404
  50.4 39.1 %copy-start.8 = (s32[672,1]{1,0:T(8,128)S(1)}, s32[672,1]{1,0:T(8,128)}, u32[]{:S(2)}) copy-start(s32[672,1]{1,0:T(8,128)} %constant.46.order_ref) | copy-start | bytes 8068
  50.4 11.8 %collective-permute-start.6 = (bf16[96,512]{1,0:T(8,128)(2,1)S(1)}, bf16[96,512]{1,0:T(8,128)(2,1)S(1)}, u32[]{:S(2)}, u32[]{:S(2)}) collective-permute-start(bf16[96,512]{1,0:T(8,128)(2,1)S(1)} %get-tuple-element.53), channel_id=1, source_target_pairs={{0,4},{1,5},{2,6},{3,7},{4,0},{5,1},{6,2},{7,3},{8,12},{9,13},{10,... | collective-permute-start | bytes 294920 | tf_op jit(solution)/shard_map/ppermute | solution.py:404
  52.4 9.9 %collective-permute-start.8 = (bf16[96,512]{1,0:T(8,128)(2,1)S(1)}, bf16[96,512]{1,0:T(8,128)(2,1)S(1)}, u32[]{:S(2)}, u32[]{:S(2)}) collective-permute-start(bf16[96,512]{1,0:T(8,128)(2,1)S(1)} %get-tuple-element.55), channel_id=1, source_target_pairs={{0,6},{1,7},{2,4},{3,5},{4,2},{5,3},{6,0},{7,1},{8,14},{9,15},{10,... | collective-permute-start | bytes 294920 | tf_op jit(solution)/shard_map/ppermute | solution.py:404
  54.4 7.9 %copy-start.25 = (bf16[96,512]{1,0:T(8,128)(2,1)}, bf16[96,512]{1,0:T(8,128)(2,1)S(1)}, u32[]{:S(2)}) copy-start(bf16[96,512]{1,0:T(8,128)(2,1)S(1)} %collective-permute-done.7.refs_3_) | copy-start | bytes 294916
  54.4 7.9 %copy-start.26 = (bf16[96,512]{1,0:T(8,128)(2,1)}, bf16[96,512]{1,0:T(8,128)(2,1)S(1)}, u32[]{:S(2)}) copy-start(bf16[96,512]{1,0:T(8,128)(2,1)S(1)} %collective-permute-done.9.refs_5_) | copy-start | bytes 294916
  62.2 0.6 copy-start.29
  62.3 0.7 copy-start.31
  62.3 0.8 copy-start.24
  65.1 0.7 copy-start.13
  65.8 8.7 %collective-permute-start.10 = (bf16[288,512]{1,0:T(8,128)(2,1)S(1)}, bf16[288,512]{1,0:T(8,128)(2,1)S(1)}, u32[]{:S(2)}, u32[]{:S(2)}) collective-permute-start(bf16[288,512]{1,0:T(8,128)(2,1)S(1)} %get-tuple-element.58), channel_id=1, source_target_pairs={{0,24},{1,25},{2,26},{3,27},{4,28},{5,29},{6,30},{7,31},{8,0},{9,1... | collective-permute-start | bytes 884744 | tf_op jit(solution)/shard_map/ppermute | solution.py:399
  68.3 2.3 %collective-permute-start.11 = (bf16[48,512]{1,0:T(8,128)(2,1)S(1)}, bf16[48,512]{1,0:T(8,128)(2,1)S(1)}, u32[]{:S(2)}, u32[]{:S(2)}) collective-permute-start(bf16[48,512]{1,0:T(8,128)(2,1)S(1)} %get-tuple-element.59), channel_id=1, source_target_pairs={{0,7},{1,0},{2,1},{3,2},{4,3},{5,4},{6,5},{7,6},{8,15},{9,8},{10,9... | collective-permute-start | bytes 147464 | tf_op jit(solution)/shard_map/ppermute | solution.py:399
  68.3 4.1 %collective-permute-start.12 = (bf16[48,512]{1,0:T(8,128)(2,1)S(1)}, bf16[48,512]{1,0:T(8,128)(2,1)S(1)}, u32[]{:S(2)}, u32[]{:S(2)}) collective-permute-start(bf16[48,512]{1,0:T(8,128)(2,1)S(1)} %get-tuple-element.60), channel_id=1, source_target_pairs={{0,31},{1,24},{2,25},{3,26},{4,27},{5,28},{6,29},{7,30},{8,7},{9,0... | collective-permute-start | bytes 147464 | tf_op jit(solution)/shard_map/ppermute | solution.py:399
  70.6 3.9 %copy-start.35 = (bf16[48,512]{1,0:T(8,128)(2,1)}, bf16[48,512]{1,0:T(8,128)(2,1)S(1)}, u32[]{:S(2)}) copy-start(bf16[48,512]{1,0:T(8,128)(2,1)S(1)} %collective-permute-done.11.east_ref) | copy-start | bytes 147460
  72.4 2.1 %copy-start.36 = (bf16[48,512]{1,0:T(8,128)(2,1)}, bf16[48,512]{1,0:T(8,128)(2,1)S(1)}, u32[]{:S(2)}) copy-start(bf16[48,512]{1,0:T(8,128)(2,1)S(1)} %collective-permute-done.12.corner_ref) | copy-start | bytes 147460
  74.5 0.7 copy-start.22
  84.6 9.3 %copy-start.14 = (bf16[288,512]{1,0:T(8,128)(2,1)}, bf16[288,512]{1,0:T(8,128)(2,1)S(1)}, u32[]{:S(2)}) copy-start(bf16[288,512]{1,0:T(8,128)(2,1)S(1)} %get-tuple-element.61.own_ref) | copy-start | bytes 884740
  84.6 9.2 %collective-permute-start.13 = (bf16[288,512]{1,0:T(8,128)(2,1)S(1)}, bf16[288,512]{1,0:T(8,128)(2,1)S(1)}, u32[]{:S(2)}, u32[]{:S(2)}) collective-permute-start(bf16[288,512]{1,0:T(8,128)(2,1)S(1)} %get-tuple-element.62), channel_id=1, source_target_pairs={{0,8},{1,9},{2,10},{3,11},{4,12},{5,13},{6,14},{7,15},{8,16},{9,17... | collective-permute-start | bytes 884744 | tf_op jit(solution)/shard_map/ppermute | solution.py:399
  86.5 5.5 %collective-permute-start.14 = (bf16[48,512]{1,0:T(8,128)(2,1)S(1)}, bf16[48,512]{1,0:T(8,128)(2,1)S(1)}, u32[]{:S(2)}, u32[]{:S(2)}) collective-permute-start(bf16[48,512]{1,0:T(8,128)(2,1)S(1)} %get-tuple-element.63), channel_id=1, source_target_pairs={{0,1},{1,2},{2,3},{3,4},{4,5},{5,6},{6,7},{7,0},{8,9},{9,10},{10,1... | collective-permute-start | bytes 147464 | tf_op jit(solution)/shard_map/ppermute | solution.py:399
  86.5 7.2 %collective-permute-start.15 = (bf16[48,512]{1,0:T(8,128)(2,1)S(1)}, bf16[48,512]{1,0:T(8,128)(2,1)S(1)}, u32[]{:S(2)}, u32[]{:S(2)}) collective-permute-start(bf16[48,512]{1,0:T(8,128)(2,1)S(1)} %get-tuple-element.64), channel_id=1, source_target_pairs={{0,9},{1,10},{2,11},{3,12},{4,13},{5,14},{6,15},{7,8},{8,17},{9,18... | collective-permute-start | bytes 147464 | tf_op jit(solution)/shard_map/ppermute | solution.py:399
  92.1 1.8 %copy-start.33 = (bf16[48,512]{1,0:T(8,128)(2,1)}, bf16[48,512]{1,0:T(8,128)(2,1)S(1)}, u32[]{:S(2)}) copy-start(bf16[48,512]{1,0:T(8,128)(2,1)S(1)} %collective-permute-done.14.west_ref) | copy-start | bytes 147460
  93.7 0.6 copy-start.34
  93.8 0.7 copy-start.21
  96.9 0.7 copy-start
  97.6 0.9 copy-start.11
  98.5 11.1 %collective-permute-start.16 = (bf16[192,512]{1,0:T(8,128)(2,1)S(1)}, bf16[192,512]{1,0:T(8,128)(2,1)S(1)}, u32[]{:S(2)}, u32[]{:S(2)}) collective-permute-start(bf16[192,512]{1,0:T(8,128)(2,1)S(1)} %get-tuple-element.70), channel_id=1, source_target_pairs={{0,2},{1,3},{2,0},{3,1},{4,6},{5,7},{6,4},{7,5},{8,10},{9,11},{10,... | collective-permute-start | bytes 589832 | tf_op jit(solution)/shard_map/ppermute | solution.py:404
  100.6 20.6 %collective-permute-start.18 = (bf16[192,512]{1,0:T(8,128)(2,1)S(1)}, bf16[192,512]{1,0:T(8,128)(2,1)S(1)}, u32[]{:S(2)}, u32[]{:S(2)}) collective-permute-start(bf16[192,512]{1,0:T(8,128)(2,1)S(1)} %get-tuple-element.73), channel_id=1, source_target_pairs={{0,4},{1,5},{2,6},{3,7},{4,0},{5,1},{6,2},{7,3},{8,12},{9,13},{10,... | collective-permute-start | bytes 589832 | tf_op jit(solution)/shard_map/ppermute | solution.py:404
  103.0 18.2 %collective-permute-start.19 = (bf16[192,512]{1,0:T(8,128)(2,1)S(1)}, bf16[192,512]{1,0:T(8,128)(2,1)S(1)}, u32[]{:S(2)}, u32[]{:S(2)}) collective-permute-start(bf16[192,512]{1,0:T(8,128)(2,1)S(1)} %get-tuple-element.74), channel_id=1, source_target_pairs={{0,6},{1,7},{2,4},{3,5},{4,2},{5,3},{6,0},{7,1},{8,14},{9,15},{10,... | collective-permute-start | bytes 589832 | tf_op jit(solution)/shard_map/ppermute | solution.py:404
  109.6 0.7 copy-start.20
  121.1 3.5 %copy-start.3 = (bf16[192,512]{1,0:T(8,128)(2,1)}, bf16[192,512]{1,0:T(8,128)(2,1)S(1)}, u32[]{:S(2)}) copy-start(bf16[192,512]{1,0:T(8,128)(2,1)S(1)} %get-tuple-element.71.refs_0_) | copy-start | bytes 589828
  121.1 22.9 %collective-permute-start.17 = (bf16[192,512]{1,0:T(8,128)(2,1)S(1)}, bf16[192,512]{1,0:T(8,128)(2,1)S(1)}, u32[]{:S(2)}, u32[]{:S(2)}) collective-permute-start(bf16[192,512]{1,0:T(8,128)(2,1)S(1)} %get-tuple-element.72), channel_id=1, source_target_pairs={{0,2},{1,3},{2,0},{3,1},{4,6},{5,7},{6,4},{7,5},{8,10},{9,11},{10,... | collective-permute-start | bytes 589832 | tf_op jit(solution)/shard_map/ppermute | solution.py:404
  121.2 0.7 copy-start.17
  121.2 0.8 copy-start.18
  124.6 15.2 %collective-permute-start.21 = (bf16[96,512]{1,0:T(8,128)(2,1)S(1)}, bf16[96,512]{1,0:T(8,128)(2,1)S(1)}, u32[]{:S(2)}, u32[]{:S(2)}) collective-permute-start(bf16[96,512]{1,0:T(8,128)(2,1)S(1)} %get-tuple-element.78), channel_id=1, source_target_pairs={{0,4},{1,5},{2,6},{3,7},{4,0},{5,1},{6,2},{7,3},{8,12},{9,13},{10,... | collective-permute-start | bytes 294920 | tf_op jit(solution)/shard_map/ppermute | solution.py:404
  128.3 16.4 %copy-start.10 = (s32[1,672]{1,0:T(1,128)S(1)}, s32[1,672]{1,0:T(1,128)}, u32[]{:S(2)}) copy-start(s32[1,672]{1,0:T(1,128)} %constant.47.order_ref) | copy-start | bytes 8068
  128.3 11.4 %collective-permute-start.23 = (bf16[96,512]{1,0:T(8,128)(2,1)S(1)}, bf16[96,512]{1,0:T(8,128)(2,1)S(1)}, u32[]{:S(2)}, u32[]{:S(2)}) collective-permute-start(bf16[96,512]{1,0:T(8,128)(2,1)S(1)} %get-tuple-element.80), channel_id=1, source_target_pairs={{0,6},{1,7},{2,4},{3,5},{4,2},{5,3},{6,0},{7,1},{8,14},{9,15},{10,... | collective-permute-start | bytes 294920 | tf_op jit(solution)/shard_map/ppermute | solution.py:404
  131.6 12.4 %collective-permute-start.20 = (bf16[96,512]{1,0:T(8,128)(2,1)S(1)}, bf16[96,512]{1,0:T(8,128)(2,1)S(1)}, u32[]{:S(2)}, u32[]{:S(2)}) collective-permute-start(bf16[96,512]{1,0:T(8,128)(2,1)S(1)} %get-tuple-element.77), channel_id=1, source_target_pairs={{0,4},{1,5},{2,6},{3,7},{4,0},{5,1},{6,2},{7,3},{8,12},{9,13},{10,... | collective-permute-start | bytes 294920 | tf_op jit(solution)/shard_map/ppermute | solution.py:404
  132.5 11.5 %collective-permute-start.22 = (bf16[96,512]{1,0:T(8,128)(2,1)S(1)}, bf16[96,512]{1,0:T(8,128)(2,1)S(1)}, u32[]{:S(2)}, u32[]{:S(2)}) collective-permute-start(bf16[96,512]{1,0:T(8,128)(2,1)S(1)} %get-tuple-element.79), channel_id=1, source_target_pairs={{0,6},{1,7},{2,4},{3,5},{4,2},{5,3},{6,0},{7,1},{8,14},{9,15},{10,... | collective-permute-start | bytes 294920 | tf_op jit(solution)/shard_map/ppermute | solution.py:404
  139.8 4.2 %copy-start.27 = (bf16[96,512]{1,0:T(8,128)(2,1)}, bf16[96,512]{1,0:T(8,128)(2,1)S(1)}, u32[]{:S(2)}) copy-start(bf16[96,512]{1,0:T(8,128)(2,1)S(1)} %collective-permute-done.21.refs_3_) | copy-start | bytes 294916
  139.8 4.2 %copy-start.28 = (bf16[96,512]{1,0:T(8,128)(2,1)}, bf16[96,512]{1,0:T(8,128)(2,1)S(1)}, u32[]{:S(2)}) copy-start(bf16[96,512]{1,0:T(8,128)(2,1)S(1)} %collective-permute-done.23.refs_5_) | copy-start | bytes 294916
  144.0 0.6 copy-start.30
  144.0 0.7 copy-start.32
  144.0 0.8 copy-start.23

commit v2 on v1

--- a/solution.py
+++ b/solution.py
@@ -42,9 +42,28 @@
     return jnp.where(spread == row, 1.0, 0.0).astype(BF16)
 
 
-def slots_of(ids, order, place_ref, pair_experts):
-    count = ids.shape[0]
-    chosen = lax.broadcasted_iota(jnp.int32, (count, LANES), 1) == ids
+class Brought:
+    def __init__(self, source, target, arrived):
+        self.target, self.pending = target, True
+        self.copy = pltpu.make_async_copy(source, target, arrived)
+        self.copy.start()
+
+    def get(self):
+        if self.pending:
+            self.copy.wait()
+            self.pending = False
+        return self.target[...]
+
+
+def upright(row):
+    return jnp.transpose(jnp.broadcast_to(row.astype(F32), (LANES, row.shape[1])))
+
+
+def slots_of(ids_row, order, place_ref, pair_experts):
+    count = ids_row.shape[1]
+    spread_ids = upright(ids_row).astype(jnp.int32)
+    ids = spread_ids[:, 0:1]
+    chosen = lax.broadcasted_iota(jnp.int32, (count, LANES), 1) == spread_ids
     earlier = lax.broadcasted_iota(jnp.int32, (count, count), 0) > lax.broadcasted_iota(jnp.int32, (count, count), 1)
     before = dot(jnp.where(earlier, 1.0, 0.0).astype(BF16), jnp.where(chosen, 1.0, 0.0).astype(BF16))
     place = jnp.sum(jnp.where(chosen, before, 0.0), axis=1, keepdims=True).astype(jnp.int32)
@@ -71,16 +90,7 @@
     return jax.nn.sigmoid(picked)
 
 
-def fetch(layer, sources, targets, arrived):
-    copies = []
-    for index, (source, target) in enumerate(zip(sources, targets)):
-        copy = pltpu.make_async_copy(source.at[layer], target, arrived.at[index])
-        copy.start()
-        copies.append(copy)
-    return copies
-
-
-def attend(frame, layer, place_ref, temper_ref, gain_ref, wqkv_ref, wproj_ref, qkv_ref, context_ref, copies):
+def attend(frame, layer, place_ref, temper_ref, gain, wqkv, wproj, qkv_ref, context_ref):
     total, channels = frame.shape
     heads = temper_ref.shape[1]
     width = channels // heads
@@ -90,9 +100,8 @@
     main = LANES
     rest = area - main
     lanes = group * area
-    normed = norm_rows(frame, gain_ref[0, 0:1, :])
-    copies[0].wait()
-    qkv_ref[...] = dot(normed, wqkv_ref[...]).astype(BF16)
+    normed = norm_rows(frame, gain.get()[0:1, :])
+    qkv_ref[...] = dot(normed, wqkv.get()).astype(BF16)
 
     lane = lax.broadcasted_iota(jnp.int32, (1, lanes), 1)
     leftover = lane >= group * main
@@ -141,39 +150,38 @@
 
     for window in range(windows):
         one_window(window)
-    copies[1].wait()
-    attended = dot(context_ref[...], wproj_ref[...])
+    attended = dot(context_ref[...], wproj.get())
     return (frame + attended).astype(BF16)
 
 
 def first_kernel(
-    place_ref, temper_ref, tokens_ref, order_ref, ids_ref, gain_ref, wqkv_hbm, wproj_hbm, router_ref,
+    place_ref, temper_ref, tokens, order, ids, gain, wqkv, wproj, router,
     mixed_ref, info_ref, *refs, layer, pair_experts
 ):
-    *piece_refs, wqkv_ref, wproj_ref, qkv_ref, context_ref, arrived = refs
-    copies = fetch(layer, (wqkv_hbm, wproj_hbm), (wqkv_ref, wproj_ref), arrived)
-    tokens = tokens_ref[...]
-    frame = dot(one_hot_columns(order_ref[...], tokens.shape[0]), tokens)
-    mixed = attend(frame, layer, place_ref, temper_ref, gain_ref, wqkv_ref, wproj_ref, qkv_ref, context_ref, copies)
+    *piece_refs, qkv_ref, context_ref = refs
+    order = upright(order.get())[:, 0:1].astype(jnp.int32)
+    rows = tokens.get()
+    frame = dot(one_hot_columns(order, rows.shape[0]), rows)
+    mixed = attend(frame, layer, place_ref, temper_ref, gain, wqkv, wproj, qkv_ref, context_ref)
     mixed_ref[...] = mixed
-    ynorm = norm_rows(mixed.astype(F32), gain_ref[0, 1:2, :])
-    experts, slot, slot_row = slots_of(ids_ref[0], order_ref[...], place_ref, pair_experts)
-    gate = route(ynorm, router_ref[0], experts, slot_row, piece_refs)
+    ynorm = norm_rows(mixed.astype(F32), gain.get()[1:2, :])
+    experts, slot, slot_row = slots_of(ids.get(), order, place_ref, pair_experts)
+    gate = route(ynorm, router.get(), experts, slot_row, piece_refs)
     info_ref[...] = jnp.concatenate([gate, slot], axis=1)
 
 
-def slots_kernel(place_ref, ids_ref, order_ref, _, columns_ref, row_ref, *, pair_experts):
-    experts, slot, slot_row = slots_of(ids_ref[0], order_ref[...], place_ref, pair_experts)
+def slots_kernel(place_ref, ids, order, _, columns_ref, row_ref, *, pair_experts):
+    order = upright(order.get())[:, 0:1].astype(jnp.int32)
+    experts, slot, slot_row = slots_of(ids.get(), order, place_ref, pair_experts)
     columns_ref[...] = jnp.concatenate([experts, slot], axis=1)
     row_ref[...] = slot_row
 
 
 def shifted_kernel(
-    place_ref, temper_ref, own_ref, north_ref, east_ref, corner_ref, gain_ref, wqkv_hbm, wproj_hbm,
+    place_ref, temper_ref, own_ref, north_ref, east_ref, corner_ref, gain, wqkv, wproj,
     low_ref, high_ref, low_edge_ref, high_edge_ref,
-    low_scratch, high_scratch, wqkv_ref, wproj_ref, qkv_ref, context_ref, arrived, *, layer
+    low_scratch, high_scratch, qkv_ref, context_ref, *, layer
 ):
-    copies = fetch(layer, (wqkv_hbm, wproj_hbm), (wqkv_ref, wproj_ref), arrived)
     half, channels = own_ref.shape
     strip = HALF * HALF
     part = WIN * HALF
@@ -187,7 +195,7 @@
         start = strip + window * part
         pieces += [low_scratch[start : start + part], high_scratch[start : start + part]]
     frame = jnp.concatenate(pieces, axis=0)
-    mixed = attend(frame, layer, place_ref, temper_ref, gain_ref, wqkv_ref, wproj_ref, qkv_ref, context_ref, copies)
+    mixed = attend(frame, layer, place_ref, temper_ref, gain, wqkv, wproj, qkv_ref, context_ref)
     mixed = mixed.astype(F32)
     low, high = split_halves(mixed)
     low_ref[...] = low.astype(BF16)
@@ -202,12 +210,12 @@
     return jnp.concatenate(pieces[0::2], axis=0), jnp.concatenate(pieces[1::2], axis=0)
 
 
-def route_kernel(own_ref, south_ref, west_ref, corner_ref, columns_ref, row_ref, gain_ref, router_ref,
+def route_kernel(own_ref, south_ref, west_ref, corner_ref, columns_ref, row_ref, gain, router,
                  rows_ref, info_ref, *piece_refs):
     mixed = jnp.concatenate([own_ref[...], south_ref[...], west_ref[...], corner_ref[...]], axis=0)
     rows_ref[...] = mixed
-    ynorm = norm_rows(mixed.astype(F32), gain_ref[0, 1:2, :])
-    gate = route(ynorm, router_ref[0], columns_ref[:, 0:1], row_ref[...], piece_refs)
+    ynorm = norm_rows(mixed.astype(F32), gain.get()[1:2, :])
+    gate = route(ynorm, router.get(), columns_ref[:, 0:1], row_ref[...], piece_refs)
     info_ref[...] = jnp.concatenate([gate, columns_ref[:, 1:2]], axis=1)
 
 
@@ -222,67 +230,61 @@
     return total
 
 
-def near_kernel(*refs, sources, plan, layer):
-    piece_hbm = refs[:sources]
-    weights = refs[sources : sources + 4]
-    out_refs = refs[sources + 4 : 2 * sources + 4]
-    first_ref, second_ref, piece_ref, arrived, here = refs[2 * sources + 4 :]
-    moves = []
-    for index, ref in enumerate(piece_hbm):
-        move = pltpu.make_async_copy(ref, piece_ref.at[index], here.at[index])
-        move.start()
-        moves.append(move)
-    copies = []
-    for unit, (which, entry, _) in enumerate(plan):
-        pair = []
-        for side, target in enumerate((first_ref, second_ref)):
-            copy = pltpu.make_async_copy(
-                weights[2 * which + side].at[layer, entry], target.at[unit], arrived.at[side, unit]
-            )
-            copy.start()
-            pair.append(copy)
-        copies.append(pair)
-    for move in moves:
-        move.wait()
+def near_kernel(*refs, plan, layer):
+    piece_ref, *weights = refs[:5]
+    out_ref, first_ref, second_ref, arrived = refs[5:]
+    ahead = 2
+    copies = {}
+
+    def begin(unit):
+        if unit < len(plan):
+            which, entry, _ = plan[unit]
+            for side, target in enumerate((first_ref, second_ref)):
+                copies[unit, side] = pltpu.make_async_copy(
+                    weights[2 * which + side].at[layer, entry], target.at[unit], arrived.at[side, unit]
+                )
+                copies[unit, side].start()
+
+    def wait_for(unit, side, ref):
+        copies[unit, side].wait()
+        if side == 0:
+            begin(unit + ahead)
+        return ref[unit]
+
+    for unit in range(ahead):
+        begin(unit)
     totals = {}
     last = {place: unit for unit, (_, _, place) in enumerate(plan)}
-    pieces = [piece_ref.at[index] for index in range(sources)]
-
-    def wait_for(unit, side, ref):
-        copies[unit][side].wait()
-        return ref[unit]
-
     for unit, (_, _, place) in enumerate(plan):
         block = slice(place * CAP, (place + 1) * CAP)
         totals[place] = expert_rows(
-            pieces, out_refs, block,
+            [piece_ref], [out_ref], block,
             functools.partial(wait_for, unit, 0, first_ref), functools.partial(wait_for, unit, 1, second_ref),
             totals.get(place), last[place] == unit,
         )
 
 
-def away_kernel(*refs, sources, plan, base):
-    piece_hbm = refs[:sources]
+def away_kernel(*refs, sources, plan, base, kept):
+    piece_refs = refs[:sources]
     first_ref, second_ref = refs[sources : sources + 2]
-    out_refs = refs[sources + 2 : 2 * sources + 2]
-    piece_ref, here = refs[2 * sources + 2 :]
-    size = out_refs[0].shape[0]
-    moves = []
-    for index, ref in enumerate(piece_hbm):
-        move = pltpu.make_async_copy(ref.at[pl.ds(base * CAP, size)], piece_ref.at[index], here.at[index])
-        move.start()
-        moves.append(move)
-    for move in moves:
-        move.wait()
+    kept_refs = refs[sources + 2 : sources + 2 + kept]
+    out_refs = list(refs[sources + 2 + kept :])
+    for index, ref in enumerate(kept_refs):
+        size = ref.shape[0]
+        out_refs[index][0:size, :] = ref[...]
+        out_refs[index] = out_refs[index].at[size:]
     totals = {}
     last = {place: unit for unit, place in plan}
-    pieces = [piece_ref.at[index] for index in range(sources)]
     for unit, place in plan:
-        block = slice((place - base) * CAP, (place - base + 1) * CAP)
-        totals[place] = expert_rows(
-            pieces, out_refs, block, lambda unit=unit: first_ref[unit], lambda unit=unit: second_ref[unit],
-            totals.get(place), last[place] == unit,
-        )
+        outs = [ref.at[pl.ds((place - base) * CAP, CAP)] for ref in out_refs]
+        block = slice(place * CAP, (place + 1) * CAP)
+        rows = jnp.concatenate([ref[block, :] for ref in piece_refs], axis=0)
+        hidden = jax.nn.gelu(dot(rows, first_ref[unit])).astype(BF16)
+        part = dot(hidden, second_ref[unit])
+        totals[place] = totals[place] + part if place in totals else part
+        if last[place] == unit:
+            for index, ref in enumerate(outs):
+                ref[...] = totals[place][index * CAP : (index + 1) * CAP].astype(BF16)
 
 
 def gathered_state(mixed_ref, info_ref, piece_refs):
@@ -303,86 +305,87 @@
     east_ref[...] = high[:edge].astype(BF16)
 
 
-def last_kernel(mixed_ref, info_ref, order_ref, *refs):
+def last_kernel(mixed_ref, info_ref, order, *refs):
     *piece_refs, out_ref = refs
     state = gathered_state(mixed_ref, info_ref, piece_refs)
-    out_ref[...] = dot(one_hot_rows(order_ref[...], out_ref.shape[0]), state).astype(BF16)
-
-
-def whole(shape):
-    return pl.BlockSpec(shape, lambda *_: (0,) * len(shape))
-
-
-def of_layer(array, layer):
-    rest = array.shape[1:]
-    return pl.BlockSpec((1,) + rest, lambda *_: (layer,) + (0,) * len(rest))
+    out_ref[...] = dot(one_hot_rows(order.get(), out_ref.shape[0]), state).astype(BF16)
 
 
 SCALARS = pl.BlockSpec(memory_space=pltpu.SMEM)
 IN_HBM = pl.BlockSpec(memory_space=pltpu.HBM)
 IN_VMEM = pl.BlockSpec(memory_space=pltpu.VMEM)
-SMALL = 1 << 14
+UNREAD = "unread"
 
 
 def keep_out(array):
-    if array.size < SMALL:
-        return array
     return pltpu.with_memory_space_constraint(array, pltpu.HBM)
 
 
 def call(kernel, ins, outs, scratch=(), limit=40, flops=0):
-    arrays = [array for array, _ in ins]
+    arrays, specs, rooms = [], [], []
+    for array, how in ins:
+        specs.append(how if how in (SCALARS, IN_VMEM) else IN_HBM)
+        arrays.append(array if how == IN_VMEM else keep_out(array))
+        if isinstance(how, tuple):
+            rooms.append(pltpu.VMEM(array.shape[len(how) :], array.dtype))
+    brought = len(rooms)
+
+    def body(*refs):
+        operands = list(refs[: len(ins)])
+        room_refs, arrived = (refs[-1 - brought : -1], refs[-1]) if brought else ((), None)
+        others = refs[len(ins) : len(refs) - (brought + 1 if brought else 0)]
+        at = 0
+        for index, (_, how) in enumerate(ins):
+            if isinstance(how, tuple):
+                source = operands[index].at[how] if how else operands[index]
+                operands[index] = Brought(source, room_refs[at], arrived.at[at])
+                at += 1
+        kernel(*operands, *others)
+
     size = sum(a.size * a.dtype.itemsize for a in arrays)
     return pl.pallas_call(
-        kernel,
-        grid=(1,),
-        in_specs=[spec if spec is not None else whole(array.shape) for array, spec in ins],
-        out_specs=[whole(o.shape) for o in outs],
+        body,
+        in_specs=specs,
+        out_specs=[IN_VMEM] * len(outs),
         out_shape=outs,
-        scratch_shapes=list(scratch),
+        scratch_shapes=list(scratch) + rooms + ([pltpu.SemaphoreType.DMA((brought,))] if brought else []),
         compiler_params=pltpu.CompilerParams(vmem_limit_bytes=limit * MIB),
         cost_estimate=pl.CostEstimate(flops=flops, bytes_accessed=size, transcendentals=0),
-    )(*[keep_out(array) if spec is not SCALARS else array for array, spec in ins])
-
-
-def run_near(pieces, weights, plan, layer):
-    sources = len(pieces)
-    slots, channels = pieces[0].shape
-    units = weights[0].shape[3]
+    )(*arrays)
+
+
+def run_near(piece, weights, plan, layer):
+    channels, units = piece.shape[1], weights[0].shape[3]
     held = [pltpu.VMEM((len(plan), channels, units), BF16), pltpu.VMEM((len(plan), units, channels), BF16)]
-    outs = pl.pallas_call(
-        functools.partial(near_kernel, sources=sources, plan=plan, layer=layer),
-        in_specs=[IN_HBM] * (sources + 4),
-        out_specs=[IN_VMEM] * (sources + 2),
-        out_shape=[jax.ShapeDtypeStruct(p.shape, BF16) for p in pieces] + held,
-        scratch_shapes=[
-            pltpu.VMEM((sources, slots, channels), BF16),
-            pltpu.SemaphoreType.DMA((2, len(plan))),
-            pltpu.SemaphoreType.DMA((sources,)),
-        ],
+    out, *held = pl.pallas_call(
+        functools.partial(near_kernel, plan=plan, layer=layer),
+        in_specs=[IN_VMEM] + [IN_HBM] * 4,
+        out_specs=[IN_VMEM] * 3,
+        out_shape=[jax.ShapeDtypeStruct(piece.shape, BF16)] + held,
+        scratch_shapes=[pltpu.SemaphoreType.DMA((2, len(plan)))],
         compiler_params=pltpu.CompilerParams(vmem_limit_bytes=24 * MIB),
         cost_estimate=pl.CostEstimate(
             flops=4_000_000_000, bytes_accessed=len(plan) * 4 * channels * units, transcendentals=0
         ),
-    )(*[keep_out(p) for p in pieces], *[keep_out(w) for w in weights])
-    return outs[:sources], outs[sources:]
-
-
-def run_away(pieces, held, plan, layer):
+    )(piece, *[keep_out(w) for w in weights])
+    return out, held
+
+
+def run_away(pieces, held, plan, kept):
     sources = len(pieces)
     channels = pieces[0].shape[1]
     places = [place for _, place in plan]
     base = min(places)
     size = (max(places) - base + 1) * CAP
+    sizes = [size + kept[k].shape[0] if k < len(kept) else size for k in range(sources)]
     return pl.pallas_call(
-        functools.partial(away_kernel, sources=sources, plan=plan, base=base),
-        in_specs=[IN_HBM] * sources + [IN_VMEM] * 2,
+        functools.partial(away_kernel, sources=sources, plan=plan, base=base, kept=len(kept)),
+        in_specs=[IN_VMEM] * (sources + 2 + len(kept)),
         out_specs=[IN_VMEM] * sources,
-        out_shape=[jax.ShapeDtypeStruct((size, channels), BF16)] * sources,
-        scratch_shapes=[pltpu.VMEM((sources, size, channels), BF16), pltpu.SemaphoreType.DMA((sources,))],
+        out_shape=[jax.ShapeDtypeStruct((rows, channels), BF16) for rows in sizes],
         compiler_params=pltpu.CompilerParams(vmem_limit_bytes=24 * MIB),
         cost_estimate=pl.CostEstimate(flops=3_000_000_000, bytes_accessed=1 << 20, transcendentals=0),
-    )(*[keep_out(p) for p in pieces], *held)
+    )(*pieces, *held, *kept)
 
 
 def lat_lon_pairs(lat_step, lon_step):
@@ -423,7 +426,7 @@
     far_out = between(weight_out, 1)
 
     router = router.transpose(0, 2, 1)
-    ids = expert_ids.reshape(LAYERS, token_count, 1)
+    ids = expert_ids.reshape(LAYERS, 1, token_count)
     seam = jnp.where(lat == lax.axis_size("lat") - 1, 1, 0)
     place = jnp.stack([seam, lon // 2, lon % 2]).astype(jnp.int32).reshape(1, 3)
 
@@ -435,37 +438,34 @@
     low, high = halves
     order1 = np.concatenate([high[strip:], gap, low[strip:], gap, lead, high[:strip], lead, low[:strip]])
     rows1 = order1.shape[0]
-    order0, order1 = jnp.asarray(order0), jnp.asarray(order1)
+    order0, order1 = jnp.asarray(order0)[None], jnp.asarray(order1)[None]
 
     shape = jax.ShapeDtypeStruct
     piece_shapes = [shape((slots, channels), BF16)] * pieces_count
     attention_scratch = [
-        pltpu.VMEM((channels, 3 * channels), BF16), pltpu.VMEM((channels, channels), BF16),
         pltpu.VMEM((token_count, 3 * channels), BF16), pltpu.VMEM((token_count, channels), BF16),
-        pltpu.SemaphoreType.DMA((2,)),
     ]
 
     layer = 0
     mixed, info, *pieces = call(
         functools.partial(first_kernel, layer=layer, pair_experts=pair_experts),
-        [(place, SCALARS), (temper, SCALARS), (tokens.reshape(token_count, channels), None),
-         (order0[:, None], None), (ids, of_layer(ids, layer)),
-         (norm_gain, of_layer(norm_gain, layer)), (weight_qkv, IN_HBM), (weight_proj, IN_HBM),
-         (router, of_layer(router, layer))],
+        [(place, SCALARS), (temper, SCALARS), (tokens.reshape(token_count, channels), ()),
+         (order0, ()), (ids, (layer,)),
+         (norm_gain, (layer,)), (weight_qkv, (layer,)), (weight_proj, (layer,)), (router, (layer,))],
         [shape((token_count, channels), BF16), shape((token_count, 2), F32)] + piece_shapes,
         attention_scratch,
         flops=4_000_000_000,
     )
     columns1, row1 = call(
         functools.partial(slots_kernel, pair_experts=pair_experts),
-        [(place, SCALARS), (ids, of_layer(ids, 1)), (order1[:, None], None), (info, IN_HBM)],
+        [(place, SCALARS), (ids, (1,)), (order1, ()), (info, IN_VMEM)],
         [shape((rows1, 2), F32), shape((1, rows1), F32)],
         flops=500_000_000,
     )
     produced = moe(pieces, weight_in, weight_out, far_in, far_out, layer)
     north, own, corner, east = call(
         combine_kernel,
-        [(mixed, None), (info, None)] + [(p, None) for p in produced],
+        [(mixed, IN_VMEM), (info, IN_VMEM)] + [(p, IN_VMEM) for p in produced],
         [shape((half, channels), BF16)] * 2 + [shape((edge, channels), BF16)] * 2,
         flops=1_000_000_000,
     )
@@ -476,8 +476,8 @@
     corner = shift(corner, -1, -1)
     low, high, low_edge, high_edge = call(
         functools.partial(shifted_kernel, layer=layer),
-        [(place, SCALARS), (temper, SCALARS), (own, None), (north, None), (east, None), (corner, None),
-         (norm_gain, of_layer(norm_gain, layer)), (weight_qkv, IN_HBM), (weight_proj, IN_HBM)],
+        [(place, SCALARS), (temper, SCALARS), (own, IN_VMEM), (north, IN_VMEM), (east, IN_VMEM), (corner, IN_VMEM),
+         (norm_gain, (layer,)), (weight_qkv, (layer,)), (weight_proj, (layer,))],
         [shape((half, channels), BF16)] * 2 + [shape((edge, channels), BF16)] * 2,
         [pltpu.VMEM((half + edge, channels), F32)] * 2 + attention_scratch,
         flops=3_000_000_000,
@@ -487,15 +487,15 @@
     high_edge = shift(high_edge, 1, 1)
     mixed, info, *pieces = call(
         route_kernel,
-        [(low, None), (high, None), (low_edge, None), (high_edge, None), (columns1, None), (row1, None),
-         (norm_gain, of_layer(norm_gain, layer)), (router, of_layer(router, layer))],
+        [(low, IN_VMEM), (high, IN_VMEM), (low_edge, IN_VMEM), (high_edge, IN_VMEM), (columns1, IN_VMEM),
+         (row1, IN_VMEM), (norm_gain, (layer,)), (router, (layer,))],
         [shape((rows1, channels), BF16), shape((rows1, 2), F32)] + piece_shapes,
         flops=1_000_000_000,
     )
     produced = moe(pieces, weight_in, weight_out, far_in, far_out, layer)
     (out,) = call(
         last_kernel,
-        [(mixed, None), (info, None), (order1[None, :], None)] + [(p, None) for p in produced],
+        [(mixed, IN_VMEM), (info, IN_VMEM), (order1, ())] + [(p, IN_VMEM) for p in produced],
         [shape((token_count, channels), BF16)],
         flops=1_000_000_000,
     )
@@ -512,18 +512,21 @@
         plan = [(0, 0, 0), (1, 0, 0)]
     places = sorted({place for _, _, place in plan})
     groups = [places[: len(places) // 2], places[len(places) // 2 :]] if len(places) > 1 else [places]
-    near, away = range(count // 2), range(count // 2, count)
-    arrived = {k: between(pieces[k], 2 * k) for k in away}
-    arrived.update({k: between(pieces[k], 2 * k) if k else pieces[k] for k in near})
+    away = list(range(count // 2, count))
+    beside = list(range(1, count // 2))
+    arrived = {k: between(pieces[k], 2 * k) for k in away + beside}
+    own, held = run_near(pieces[0], [own_in, own_out, far_in, far_out], plan, layer)
     back = {k: [] for k in range(count)}
-    outs, held = run_near([arrived[k] for k in near], [own_in, own_out, far_in, far_out], plan, layer)
-    for k, value in zip(near, outs):
-        back[k].append(between(value, 2 * k) if k else value)
-    for group in groups:
+    kept = []
+    for turn, group in enumerate(groups):
         units = [(unit, place) for unit, (_, _, place) in enumerate(plan) if place in group]
-        outs = run_away([arrived[k] for k in away], held, units, layer)
-        for k, value in zip(away, outs):
+        outs = run_away([arrived[k] for k in beside + away], held, units, kept)
+        kept = outs[: len(beside)]
+        for k, value in zip(away, outs[len(beside) :]):
             back[k].append(between(value, 2 * k))
+    back[0] = [own]
+    for k, value in zip(beside, kept):
+        back[k] = [between(value, 2 * k)]
     return [value for k in range(count) for value in back[k]]
 
 

time: 149 us -> 136 us (0.913)
  Pallas kernels: 64.5 us -> 51.8 us
  local copies, waits for them, and re-layouts: 11.4 us -> 0 us
  starting transfers between devices: 35.8 us -> 44.2 us
  waiting for transfers between devices: 35.3 us -> 38.3 us
    unnamed x74 -> x0, local copies, waits for them, and re-layouts: 11.2 us -> none
    pallas_call x8, Pallas kernels: 54 us -> 44.8 us  [the longest x6 30.5 us: call(): pl.pallas_call(body, in_specs=specs, out_specs=[IN_VMEM] * len(outs), out...]
    ppermute x18, starting transfers between devices: 26.1 us -> 32.5 us  [between(): lax.ppermute(value, 'lon', [(s, s ^ distance) for s in range(sectors)])]
    ppermute x18, waiting for transfers between devices: 29.6 us -> 35 us  [between(): lax.ppermute(value, 'lon', [(s, s ^ distance) for s in range(sectors)])]
    pallas_call x4, Pallas kernels: 10.5 us -> 6.97 us  [run_away(): pl.pallas_call(functools.partial(away_kernel, sources=sources, plan=plan,...]
    ppermute x6, waiting for transfers between devices: 5.7 us -> 3.22 us  [shift(): lax.ppermute(value, ('lat', 'lon'), lat_lon_pairs(lat_step, lon_step))]
    ppermute x6, starting transfers between devices: 9.68 us -> 11.7 us  [shift(): lax.ppermute(value, ('lat', 'lon'), lat_lon_pairs(lat_step, lon_step))]
  transfers between devices with their start and end apart: 24 -> 24, of which waited for: 9 -> 9; matrix products, arithmetic and copies ran while one was open for 1% -> 0% of each run, Pallas kernels for 30% -> 23%
where the time goes in v2:
time: 136 us; the launch traced here: 135 us
  Pallas kernels  51.8 us (38%)
  starting transfers between devices  44.2 us (32%)
  waiting for transfers between devices  38.3 us (28%)
    ppermute x18, waiting for transfers between devices, between(): lax.ppermute(value, 'lon', [(s, s ^ distance) for s in range(sectors)])  35 us
    ppermute x18, starting transfers between devices, between(): lax.ppermute(value, 'lon', [(s, s ^ distance) for s in range(sectors)])  32.5 us
    pallas_call x6, Pallas kernels, call(): pl.pallas_call(body, in_specs=specs, out_specs=[IN_VMEM] * len(outs), out...  30.5 us
    pallas_call x2, Pallas kernels, run_near(): pl.pallas_call(functools.partial(near_kernel, plan=plan, layer=layer), in...  14.4 us
    ppermute x6, starting transfers between devices, shift(): lax.ppermute(value, ('lat', 'lon'), lat_lon_pairs(lat_step, lon_step))  11.7 us
    pallas_call x4, Pallas kernels, run_away(): pl.pallas_call(functools.partial(away_kernel, sources=sources, plan=plan,...  6.97 us
    ppermute x6, waiting for transfers between devices, shift(): lax.ppermute(value, ('lat', 'lon'), lat_lon_pairs(lat_step, lon_step))  3.22 us
  transfers between devices with their start and end apart: 24, of which 9 were waited for; matrix products, arithmetic and copies ran while one was open for 0% of the time, Pallas kernels for 23%

profile of v2, /device:TPU:0, one launch (start us, length us, event | category | flops | bytes accessed | tf_op | source)
XLA Modules:
  0.0 135.2 jit_solution(3248194080245046896)
XLA Ops:
  0.0 0.5 collective-permute-start
  0.5 0.1 collective-permute-start.1
  0.5 0.6 add_bitcast_fusion.refs_0_
  1.1 12.8 %shard_map.109 = (bf16[576,512]{1,0:T(8,128)(2,1)S(1)}, f32[576,2]{1,0:T(8,128)S(1)}, bf16[192,512]{1,0:T(8,128)(2,1)S(1)}, bf16[192,512]{1,0:T(8,128)(2,1)S(1)}...) custom-call(s32[1,3]{1,0:T(1,128)} %add_bitcast_fusion.refs_0_, f32[2,16]{1,0:T(2,128)} %refs_1_.6, ...), custom_call_target="tpu_custom_call" | custom-call | flops 4000000000 | bytes 4832140 | tf_op jit(solution)/shard_map/pallas_call | solution.py:346
  13.9 3.1 %collective-permute-start.2 = (bf16[192,512]{1,0:T(8,128)(2,1)S(1)}, bf16[192,512]{1,0:T(8,128)(2,1)S(1)}, u32[]{:S(2)}, u32[]{:S(2)}) collective-permute-start(bf16[192,512]{1,0:T(8,128)(2,1)S(1)} %get-tuple-element.49), channel_id=1, source_target_pairs={{0,2},{1,3},{2,0},{3,1},{4,6},{5,7},{6,4},{7,5},{8,10},{9,11},{10,... | collective-permute-start | bytes 589832 | tf_op jit(solution)/shard_map/ppermute | solution.py:407
  17.0 2.6 %collective-permute-start.3 = (bf16[192,512]{1,0:T(8,128)(2,1)S(1)}, bf16[192,512]{1,0:T(8,128)(2,1)S(1)}, u32[]{:S(2)}, u32[]{:S(2)}) collective-permute-start(bf16[192,512]{1,0:T(8,128)(2,1)S(1)} %get-tuple-element.50), channel_id=1, source_target_pairs={{0,4},{1,5},{2,6},{3,7},{4,0},{5,1},{6,2},{7,3},{8,12},{9,13},{10,... | collective-permute-start | bytes 589832 | tf_op jit(solution)/shard_map/ppermute | solution.py:407
  19.6 0.0 collective-permute-start.4
  19.6 0.0 collective-permute-done.refs_3_
  19.6 6.0 %collective-permute-done.1.refs_4_ = bf16[2,4,1024,512]{3,2,1,0:T(8,128)(2,1)} collective-permute-done((bf16[2,4,1024,512]{3,2,1,0:T(8,128)(2,1)}, bf16[2,4,1024,512]{3,2,1,0:T(8,128)(2,1)}, u32[]{:S(2)}, u32[]{:S(2)}) %collective-permute-start.1) | collective-permute-done | bytes 8388640 | tf_op jit(solution)/shard_map/ppermute | solution.py:407
  25.6 7.3 %shard_map.110 = (bf16[192,512]{1,0:T(8,128)(2,1)S(1)}, bf16[8,512,1024]{2,1,0:T(8,128)(2,1)S(1)}, bf16[8,1024,512]{2,1,0:T(8,128)(2,1)S(1)}) custom-call(bf16[192,512]{1,0:T(8,128)(2,1)S(1)} %get-tuple-element.47.refs_0_, bf16[2,4,512,1024]{3,2,1,0:T(8,128)(2,1)} %refs_1_.7, bf16[2,4,1024,512]{3,2,1,0:T(8,128)(2,1)} %refs_2_.3, ...), custom_call_target="tpu_custom_call" | custom-call | flops 4000000000 | bytes 16777216 | tf_op jit(solution)/shard_map/pallas_call | solution.py:360
  32.9 0.0 collective-permute-done.2.refs_0_
  32.9 1.2 collective-permute-done.3.refs_1_
  34.1 0.0 collective-permute-done.4.refs_2_
  34.1 1.7 %shard_map.111 = (bf16[96,512]{1,0:T(8,128)(2,1)S(1)}, bf16[96,512]{1,0:T(8,128)(2,1)S(1)}, bf16[96,512]{1,0:T(8,128)(2,1)S(1)}) custom-call(bf16[192,512]{1,0:T(8,128)(2,1)S(1)} %collective-permute-done.2.refs_0_, bf16[192,512]{1,0:T(8,128)(2,1)S(1)} %collective-permute-done.3.refs_1_, bf16[192,512]{1,0:T(8,128)(2,1)S(1)} %collective-permute-done.4.refs_2_, ...), custom_call_target="tpu_custom_call" | custom-call | flops 3000000000 | bytes 1048576 | tf_op jit(solution)/shard_map/pallas_call | solution.py:381
  35.8 1.7 %shard_map.112 = (bf16[192,512]{1,0:T(8,128)(2,1)S(1)}, bf16[96,512]{1,0:T(8,128)(2,1)S(1)}, bf16[96,512]{1,0:T(8,128)(2,1)S(1)}) custom-call(bf16[192,512]{1,0:T(8,128)(2,1)S(1)} %collective-permute-done.2.refs_0_, bf16[192,512]{1,0:T(8,128)(2,1)S(1)} %collective-permute-done.3.refs_1_, bf16[192,512]{1,0:T(8,128)(2,1)S(1)} %collective-permute-done.4.refs_2_, ...), custom_call_target="tpu_custom_call" | custom-call | flops 3000000000 | bytes 1048576 | tf_op jit(solution)/shard_map/pallas_call | solution.py:381
  37.6 3.6 %collective-permute-start.5 = (bf16[192,512]{1,0:T(8,128)(2,1)S(1)}, bf16[192,512]{1,0:T(8,128)(2,1)S(1)}, u32[]{:S(2)}, u32[]{:S(2)}) collective-permute-start(bf16[192,512]{1,0:T(8,128)(2,1)S(1)} %get-tuple-element.55), channel_id=1, source_target_pairs={{0,2},{1,3},{2,0},{3,1},{4,6},{5,7},{6,4},{7,5},{8,10},{9,11},{10,... | collective-permute-start | bytes 589832 | tf_op jit(solution)/shard_map/ppermute | solution.py:407
  41.2 1.1 collective-permute-start.6
  42.3 1.9 %collective-permute-start.7 = (bf16[96,512]{1,0:T(8,128)(2,1)S(1)}, bf16[96,512]{1,0:T(8,128)(2,1)S(1)}, u32[]{:S(2)}, u32[]{:S(2)}) collective-permute-start(bf16[96,512]{1,0:T(8,128)(2,1)S(1)} %get-tuple-element.57), channel_id=1, source_target_pairs={{0,4},{1,5},{2,6},{3,7},{4,0},{5,1},{6,2},{7,3},{8,12},{9,13},{10,... | collective-permute-start | bytes 294920 | tf_op jit(solution)/shard_map/ppermute | solution.py:407
  44.2 2.5 %collective-permute-start.8 = (bf16[96,512]{1,0:T(8,128)(2,1)S(1)}, bf16[96,512]{1,0:T(8,128)(2,1)S(1)}, u32[]{:S(2)}, u32[]{:S(2)}) collective-permute-start(bf16[96,512]{1,0:T(8,128)(2,1)S(1)} %get-tuple-element.58), channel_id=1, source_target_pairs={{0,6},{1,7},{2,4},{3,5},{4,2},{5,3},{6,0},{7,1},{8,14},{9,15},{10,... | collective-permute-start | bytes 294920 | tf_op jit(solution)/shard_map/ppermute | solution.py:407
  46.6 1.4 %collective-permute-start.9 = (bf16[96,512]{1,0:T(8,128)(2,1)S(1)}, bf16[96,512]{1,0:T(8,128)(2,1)S(1)}, u32[]{:S(2)}, u32[]{:S(2)}) collective-permute-start(bf16[96,512]{1,0:T(8,128)(2,1)S(1)} %get-tuple-element.59), channel_id=1, source_target_pairs={{0,6},{1,7},{2,4},{3,5},{4,2},{5,3},{6,0},{7,1},{8,14},{9,15},{10,... | collective-permute-start | bytes 294920 | tf_op jit(solution)/shard_map/ppermute | solution.py:407
  48.0 7.9 %collective-permute-done.6.refs_4_ = bf16[96,512]{1,0:T(8,128)(2,1)S(1)} collective-permute-done((bf16[96,512]{1,0:T(8,128)(2,1)S(1)}, bf16[96,512]{1,0:T(8,128)(2,1)S(1)}, u32[]{:S(2)}, u32[]{:S(2)}) %collective-permute-start.6) | collective-permute-done | bytes 98336 | tf_op jit(solution)/shard_map/ppermute | solution.py:407
  55.9 2.1 %collective-permute-done.7.refs_5_ = bf16[96,512]{1,0:T(8,128)(2,1)S(1)} collective-permute-done((bf16[96,512]{1,0:T(8,128)(2,1)S(1)}, bf16[96,512]{1,0:T(8,128)(2,1)S(1)}, u32[]{:S(2)}, u32[]{:S(2)}) %collective-permute-start.7) | collective-permute-done | bytes 98336 | tf_op jit(solution)/shard_map/ppermute | solution.py:407
  58.0 0.0 collective-permute-done.8.refs_6_
  58.0 0.0 collective-permute-done.9.refs_7_
  58.0 0.0 collective-permute-done.5.refs_3_
  58.0 0.7 shard_map.113
  58.7 2.5 %collective-permute-start.10 = (bf16[288,512]{1,0:T(8,128)(2,1)S(1)}, bf16[288,512]{1,0:T(8,128)(2,1)S(1)}, u32[]{:S(2)}, u32[]{:S(2)}) collective-permute-start(bf16[288,512]{1,0:T(8,128)(2,1)S(1)} %get-tuple-element.61), channel_id=1, source_target_pairs={{0,24},{1,25},{2,26},{3,27},{4,28},{5,29},{6,30},{7,31},{8,0},{9,1... | collective-permute-start | bytes 884744 | tf_op jit(solution)/shard_map/ppermute | solution.py:402
  61.2 0.0 collective-permute-start.11
  61.2 2.1 %collective-permute-start.12 = (bf16[48,512]{1,0:T(8,128)(2,1)S(1)}, bf16[48,512]{1,0:T(8,128)(2,1)S(1)}, u32[]{:S(2)}, u32[]{:S(2)}) collective-permute-start(bf16[48,512]{1,0:T(8,128)(2,1)S(1)} %get-tuple-element.63), channel_id=1, source_target_pairs={{0,31},{1,24},{2,25},{3,26},{4,27},{5,28},{6,29},{7,30},{8,7},{9,0... | collective-permute-start | bytes 147464 | tf_op jit(solution)/shard_map/ppermute | solution.py:402
  63.3 0.0 collective-permute-done.11.refs_4_
  63.3 2.0 %collective-permute-done.12.refs_5_ = bf16[48,512]{1,0:T(8,128)(2,1)S(1)} collective-permute-done((bf16[48,512]{1,0:T(8,128)(2,1)S(1)}, bf16[48,512]{1,0:T(8,128)(2,1)S(1)}, u32[]{:S(2)}, u32[]{:S(2)}) %collective-permute-start.12) | collective-permute-done | bytes 49184 | tf_op jit(solution)/shard_map/ppermute | solution.py:402
  65.3 1.2 collective-permute-done.10.refs_3_
  66.6 9.0 %shard_map.114 = (bf16[288,512]{1,0:T(8,128)(2,1)S(1)}, bf16[288,512]{1,0:T(8,128)(2,1)S(1)}, bf16[48,512]{1,0:T(8,128)(2,1)S(1)}, bf16[48,512]{1,0:T(8,128)(2,1)S(1)}) custom-call(s32[1,3]{1,0:T(1,128)} %add_bitcast_fusion.refs_0_, f32[2,16]{1,0:T(2,128)} %refs_1_.6, bf16[288,512]{1,0:T(8,128)(2,1)S(1)} %get-tuple-element.60.refs_2_, ...), custom_call_target="tpu_custom_call" | custom-call | flops 3000000000 | bytes 4890764 | tf_op jit(solution)/shard_map/pallas_call | solution.py:346
  75.6 2.4 %collective-permute-start.13 = (bf16[288,512]{1,0:T(8,128)(2,1)S(1)}, bf16[288,512]{1,0:T(8,128)(2,1)S(1)}, u32[]{:S(2)}, u32[]{:S(2)}) collective-permute-start(bf16[288,512]{1,0:T(8,128)(2,1)S(1)} %get-tuple-element.65), channel_id=1, source_target_pairs={{0,8},{1,9},{2,10},{3,11},{4,12},{5,13},{6,14},{7,15},{8,16},{9,17... | collective-permute-start | bytes 884744 | tf_op jit(solution)/shard_map/ppermute | solution.py:402
  78.0 0.0 collective-permute-start.14
  78.0 4.7 %collective-permute-start.15 = (bf16[48,512]{1,0:T(8,128)(2,1)S(1)}, bf16[48,512]{1,0:T(8,128)(2,1)S(1)}, u32[]{:S(2)}, u32[]{:S(2)}) collective-permute-start(bf16[48,512]{1,0:T(8,128)(2,1)S(1)} %get-tuple-element.67), channel_id=1, source_target_pairs={{0,9},{1,10},{2,11},{3,12},{4,13},{5,14},{6,15},{7,8},{8,17},{9,18... | collective-permute-start | bytes 147464 | tf_op jit(solution)/shard_map/ppermute | solution.py:402
  82.7 3.6 %shard_map.115 = (f32[672,2]{1,0:T(8,128)S(1)}, f32[1,672]{1,0:T(1,128)S(1)}) custom-call(s32[1,3]{1,0:T(1,128)} %add_bitcast_fusion.refs_0_, s32[2,1,576]{2,1,0:T(1,128)} %bitcast.13, s32[1,672]{1,0:T(1,128)} %constant.46.refs_2_, f32[576,2]{1,0:T(8,128)S(1)} %get-tuple-element.46.refs_1_.refs_3_), custom_call_target="tpu_custom_call" | custom-call | flops 500000000 | bytes 11916 | tf_op jit(solution)/shard_map/pallas_call | solution.py:346
  86.3 0.0 collective-permute-done.14.refs_2_
  86.3 0.0 collective-permute-done.15.refs_3_
  86.3 0.0 collective-permute-done.13.refs_1_
  86.4 2.1 %shard_map.116 = (bf16[672,512]{1,0:T(8,128)(2,1)S(1)}, f32[672,2]{1,0:T(8,128)S(1)}, bf16[192,512]{1,0:T(8,128)(2,1)S(1)}, bf16[192,512]{1,0:T(8,128)(2,1)S(1)}...) custom-call(bf16[288,512]{1,0:T(8,128)(2,1)S(1)} %get-tuple-element.64.refs_0_, ...), custom_call_target="tpu_custom_call" | custom-call | flops 1000000000 | bytes 737152 | tf_op jit(solution)/shard_map/pallas_call | solution.py:346
  88.5 2.8 %collective-permute-start.16 = (bf16[192,512]{1,0:T(8,128)(2,1)S(1)}, bf16[192,512]{1,0:T(8,128)(2,1)S(1)}, u32[]{:S(2)}, u32[]{:S(2)}) collective-permute-start(bf16[192,512]{1,0:T(8,128)(2,1)S(1)} %get-tuple-element.74), channel_id=1, source_target_pairs={{0,2},{1,3},{2,0},{3,1},{4,6},{5,7},{6,4},{7,5},{8,10},{9,11},{10,... | collective-permute-start | bytes 589832 | tf_op jit(solution)/shard_map/ppermute | solution.py:407
  91.3 0.9 collective-permute-start.17
  92.2 1.6 %collective-permute-start.18 = (bf16[192,512]{1,0:T(8,128)(2,1)S(1)}, bf16[192,512]{1,0:T(8,128)(2,1)S(1)}, u32[]{:S(2)}, u32[]{:S(2)}) collective-permute-start(bf16[192,512]{1,0:T(8,128)(2,1)S(1)} %get-tuple-element.76), channel_id=1, source_target_pairs={{0,6},{1,7},{2,4},{3,5},{4,2},{5,3},{6,0},{7,1},{8,14},{9,15},{10,... | collective-permute-start | bytes 589832 | tf_op jit(solution)/shard_map/ppermute | solution.py:407
  93.7 7.1 %shard_map.117 = (bf16[192,512]{1,0:T(8,128)(2,1)S(1)}, bf16[8,512,1024]{2,1,0:T(8,128)(2,1)S(1)}, bf16[8,1024,512]{2,1,0:T(8,128)(2,1)S(1)}) custom-call(bf16[192,512]{1,0:T(8,128)(2,1)S(1)} %get-tuple-element.72.refs_0_, bf16[2,4,512,1024]{3,2,1,0:T(8,128)(2,1)} %refs_1_.7, bf16[2,4,1024,512]{3,2,1,0:T(8,128)(2,1)} %refs_2_.3, ...), custom_call_target="tpu_custom_call" | custom-call | flops 4000000000 | bytes 16777216 | tf_op jit(solution)/shard_map/pallas_call | solution.py:360
  100.8 0.0 collective-permute-done.16.refs_0_
  100.9 7.6 %collective-permute-done.17.refs_1_ = bf16[192,512]{1,0:T(8,128)(2,1)S(1)} collective-permute-done((bf16[192,512]{1,0:T(8,128)(2,1)S(1)}, bf16[192,512]{1,0:T(8,128)(2,1)S(1)}, u32[]{:S(2)}, u32[]{:S(2)}) %collective-permute-start.17) | collective-permute-done | bytes 196640 | tf_op jit(solution)/shard_map/ppermute | solution.py:407
  108.4 0.0 collective-permute-done.18.refs_2_
  108.4 1.7 %shard_map.118 = (bf16[96,512]{1,0:T(8,128)(2,1)S(1)}, bf16[96,512]{1,0:T(8,128)(2,1)S(1)}, bf16[96,512]{1,0:T(8,128)(2,1)S(1)}) custom-call(bf16[192,512]{1,0:T(8,128)(2,1)S(1)} %collective-permute-done.16.refs_0_, bf16[192,512]{1,0:T(8,128)(2,1)S(1)} %collective-permute-done.17.refs_1_, bf16[192,512]{1,0:T(8,128)(2,1)S(1)} %collective-permute-done.18.refs_2_, ...), custom_call_target="tpu_custom_call" | custom-call | flops 3000000000 | bytes 1048576 | tf_op jit(solution)/shard_map/pallas_call | solution.py:381
  110.2 1.7 %shard_map.119 = (bf16[192,512]{1,0:T(8,128)(2,1)S(1)}, bf16[96,512]{1,0:T(8,128)(2,1)S(1)}, bf16[96,512]{1,0:T(8,128)(2,1)S(1)}) custom-call(bf16[192,512]{1,0:T(8,128)(2,1)S(1)} %collective-permute-done.16.refs_0_, bf16[192,512]{1,0:T(8,128)(2,1)S(1)} %collective-permute-done.17.refs_1_, bf16[192,512]{1,0:T(8,128)(2,1)S(1)} %collective-permute-done.18.refs_2_, ...), custom_call_target="tpu_custom_call" | custom-call | flops 3000000000 | bytes 1048576 | tf_op jit(solution)/shard_map/pallas_call | solution.py:381
  111.9 4.0 %collective-permute-start.19 = (bf16[192,512]{1,0:T(8,128)(2,1)S(1)}, bf16[192,512]{1,0:T(8,128)(2,1)S(1)}, u32[]{:S(2)}, u32[]{:S(2)}) collective-permute-start(bf16[192,512]{1,0:T(8,128)(2,1)S(1)} %get-tuple-element.80), channel_id=1, source_target_pairs={{0,2},{1,3},{2,0},{3,1},{4,6},{5,7},{6,4},{7,5},{8,10},{9,11},{10,... | collective-permute-start | bytes 589832 | tf_op jit(solution)/shard_map/ppermute | solution.py:407
  115.9 0.4 collective-permute-start.20
  116.3 2.6 %collective-permute-start.21 = (bf16[96,512]{1,0:T(8,128)(2,1)S(1)}, bf16[96,512]{1,0:T(8,128)(2,1)S(1)}, u32[]{:S(2)}, u32[]{:S(2)}) collective-permute-start(bf16[96,512]{1,0:T(8,128)(2,1)S(1)} %get-tuple-element.82), channel_id=1, source_target_pairs={{0,4},{1,5},{2,6},{3,7},{4,0},{5,1},{6,2},{7,3},{8,12},{9,13},{10,... | collective-permute-start | bytes 294920 | tf_op jit(solution)/shard_map/ppermute | solution.py:407
  118.8 1.8 %collective-permute-start.22 = (bf16[96,512]{1,0:T(8,128)(2,1)S(1)}, bf16[96,512]{1,0:T(8,128)(2,1)S(1)}, u32[]{:S(2)}, u32[]{:S(2)}) collective-permute-start(bf16[96,512]{1,0:T(8,128)(2,1)S(1)} %get-tuple-element.83), channel_id=1, source_target_pairs={{0,6},{1,7},{2,4},{3,5},{4,2},{5,3},{6,0},{7,1},{8,14},{9,15},{10,... | collective-permute-start | bytes 294920 | tf_op jit(solution)/shard_map/ppermute | solution.py:407
  120.6 2.1 %collective-permute-start.23 = (bf16[96,512]{1,0:T(8,128)(2,1)S(1)}, bf16[96,512]{1,0:T(8,128)(2,1)S(1)}, u32[]{:S(2)}, u32[]{:S(2)}) collective-permute-start(bf16[96,512]{1,0:T(8,128)(2,1)S(1)} %get-tuple-element.84), channel_id=1, source_target_pairs={{0,6},{1,7},{2,4},{3,5},{4,2},{5,3},{6,0},{7,1},{8,14},{9,15},{10,... | collective-permute-start | bytes 294920 | tf_op jit(solution)/shard_map/ppermute | solution.py:407
  122.6 8.1 %collective-permute-done.20.refs_5_ = bf16[96,512]{1,0:T(8,128)(2,1)S(1)} collective-permute-done((bf16[96,512]{1,0:T(8,128)(2,1)S(1)}, bf16[96,512]{1,0:T(8,128)(2,1)S(1)}, u32[]{:S(2)}, u32[]{:S(2)}) %collective-permute-start.20) | collective-permute-done | bytes 98336 | tf_op jit(solution)/shard_map/ppermute | solution.py:407
  130.7 2.1 %collective-permute-done.21.refs_6_ = bf16[96,512]{1,0:T(8,128)(2,1)S(1)} collective-permute-done((bf16[96,512]{1,0:T(8,128)(2,1)S(1)}, bf16[96,512]{1,0:T(8,128)(2,1)S(1)}, u32[]{:S(2)}, u32[]{:S(2)}) %collective-permute-start.21) | collective-permute-done | bytes 98336 | tf_op jit(solution)/shard_map/ppermute | solution.py:407
  132.8 0.0 collective-permute-done.22.refs_7_
  132.8 0.0 collective-permute-done.23.refs_8_
  132.8 0.0 collective-permute-done.19.refs_4_
  132.8 2.2 %shard_map.120 = bf16[576,512]{1,0:T(8,128)(2,1)} custom-call(bf16[672,512]{1,0:T(8,128)(2,1)S(1)} %get-tuple-element.70.refs_0_, f32[672,2]{1,0:T(8,128)S(1)} %get-tuple-element.71.refs_1_, s32[1,672]{1,0:T(1,128)} %constant.46.refs_2_, bf16[192,512]{1,0:T(8,128)(2,1)S(1)} %get-tuple-element.73.refs_3_, ...), custom_call_target="tpu_custom_call" | custom-call | flops 1000000000 | bytes 1482624 | tf_op jit(solution)/shard_map/pallas_call | solution.py:346
Async XLA Ops:
  0.0 19.6 %collective-permute-start = (bf16[2,4,512,1024]{3,2,1,0:T(8,128)(2,1)}, bf16[2,4,512,1024]{3,2,1,0:T(8,128)(2,1)}, u32[]{:S(2)}, u32[]{:S(2)}) collective-permute-start(bf16[2,4,512,1024]{3,2,1,0:T(8,128)(2,1)} %refs_1_.7), channel_id=1, source_target_pairs={{0,1},{1,0},{2,3},{3,2},{4,5},{5,4},{6,7},{7,6},{8,9},{9,8},{10,11... | collective-permute-start | bytes 25165832 | tf_op jit(solution)/shard_map/ppermute | solution.py:407
  0.5 25.1 %collective-permute-start.1 = (bf16[2,4,1024,512]{3,2,1,0:T(8,128)(2,1)}, bf16[2,4,1024,512]{3,2,1,0:T(8,128)(2,1)}, u32[]{:S(2)}, u32[]{:S(2)}) collective-permute-start(bf16[2,4,1024,512]{3,2,1,0:T(8,128)(2,1)} %refs_2_.3), channel_id=1, source_target_pairs={{0,1},{1,0},{2,3},{3,2},{4,5},{5,4},{6,7},{7,6},{8,9},{9,8},{10,11... | collective-permute-start | bytes 25165832 | tf_op jit(solution)/shard_map/ppermute | solution.py:407
  13.9 19.0 %collective-permute-start.2 = (bf16[192,512]{1,0:T(8,128)(2,1)S(1)}, bf16[192,512]{1,0:T(8,128)(2,1)S(1)}, u32[]{:S(2)}, u32[]{:S(2)}) collective-permute-start(bf16[192,512]{1,0:T(8,128)(2,1)S(1)} %get-tuple-element.49), channel_id=1, source_target_pairs={{0,2},{1,3},{2,0},{3,1},{4,6},{5,7},{6,4},{7,5},{8,10},{9,11},{10,... | collective-permute-start | bytes 589832 | tf_op jit(solution)/shard_map/ppermute | solution.py:407
  17.0 17.1 %collective-permute-start.3 = (bf16[192,512]{1,0:T(8,128)(2,1)S(1)}, bf16[192,512]{1,0:T(8,128)(2,1)S(1)}, u32[]{:S(2)}, u32[]{:S(2)}) collective-permute-start(bf16[192,512]{1,0:T(8,128)(2,1)S(1)} %get-tuple-element.50), channel_id=1, source_target_pairs={{0,4},{1,5},{2,6},{3,7},{4,0},{5,1},{6,2},{7,3},{8,12},{9,13},{10,... | collective-permute-start | bytes 589832 | tf_op jit(solution)/shard_map/ppermute | solution.py:407
  19.6 14.5 %collective-permute-start.4 = (bf16[192,512]{1,0:T(8,128)(2,1)S(1)}, bf16[192,512]{1,0:T(8,128)(2,1)S(1)}, u32[]{:S(2)}, u32[]{:S(2)}) collective-permute-start(bf16[192,512]{1,0:T(8,128)(2,1)S(1)} %get-tuple-element.51), channel_id=1, source_target_pairs={{0,6},{1,7},{2,4},{3,5},{4,2},{5,3},{6,0},{7,1},{8,14},{9,15},{10,... | collective-permute-start | bytes 589832 | tf_op jit(solution)/shard_map/ppermute | solution.py:407
  37.6 20.4 %collective-permute-start.5 = (bf16[192,512]{1,0:T(8,128)(2,1)S(1)}, bf16[192,512]{1,0:T(8,128)(2,1)S(1)}, u32[]{:S(2)}, u32[]{:S(2)}) collective-permute-start(bf16[192,512]{1,0:T(8,128)(2,1)S(1)} %get-tuple-element.55), channel_id=1, source_target_pairs={{0,2},{1,3},{2,0},{3,1},{4,6},{5,7},{6,4},{7,5},{8,10},{9,11},{10,... | collective-permute-start | bytes 589832 | tf_op jit(solution)/shard_map/ppermute | solution.py:407
  41.2 14.7 %collective-permute-start.6 = (bf16[96,512]{1,0:T(8,128)(2,1)S(1)}, bf16[96,512]{1,0:T(8,128)(2,1)S(1)}, u32[]{:S(2)}, u32[]{:S(2)}) collective-permute-start(bf16[96,512]{1,0:T(8,128)(2,1)S(1)} %get-tuple-element.56), channel_id=1, source_target_pairs={{0,4},{1,5},{2,6},{3,7},{4,0},{5,1},{6,2},{7,3},{8,12},{9,13},{10,... | collective-permute-start | bytes 294920 | tf_op jit(solution)/shard_map/ppermute | solution.py:407
  42.3 15.7 %collective-permute-start.7 = (bf16[96,512]{1,0:T(8,128)(2,1)S(1)}, bf16[96,512]{1,0:T(8,128)(2,1)S(1)}, u32[]{:S(2)}, u32[]{:S(2)}) collective-permute-start(bf16[96,512]{1,0:T(8,128)(2,1)S(1)} %get-tuple-element.57), channel_id=1, source_target_pairs={{0,4},{1,5},{2,6},{3,7},{4,0},{5,1},{6,2},{7,3},{8,12},{9,13},{10,... | collective-permute-start | bytes 294920 | tf_op jit(solution)/shard_map/ppermute | solution.py:407
  44.2 13.9 %collective-permute-start.8 = (bf16[96,512]{1,0:T(8,128)(2,1)S(1)}, bf16[96,512]{1,0:T(8,128)(2,1)S(1)}, u32[]{:S(2)}, u32[]{:S(2)}) collective-permute-start(bf16[96,512]{1,0:T(8,128)(2,1)S(1)} %get-tuple-element.58), channel_id=1, source_target_pairs={{0,6},{1,7},{2,4},{3,5},{4,2},{5,3},{6,0},{7,1},{8,14},{9,15},{10,... | collective-permute-start | bytes 294920 | tf_op jit(solution)/shard_map/ppermute | solution.py:407
  46.6 11.4 %collective-permute-start.9 = (bf16[96,512]{1,0:T(8,128)(2,1)S(1)}, bf16[96,512]{1,0:T(8,128)(2,1)S(1)}, u32[]{:S(2)}, u32[]{:S(2)}) collective-permute-start(bf16[96,512]{1,0:T(8,128)(2,1)S(1)} %get-tuple-element.59), channel_id=1, source_target_pairs={{0,6},{1,7},{2,4},{3,5},{4,2},{5,3},{6,0},{7,1},{8,14},{9,15},{10,... | collective-permute-start | bytes 294920 | tf_op jit(solution)/shard_map/ppermute | solution.py:407
  58.7 7.8 %collective-permute-start.10 = (bf16[288,512]{1,0:T(8,128)(2,1)S(1)}, bf16[288,512]{1,0:T(8,128)(2,1)S(1)}, u32[]{:S(2)}, u32[]{:S(2)}) collective-permute-start(bf16[288,512]{1,0:T(8,128)(2,1)S(1)} %get-tuple-element.61), channel_id=1, source_target_pairs={{0,24},{1,25},{2,26},{3,27},{4,28},{5,29},{6,30},{7,31},{8,0},{9,1... | collective-permute-start | bytes 884744 | tf_op jit(solution)/shard_map/ppermute | solution.py:402
  61.2 2.1 %collective-permute-start.11 = (bf16[48,512]{1,0:T(8,128)(2,1)S(1)}, bf16[48,512]{1,0:T(8,128)(2,1)S(1)}, u32[]{:S(2)}, u32[]{:S(2)}) collective-permute-start(bf16[48,512]{1,0:T(8,128)(2,1)S(1)} %get-tuple-element.62), channel_id=1, source_target_pairs={{0,7},{1,0},{2,1},{3,2},{4,3},{5,4},{6,5},{7,6},{8,15},{9,8},{10,9... | collective-permute-start | bytes 147464 | tf_op jit(solution)/shard_map/ppermute | solution.py:402
  61.2 4.1 %collective-permute-start.12 = (bf16[48,512]{1,0:T(8,128)(2,1)S(1)}, bf16[48,512]{1,0:T(8,128)(2,1)S(1)}, u32[]{:S(2)}, u32[]{:S(2)}) collective-permute-start(bf16[48,512]{1,0:T(8,128)(2,1)S(1)} %get-tuple-element.63), channel_id=1, source_target_pairs={{0,31},{1,24},{2,25},{3,26},{4,27},{5,28},{6,29},{7,30},{8,7},{9,0... | collective-permute-start | bytes 147464 | tf_op jit(solution)/shard_map/ppermute | solution.py:402
  75.6 10.7 %collective-permute-start.13 = (bf16[288,512]{1,0:T(8,128)(2,1)S(1)}, bf16[288,512]{1,0:T(8,128)(2,1)S(1)}, u32[]{:S(2)}, u32[]{:S(2)}) collective-permute-start(bf16[288,512]{1,0:T(8,128)(2,1)S(1)} %get-tuple-element.65), channel_id=1, source_target_pairs={{0,8},{1,9},{2,10},{3,11},{4,12},{5,13},{6,14},{7,15},{8,16},{9,17... | collective-permute-start | bytes 884744 | tf_op jit(solution)/shard_map/ppermute | solution.py:402
  78.0 8.3 %collective-permute-start.14 = (bf16[48,512]{1,0:T(8,128)(2,1)S(1)}, bf16[48,512]{1,0:T(8,128)(2,1)S(1)}, u32[]{:S(2)}, u32[]{:S(2)}) collective-permute-start(bf16[48,512]{1,0:T(8,128)(2,1)S(1)} %get-tuple-element.66), channel_id=1, source_target_pairs={{0,1},{1,2},{2,3},{3,4},{4,5},{5,6},{6,7},{7,0},{8,9},{9,10},{10,1... | collective-permute-start | bytes 147464 | tf_op jit(solution)/shard_map/ppermute | solution.py:402
  78.0 8.3 %collective-permute-start.15 = (bf16[48,512]{1,0:T(8,128)(2,1)S(1)}, bf16[48,512]{1,0:T(8,128)(2,1)S(1)}, u32[]{:S(2)}, u32[]{:S(2)}) collective-permute-start(bf16[48,512]{1,0:T(8,128)(2,1)S(1)} %get-tuple-element.67), channel_id=1, source_target_pairs={{0,9},{1,10},{2,11},{3,12},{4,13},{5,14},{6,15},{7,8},{8,17},{9,18... | collective-permute-start | bytes 147464 | tf_op jit(solution)/shard_map/ppermute | solution.py:402
  88.5 12.4 %collective-permute-start.16 = (bf16[192,512]{1,0:T(8,128)(2,1)S(1)}, bf16[192,512]{1,0:T(8,128)(2,1)S(1)}, u32[]{:S(2)}, u32[]{:S(2)}) collective-permute-start(bf16[192,512]{1,0:T(8,128)(2,1)S(1)} %get-tuple-element.74), channel_id=1, source_target_pairs={{0,2},{1,3},{2,0},{3,1},{4,6},{5,7},{6,4},{7,5},{8,10},{9,11},{10,... | collective-permute-start | bytes 589832 | tf_op jit(solution)/shard_map/ppermute | solution.py:407
  91.3 17.1 %collective-permute-start.17 = (bf16[192,512]{1,0:T(8,128)(2,1)S(1)}, bf16[192,512]{1,0:T(8,128)(2,1)S(1)}, u32[]{:S(2)}, u32[]{:S(2)}) collective-permute-start(bf16[192,512]{1,0:T(8,128)(2,1)S(1)} %get-tuple-element.75), channel_id=1, source_target_pairs={{0,4},{1,5},{2,6},{3,7},{4,0},{5,1},{6,2},{7,3},{8,12},{9,13},{10,... | collective-permute-start | bytes 589832 | tf_op jit(solution)/shard_map/ppermute | solution.py:407
  92.2 16.3 %collective-permute-start.18 = (bf16[192,512]{1,0:T(8,128)(2,1)S(1)}, bf16[192,512]{1,0:T(8,128)(2,1)S(1)}, u32[]{:S(2)}, u32[]{:S(2)}) collective-permute-start(bf16[192,512]{1,0:T(8,128)(2,1)S(1)} %get-tuple-element.76), channel_id=1, source_target_pairs={{0,6},{1,7},{2,4},{3,5},{4,2},{5,3},{6,0},{7,1},{8,14},{9,15},{10,... | collective-permute-start | bytes 589832 | tf_op jit(solution)/shard_map/ppermute | solution.py:407
  111.9 20.9 %collective-permute-start.19 = (bf16[192,512]{1,0:T(8,128)(2,1)S(1)}, bf16[192,512]{1,0:T(8,128)(2,1)S(1)}, u32[]{:S(2)}, u32[]{:S(2)}) collective-permute-start(bf16[192,512]{1,0:T(8,128)(2,1)S(1)} %get-tuple-element.80), channel_id=1, source_target_pairs={{0,2},{1,3},{2,0},{3,1},{4,6},{5,7},{6,4},{7,5},{8,10},{9,11},{10,... | collective-permute-start | bytes 589832 | tf_op jit(solution)/shard_map/ppermute | solution.py:407
  115.9 14.8 %collective-permute-start.20 = (bf16[96,512]{1,0:T(8,128)(2,1)S(1)}, bf16[96,512]{1,0:T(8,128)(2,1)S(1)}, u32[]{:S(2)}, u32[]{:S(2)}) collective-permute-start(bf16[96,512]{1,0:T(8,128)(2,1)S(1)} %get-tuple-element.81), channel_id=1, source_target_pairs={{0,4},{1,5},{2,6},{3,7},{4,0},{5,1},{6,2},{7,3},{8,12},{9,13},{10,... | collective-permute-start | bytes 294920 | tf_op jit(solution)/shard_map/ppermute | solution.py:407
  116.3 16.6 %collective-permute-start.21 = (bf16[96,512]{1,0:T(8,128)(2,1)S(1)}, bf16[96,512]{1,0:T(8,128)(2,1)S(1)}, u32[]{:S(2)}, u32[]{:S(2)}) collective-permute-start(bf16[96,512]{1,0:T(8,128)(2,1)S(1)} %get-tuple-element.82), channel_id=1, source_target_pairs={{0,4},{1,5},{2,6},{3,7},{4,0},{5,1},{6,2},{7,3},{8,12},{9,13},{10,... | collective-permute-start | bytes 294920 | tf_op jit(solution)/shard_map/ppermute | solution.py:407
  118.8 14.0 %collective-permute-start.22 = (bf16[96,512]{1,0:T(8,128)(2,1)S(1)}, bf16[96,512]{1,0:T(8,128)(2,1)S(1)}, u32[]{:S(2)}, u32[]{:S(2)}) collective-permute-start(bf16[96,512]{1,0:T(8,128)(2,1)S(1)} %get-tuple-element.83), channel_id=1, source_target_pairs={{0,6},{1,7},{2,4},{3,5},{4,2},{5,3},{6,0},{7,1},{8,14},{9,15},{10,... | collective-permute-start | bytes 294920 | tf_op jit(solution)/shard_map/ppermute | solution.py:407
  120.6 12.3 %collective-permute-start.23 = (bf16[96,512]{1,0:T(8,128)(2,1)S(1)}, bf16[96,512]{1,0:T(8,128)(2,1)S(1)}, u32[]{:S(2)}, u32[]{:S(2)}) collective-permute-start(bf16[96,512]{1,0:T(8,128)(2,1)S(1)} %get-tuple-element.84), channel_id=1, source_target_pairs={{0,6},{1,7},{2,4},{3,5},{4,2},{5,3},{6,0},{7,1},{8,14},{9,15},{10,... | collective-permute-start | bytes 294920 | tf_op jit(solution)/shard_map/ppermute | solution.py:407

commit v3 on v2

--- a/solution.py
+++ b/solution.py
@@ -59,7 +59,7 @@
     return jnp.transpose(jnp.broadcast_to(row.astype(F32), (LANES, row.shape[1])))
 
 
-def slots_of(ids_row, order, place_ref, pair_experts):
+def slots_of(ids_row, reorder, place_ref, pair_experts):
     count = ids_row.shape[1]
     spread_ids = upright(ids_row).astype(jnp.int32)
     ids = spread_ids[:, 0:1]
@@ -67,12 +67,13 @@
     earlier = lax.broadcasted_iota(jnp.int32, (count, count), 0) > lax.broadcasted_iota(jnp.int32, (count, count), 1)
     before = dot(jnp.where(earlier, 1.0, 0.0).astype(BF16), jnp.where(chosen, 1.0, 0.0).astype(BF16))
     place = jnp.sum(jnp.where(chosen, before, 0.0), axis=1, keepdims=True).astype(jnp.int32)
-    piece = lax.div(ids, pair_experts) ^ place_ref[0, 1]
-    inner = lax.rem(ids, pair_experts) ^ (place_ref[0, 2] * (pair_experts // 2))
+    shift_by = pair_experts.bit_length() - 1
+    piece = (ids >> shift_by) ^ place_ref[0, 1]
+    inner = (ids & (pair_experts - 1)) ^ (place_ref[0, 2] * (pair_experts // 2))
     target = (piece * pair_experts + inner) * CAP + place
     lane = lax.broadcasted_iota(jnp.int32, (count, LANES), 1)
-    parts = jnp.where(lane == 0, target // 256, jnp.where(lane == 1, target % 256, jnp.where(lane == 2, ids, 1)))
-    moved = dot(one_hot_columns(order, count), parts.astype(F32).astype(BF16))
+    parts = jnp.where(lane == 0, target >> 8, jnp.where(lane == 1, target & 255, jnp.where(lane == 2, ids, 1)))
+    moved = dot(reorder, parts.astype(F32).astype(BF16))
     slot = jnp.where(moved[:, 3:4] > 0.5, moved[:, 0:1] * 256.0 + moved[:, 1:2], -1.0)
     row = jnp.transpose(jnp.broadcast_to(slot, (slot.shape[0], LANES)))[0:1, :]
     return moved[:, 2:3], slot, row
@@ -83,10 +84,11 @@
     chosen = lax.broadcasted_iota(jnp.int32, logits.shape, 1) == experts.astype(jnp.int32)
     picked = jnp.sum(jnp.where(chosen, logits, 0.0), axis=1, keepdims=True)
     target = target_row.astype(jnp.int32)
-    slots = piece_refs[0].shape[0]
-    for index, piece_ref in enumerate(piece_refs):
-        spread = one_hot_rows(target - index * slots, slots)
-        piece_ref[...] = dot(spread, ynorm).astype(BF16)
+    start = 0
+    for piece_ref in piece_refs:
+        slots = piece_ref.shape[0]
+        piece_ref[...] = dot(one_hot_rows(target - start, slots), ynorm).astype(BF16)
+        start += slots
     return jax.nn.sigmoid(picked)
 
 
@@ -101,7 +103,7 @@
     rest = area - main
     lanes = group * area
     normed = norm_rows(frame, gain.get()[0:1, :])
-    qkv_ref[...] = dot(normed, wqkv.get()).astype(BF16)
+    qkv_ref[...] = dot(normed, wqkv()).astype(BF16)
 
     lane = lax.broadcasted_iota(jnp.int32, (1, lanes), 1)
     leftover = lane >= group * main
@@ -150,7 +152,7 @@
 
     for window in range(windows):
         one_window(window)
-    attended = dot(context_ref[...], wproj.get())
+    attended = dot(context_ref[...], wproj())
     return (frame + attended).astype(BF16)
 
 
@@ -159,26 +161,35 @@
     mixed_ref, info_ref, *refs, layer, pair_experts
 ):
     *piece_refs, qkv_ref, context_ref = refs
-    order = upright(order.get())[:, 0:1].astype(jnp.int32)
-    rows = tokens.get()
-    frame = dot(one_hot_columns(order, rows.shape[0]), rows)
-    mixed = attend(frame, layer, place_ref, temper_ref, gain, wqkv, wproj, qkv_ref, context_ref)
+    reorder = one_hot_columns(upright(order.get())[:, 0:1].astype(jnp.int32), order.target.shape[1])
+    experts, slot, slot_row = slots_of(ids.get(), reorder, place_ref, pair_experts)
+    frame = dot(reorder, tokens.get())
+    mixed = attend(frame, layer, place_ref, temper_ref, gain, wqkv.get, wproj.get, qkv_ref, context_ref)
     mixed_ref[...] = mixed
     ynorm = norm_rows(mixed.astype(F32), gain.get()[1:2, :])
-    experts, slot, slot_row = slots_of(ids.get(), order, place_ref, pair_experts)
     gate = route(ynorm, router.get(), experts, slot_row, piece_refs)
     info_ref[...] = jnp.concatenate([gate, slot], axis=1)
 
 
-def slots_kernel(place_ref, ids, order, _, columns_ref, row_ref, *, pair_experts):
-    order = upright(order.get())[:, 0:1].astype(jnp.int32)
-    experts, slot, slot_row = slots_of(ids.get(), order, place_ref, pair_experts)
+def ahead_kernel(place_ref, ids, order, wqkv_hbm, wproj_hbm, _, columns_ref, row_ref, wqkv_ref, wproj_ref, arrived,
+                 *, layer, pair_experts):
+    copies = [
+        pltpu.make_async_copy(source.at[layer], target, arrived.at[index])
+        for index, (source, target) in enumerate(((wqkv_hbm, wqkv_ref), (wproj_hbm, wproj_ref)))
+    ]
+    for copy in copies:
+        copy.start()
+    ids_row = ids.get()
+    reorder = one_hot_columns(upright(order.get())[:, 0:1].astype(jnp.int32), ids_row.shape[1])
+    experts, slot, slot_row = slots_of(ids_row, reorder, place_ref, pair_experts)
     columns_ref[...] = jnp.concatenate([experts, slot], axis=1)
     row_ref[...] = slot_row
+    for copy in copies:
+        copy.wait()
 
 
 def shifted_kernel(
-    place_ref, temper_ref, own_ref, north_ref, east_ref, corner_ref, gain, wqkv, wproj,
+    place_ref, temper_ref, own_ref, north_ref, east_ref, corner_ref, gain, wqkv_ref, wproj_ref,
     low_ref, high_ref, low_edge_ref, high_edge_ref,
     low_scratch, high_scratch, qkv_ref, context_ref, *, layer
 ):
@@ -195,7 +206,9 @@
         start = strip + window * part
         pieces += [low_scratch[start : start + part], high_scratch[start : start + part]]
     frame = jnp.concatenate(pieces, axis=0)
-    mixed = attend(frame, layer, place_ref, temper_ref, gain, wqkv, wproj, qkv_ref, context_ref)
+    mixed = attend(
+        frame, layer, place_ref, temper_ref, gain, lambda: wqkv_ref[...], lambda: wproj_ref[...], qkv_ref, context_ref
+    )
     mixed = mixed.astype(F32)
     low, high = split_halves(mixed)
     low_ref[...] = low.astype(BF16)
@@ -219,20 +232,21 @@
     info_ref[...] = jnp.concatenate([gate, columns_ref[:, 1:2]], axis=1)
 
 
-def expert_rows(piece_refs, out_refs, block, first, second, carried, last):
-    rows = jnp.concatenate([ref[block, :] for ref in piece_refs], axis=0)
+def expert_rows(piece_refs, starts, out_refs, first, second, carried, last):
+    rows = jnp.concatenate([ref[start : start + CAP, :] for ref, start in zip(piece_refs, starts)], axis=0)
     hidden = jax.nn.gelu(dot(rows, first())).astype(BF16)
     part = dot(hidden, second())
     total = part if carried is None else carried + part
     if last:
-        for index, ref in enumerate(out_refs):
-            ref[block, :] = total[index * CAP : (index + 1) * CAP].astype(BF16)
+        for index, (ref, start) in enumerate(out_refs):
+            ref[start : start + CAP, :] = total[index * CAP : (index + 1) * CAP].astype(BF16)
     return total
 
 
-def near_kernel(*refs, plan, layer):
-    piece_ref, *weights = refs[:5]
-    out_ref, first_ref, second_ref, arrived = refs[5:]
+def near_kernel(*refs, plan, base, layer):
+    piece_ref = refs[0]
+    weights = refs[1:-4]
+    out_ref, first_ref, second_ref, arrived = refs[-4:]
     ahead = 2
     copies = {}
 
@@ -256,35 +270,33 @@
     totals = {}
     last = {place: unit for unit, (_, _, place) in enumerate(plan)}
     for unit, (_, _, place) in enumerate(plan):
-        block = slice(place * CAP, (place + 1) * CAP)
+        start = (place - base) * CAP
         totals[place] = expert_rows(
-            [piece_ref], [out_ref], block,
+            [piece_ref], [start], [(out_ref, start)],
             functools.partial(wait_for, unit, 0, first_ref), functools.partial(wait_for, unit, 1, second_ref),
             totals.get(place), last[place] == unit,
         )
 
 
-def away_kernel(*refs, sources, plan, base, kept):
-    piece_refs = refs[:sources]
-    first_ref, second_ref = refs[sources : sources + 2]
-    kept_refs = refs[sources + 2 : sources + 2 + kept]
-    out_refs = list(refs[sources + 2 + kept :])
+def away_kernel(*refs, whole, cut, plan, base, kept):
+    piece_refs = refs[: whole + cut]
+    first_ref, second_ref = refs[whole + cut : whole + cut + 2]
+    kept_refs = refs[whole + cut + 2 : whole + cut + 2 + kept]
+    out_refs = refs[whole + cut + 2 + kept :]
+    lead = [0] * (whole + cut)
     for index, ref in enumerate(kept_refs):
-        size = ref.shape[0]
-        out_refs[index][0:size, :] = ref[...]
-        out_refs[index] = out_refs[index].at[size:]
+        lead[index] = ref.shape[0]
+        out_refs[index][0 : lead[index], :] = ref[...]
     totals = {}
-    last = {place: unit for unit, place in plan}
-    for unit, place in plan:
-        outs = [ref.at[pl.ds((place - base) * CAP, CAP)] for ref in out_refs]
-        block = slice(place * CAP, (place + 1) * CAP)
-        rows = jnp.concatenate([ref[block, :] for ref in piece_refs], axis=0)
-        hidden = jax.nn.gelu(dot(rows, first_ref[unit])).astype(BF16)
-        part = dot(hidden, second_ref[unit])
-        totals[place] = totals[place] + part if place in totals else part
-        if last[place] == unit:
-            for index, ref in enumerate(outs):
-                ref[...] = totals[place][index * CAP : (index + 1) * CAP].astype(BF16)
+    last = {place: unit for unit, (_, _, place) in enumerate(plan)}
+    for unit, (_, _, place) in enumerate(plan):
+        inner = (place - base) * CAP
+        totals[place] = expert_rows(
+            piece_refs, [place * CAP] * whole + [inner] * cut,
+            [(ref, start + inner) for ref, start in zip(out_refs, lead)],
+            lambda unit=unit: first_ref[unit], lambda unit=unit: second_ref[unit],
+            totals.get(place), last[place] == unit,
+        )
 
 
 def gathered_state(mixed_ref, info_ref, piece_refs):
@@ -294,7 +306,7 @@
     return (mixed_ref[...].astype(F32) + info_ref[:, 0:1] * combined).astype(BF16)
 
 
-def combine_kernel(mixed_ref, info_ref, *refs):
+def combine_kernel(mixed_ref, info_ref, _, *refs):
     *piece_refs, north_ref, own_ref, corner_ref, east_ref = refs
     state = gathered_state(mixed_ref, info_ref, piece_refs).astype(F32)
     low, high = split_halves(state)
@@ -354,34 +366,32 @@
     )(*arrays)
 
 
-def run_near(piece, weights, plan, layer):
+def run_near(piece, weights, plan, base, layer):
     channels, units = piece.shape[1], weights[0].shape[3]
     held = [pltpu.VMEM((len(plan), channels, units), BF16), pltpu.VMEM((len(plan), units, channels), BF16)]
     out, *held = pl.pallas_call(
-        functools.partial(near_kernel, plan=plan, layer=layer),
-        in_specs=[IN_VMEM] + [IN_HBM] * 4,
+        functools.partial(near_kernel, plan=plan, base=base, layer=layer),
+        in_specs=[IN_VMEM] + [IN_HBM] * len(weights),
         out_specs=[IN_VMEM] * 3,
         out_shape=[jax.ShapeDtypeStruct(piece.shape, BF16)] + held,
         scratch_shapes=[pltpu.SemaphoreType.DMA((2, len(plan)))],
         compiler_params=pltpu.CompilerParams(vmem_limit_bytes=24 * MIB),
         cost_estimate=pl.CostEstimate(
-            flops=4_000_000_000, bytes_accessed=len(plan) * 4 * channels * units, transcendentals=0
+            flops=3_000_000_000, bytes_accessed=len(plan) * 4 * channels * units, transcendentals=0
         ),
     )(piece, *[keep_out(w) for w in weights])
     return out, held
 
 
-def run_away(pieces, held, plan, kept):
-    sources = len(pieces)
+def run_away(whole, cut, held, plan, base, kept):
+    pieces = whole + cut
     channels = pieces[0].shape[1]
-    places = [place for _, place in plan]
-    base = min(places)
-    size = (max(places) - base + 1) * CAP
-    sizes = [size + kept[k].shape[0] if k < len(kept) else size for k in range(sources)]
+    size = (max(place for _, _, place in plan) - base + 1) * CAP
+    sizes = [size + rows.shape[0] for rows in kept] + [size] * (len(pieces) - len(kept))
     return pl.pallas_call(
-        functools.partial(away_kernel, sources=sources, plan=plan, base=base, kept=len(kept)),
-        in_specs=[IN_VMEM] * (sources + 2 + len(kept)),
-        out_specs=[IN_VMEM] * sources,
+        functools.partial(away_kernel, whole=len(whole), cut=len(cut), plan=plan, base=base, kept=len(kept)),
+        in_specs=[IN_VMEM] * (len(pieces) + 2 + len(kept)),
+        out_specs=[IN_VMEM] * len(pieces),
         out_shape=[jax.ShapeDtypeStruct((rows, channels), BF16) for rows in sizes],
         compiler_params=pltpu.CompilerParams(vmem_limit_bytes=24 * MIB),
         cost_estimate=pl.CostEstimate(flops=3_000_000_000, bytes_accessed=1 << 20, transcendentals=0),
@@ -441,7 +451,8 @@
     order0, order1 = jnp.asarray(order0)[None], jnp.asarray(order1)[None]
 
     shape = jax.ShapeDtypeStruct
-    piece_shapes = [shape((slots, channels), BF16)] * pieces_count
+    chunks = 2 if local > 1 else 1
+    piece_shapes = [shape((rows, channels), BF16) for rows in piece_sizes(pieces_count, slots, chunks)]
     attention_scratch = [
         pltpu.VMEM((token_count, 3 * channels), BF16), pltpu.VMEM((token_count, channels), BF16),
     ]
@@ -456,16 +467,18 @@
         attention_scratch,
         flops=4_000_000_000,
     )
-    columns1, row1 = call(
-        functools.partial(slots_kernel, pair_experts=pair_experts),
-        [(place, SCALARS), (ids, (1,)), (order1, ()), (info, IN_VMEM)],
-        [shape((rows1, 2), F32), shape((1, rows1), F32)],
-        flops=500_000_000,
-    )
-    produced = moe(pieces, weight_in, weight_out, far_in, far_out, layer)
+    columns1, row1, wqkv1, wproj1 = call(
+        functools.partial(ahead_kernel, layer=1, pair_experts=pair_experts),
+        [(place, SCALARS), (ids, (1,)), (order1, ()), (weight_qkv, UNREAD), (weight_proj, UNREAD), (info, IN_VMEM)],
+        [shape((rows1, 2), F32), shape((1, rows1), F32),
+         pltpu.VMEM((channels, 3 * channels), BF16), pltpu.VMEM((channels, channels), BF16)],
+        [pltpu.SemaphoreType.DMA((2,))],
+        flops=2_000_000_000,
+    )
+    produced = moe(pieces, pieces_count, weight_in, weight_out, far_in, far_out, layer)
     north, own, corner, east = call(
         combine_kernel,
-        [(mixed, IN_VMEM), (info, IN_VMEM)] + [(p, IN_VMEM) for p in produced],
+        [(mixed, IN_VMEM), (info, IN_VMEM), (row1, IN_VMEM)] + [(p, IN_VMEM) for p in produced],
         [shape((half, channels), BF16)] * 2 + [shape((edge, channels), BF16)] * 2,
         flops=1_000_000_000,
     )
@@ -477,7 +490,7 @@
     low, high, low_edge, high_edge = call(
         functools.partial(shifted_kernel, layer=layer),
         [(place, SCALARS), (temper, SCALARS), (own, IN_VMEM), (north, IN_VMEM), (east, IN_VMEM), (corner, IN_VMEM),
-         (norm_gain, (layer,)), (weight_qkv, (layer,)), (weight_proj, (layer,))],
+         (norm_gain, (layer,)), (wqkv1, IN_VMEM), (wproj1, IN_VMEM)],
         [shape((half, channels), BF16)] * 2 + [shape((edge, channels), BF16)] * 2,
         [pltpu.VMEM((half + edge, channels), F32)] * 2 + attention_scratch,
         flops=3_000_000_000,
@@ -492,7 +505,7 @@
         [shape((rows1, channels), BF16), shape((rows1, 2), F32)] + piece_shapes,
         flops=1_000_000_000,
     )
-    produced = moe(pieces, weight_in, weight_out, far_in, far_out, layer)
+    produced = moe(pieces, pieces_count, weight_in, weight_out, far_in, far_out, layer)
     (out,) = call(
         last_kernel,
         [(mixed, IN_VMEM), (info, IN_VMEM), (order1, ())] + [(p, IN_VMEM) for p in produced],
@@ -502,29 +515,56 @@
     return out.reshape(row_count, col_count, channels)
 
 
-def moe(pieces, own_in, own_out, far_in, far_out, layer):
+def after(value, done):
+    return lax.optimization_barrier((value, done))[0]
+
+
+def in_chunks(count, k):
+    return k == 0 or k >= count // 2
+
+
+def piece_sizes(count, slots, chunks):
+    return [n for k in range(count) for n in ([slots // chunks] * chunks if in_chunks(count, k) else [slots])]
+
+
+def moe(flat, count, own_in, own_out, far_in, far_out, layer):
     local = own_in.shape[1]
-    count = len(pieces)
     if local > 1:
-        plan = [(0, entry, entry // 2) for entry in range(local)]
-        plan += [(1, entry, local // 2 + entry // 2) for entry in range(local)]
+        half = local // 2
+        turns = [
+            ([own_in, own_out], [(0, entry, entry // 2) for entry in range(local)], 0),
+            ([far_in, far_out], [(0, entry, half + entry // 2) for entry in range(local)], half),
+        ]
     else:
-        plan = [(0, 0, 0), (1, 0, 0)]
-    places = sorted({place for _, _, place in plan})
-    groups = [places[: len(places) // 2], places[len(places) // 2 :]] if len(places) > 1 else [places]
-    away = list(range(count // 2, count))
-    beside = list(range(1, count // 2))
-    arrived = {k: between(pieces[k], 2 * k) for k in away + beside}
-    own, held = run_near(pieces[0], [own_in, own_out, far_in, far_out], plan, layer)
-    back = {k: [] for k in range(count)}
+        turns = [([own_in, own_out, far_in, far_out], [(0, 0, 0), (1, 0, 0)], 0)]
+    rest = iter(flat)
+    pieces = [[next(rest) for _ in turns] if in_chunks(count, k) else next(rest) for k in range(count)]
+    away = [k for k in range(1, count) if in_chunks(count, k)]
+    beside = [k for k in range(1, count) if not in_chunks(count, k)]
+    own, held, arrived, whole = [], [], [], None
+    for turn, (weights, plan, base) in enumerate(turns):
+        sent = [pieces[k][turn] for k in away]
+        if own:
+            sent = [after(value, own[-1]) for value in sent]
+        arrived.append([between(value, 2 * k) for k, value in zip(away, sent)])
+        if whole is None:
+            whole = [between(pieces[k], 2 * k) for k in beside]
+        piece = pieces[0][turn]
+        if own:
+            piece = after((piece, sent), own[-1])[0]
+        out, weights_here = run_near(piece, weights, plan, base, layer)
+        own.append(out)
+        held.append(weights_here)
+    back = {k: [] for k in away}
     kept = []
-    for turn, group in enumerate(groups):
-        units = [(unit, place) for unit, (_, _, place) in enumerate(plan) if place in group]
-        outs = run_away([arrived[k] for k in beside + away], held, units, kept)
-        kept = outs[: len(beside)]
-        for k, value in zip(away, outs[len(beside) :]):
+    for turn, (_, plan, base) in enumerate(turns):
+        outs = run_away(whole, arrived[turn], held[turn], plan, base, kept)
+        kept = outs[: len(whole)]
+        for k, value in zip(away, outs[len(whole) :]):
+            if back[k]:
+                value = after(value, back[k][-1])
             back[k].append(between(value, 2 * k))
-    back[0] = [own]
+    back[0] = own
     for k, value in zip(beside, kept):
         back[k] = [between(value, 2 * k)]
     return [value for k in range(count) for value in back[k]]

time: 136 us -> 125 us (0.919)
  waiting for transfers between devices: 38.3 us -> 28.6 us
  starting transfers between devices: 44.2 us -> 41.2 us
  Pallas kernels: 51.8 us -> 54.3 us
    ppermute x18 -> x22, waiting for transfers between devices: 35 us -> 18.6 us  [between(): lax.ppermute(value, 'lon', [(s, s ^ distance) for s in range(sectors)])]
    ppermute x6, waiting for transfers between devices: 3.22 us -> 10 us  [shift(): lax.ppermute(value, ('lat', 'lon'), lat_lon_pairs(lat_step, lon_step))]
    ppermute x6, starting transfers between devices: 11.7 us -> 8.26 us  [shift(): lax.ppermute(value, ('lat', 'lon'), lat_lon_pairs(lat_step, lon_step))]
    pallas_call x6 -> x8, Pallas kernels: 21.4 us -> 23.8 us  [the longest x4 16.6 us: run_near(): pl.pallas_call(functools.partial(near_kernel, plan=plan, base=base, layer...]
    ppermute x18 -> x22, starting transfers between devices: 32.5 us -> 32.9 us  [between(): lax.ppermute(value, 'lon', [(s, s ^ distance) for s in range(sectors)])]
  transfers between devices with their start and end apart: 24 -> 28, of which waited for: 9 -> 12; matrix products, arithmetic and copies ran while one was open for 0% -> 0% of each run, Pallas kernels for 23% -> 33%
where the time goes in v3:
time: 125 us
  Pallas kernels  54.3 us (43%)
  starting transfers between devices  41.2 us (33%)
  waiting for transfers between devices  28.6 us (23%)
    ppermute x22, starting transfers between devices, between(): lax.ppermute(value, 'lon', [(s, s ^ distance) for s in range(sectors)])  32.9 us
    pallas_call x6, Pallas kernels, call(): pl.pallas_call(body, in_specs=specs, out_specs=[IN_VMEM] * len(outs), out...  30.5 us
    ppermute x22, waiting for transfers between devices, between(): lax.ppermute(value, 'lon', [(s, s ^ distance) for s in range(sectors)])  18.6 us
    pallas_call x4, Pallas kernels, run_near(): pl.pallas_call(functools.partial(near_kernel, plan=plan, base=base, layer...  16.6 us
    ppermute x6, waiting for transfers between devices, shift(): lax.ppermute(value, ('lat', 'lon'), lat_lon_pairs(lat_step, lon_step))  10 us
    ppermute x6, starting transfers between devices, shift(): lax.ppermute(value, ('lat', 'lon'), lat_lon_pairs(lat_step, lon_step))  8.26 us
    pallas_call x4, Pallas kernels, run_away(): pl.pallas_call(functools.partial(away_kernel, whole=len(whole), cut=len(c...  7.2 us
  transfers between devices with their start and end apart: 28, of which 12 were waited for; matrix products, arithmetic and copies ran while one was open for 0% of the time, Pallas kernels for 33%

profile of v3, /device:TPU:0, one launch (start us, length us, event | category | flops | bytes accessed | tf_op | source)
XLA Modules:
  0.0 125.0 jit_solution(11894400110541886142)
XLA Ops:
  0.0 0.5 collective-permute-start
  0.5 0.1 collective-permute-start.1
  0.5 0.6 add_bitcast_fusion.refs_0_
  1.1 12.9 %shard_map.109 = (bf16[576,512]{1,0:T(8,128)(2,1)S(1)}, f32[576,2]{1,0:T(8,128)S(1)}, bf16[96,512]{1,0:T(8,128)(2,1)S(1)}, bf16[96,512]{1,0:T(8,128)(2,1)S(1)}, ...) custom-call(s32[1,3]{1,0:T(1,128)} %add_bitcast_fusion.refs_0_, ...), custom_call_target="tpu_custom_call" | custom-call | flops 4000000000 | bytes 4832140 | tf_op jit(solution)/shard_map/pallas_call | solution.py:358
  14.0 4.1 %collective-permute-start.5 = (bf16[96,512]{1,0:T(8,128)(2,1)S(1)}, bf16[96,512]{1,0:T(8,128)(2,1)S(1)}, u32[]{:S(2)}, u32[]{:S(2)}) collective-permute-start(bf16[96,512]{1,0:T(8,128)(2,1)S(1)} %get-tuple-element.84), channel_id=1, source_target_pairs={{0,4},{1,5},{2,6},{3,7},{4,0},{5,1},{6,2},{7,3},{8,12},{9,13},{10,... | collective-permute-start | bytes 294920 | tf_op jit(solution)/shard_map/ppermute | solution.py:417
  18.1 1.3 %collective-permute-start.6 = (bf16[96,512]{1,0:T(8,128)(2,1)S(1)}, bf16[96,512]{1,0:T(8,128)(2,1)S(1)}, u32[]{:S(2)}, u32[]{:S(2)}) collective-permute-start(bf16[96,512]{1,0:T(8,128)(2,1)S(1)} %get-tuple-element.85), channel_id=1, source_target_pairs={{0,6},{1,7},{2,4},{3,5},{4,2},{5,3},{6,0},{7,1},{8,14},{9,15},{10,... | collective-permute-start | bytes 294920 | tf_op jit(solution)/shard_map/ppermute | solution.py:417
  19.5 0.2 collective-permute-start.2
  19.7 4.1 %shard_map.111 = (bf16[96,512]{1,0:T(8,128)(2,1)S(1)}, bf16[4,512,1024]{2,1,0:T(8,128)(2,1)S(1)}, bf16[4,1024,512]{2,1,0:T(8,128)(2,1)S(1)}) custom-call(bf16[96,512]{1,0:T(8,128)(2,1)S(1)} %get-tuple-element.72.refs_0_, bf16[2,4,512,1024]{3,2,1,0:T(8,128)(2,1)} %refs_1_.7, bf16[2,4,1024,512]{3,2,1,0:T(8,128)(2,1)} %refs_2_.3), custom_call_target="tpu_custom_call" | custom-call | flops 3000000000 | bytes 8388608 | tf_op jit(solution)/shard_map/pallas_call | solution.py:372
  23.8 2.1 %collective-permute-done.5.refs_1_ = bf16[96,512]{1,0:T(8,128)(2,1)S(1)} collective-permute-done((bf16[96,512]{1,0:T(8,128)(2,1)S(1)}, bf16[96,512]{1,0:T(8,128)(2,1)S(1)}, u32[]{:S(2)}, u32[]{:S(2)}) %collective-permute-start.5) | collective-permute-done | bytes 98336 | tf_op jit(solution)/shard_map/ppermute | solution.py:417
  26.0 0.8 collective-permute-start.3
  26.7 0.0 collective-permute-done.6.refs_2_
  26.7 2.2 %collective-permute-start.4 = (bf16[96,512]{1,0:T(8,128)(2,1)S(1)}, bf16[96,512]{1,0:T(8,128)(2,1)S(1)}, u32[]{:S(2)}, u32[]{:S(2)}) collective-permute-start(bf16[96,512]{1,0:T(8,128)(2,1)S(1)} %get-tuple-element.78), channel_id=1, source_target_pairs={{0,6},{1,7},{2,4},{3,5},{4,2},{5,3},{6,0},{7,1},{8,14},{9,15},{10,... | collective-permute-start | bytes 294920 | tf_op jit(solution)/shard_map/ppermute | solution.py:417
  29.0 0.9 collective-permute-done.2.refs_0_
  29.8 1.9 %shard_map.113 = (bf16[96,512]{1,0:T(8,128)(2,1)S(1)}, bf16[96,512]{1,0:T(8,128)(2,1)S(1)}, bf16[96,512]{1,0:T(8,128)(2,1)S(1)}) custom-call(bf16[192,512]{1,0:T(8,128)(2,1)S(1)} %collective-permute-done.2.refs_0_, bf16[96,512]{1,0:T(8,128)(2,1)S(1)} %collective-permute-done.5.refs_1_, bf16[96,512]{1,0:T(8,128)(2,1)S(1)} %collective-permute-done.6.refs_2_, ...), custom_call_target="tpu_custom_call" | custom-call | flops 3000000000 | bytes 1048576 | tf_op jit(solution)/shard_map/pallas_call | solution.py:391
  31.8 1.2 collective-permute-start.8
  33.0 0.0 collective-permute-done.refs_1_
  33.0 2.6 %collective-permute-start.10 = (bf16[96,512]{1,0:T(8,128)(2,1)S(1)}, bf16[96,512]{1,0:T(8,128)(2,1)S(1)}, u32[]{:S(2)}, u32[]{:S(2)}) collective-permute-start(bf16[96,512]{1,0:T(8,128)(2,1)S(1)} %get-tuple-element.93), channel_id=1, source_target_pairs={{0,6},{1,7},{2,4},{3,5},{4,2},{5,3},{6,0},{7,1},{8,14},{9,15},{10,... | collective-permute-start | bytes 294920 | tf_op jit(solution)/shard_map/ppermute | solution.py:417
  35.6 0.0 collective-permute-done.1.refs_2_
  35.6 4.1 %shard_map.112 = (bf16[96,512]{1,0:T(8,128)(2,1)S(1)}, bf16[4,512,1024]{2,1,0:T(8,128)(2,1)S(1)}, bf16[4,1024,512]{2,1,0:T(8,128)(2,1)S(1)}) custom-call(bf16[96,512]{1,0:T(8,128)(2,1)S(1)} %get-tuple-element.79.refs_0_, bf16[2,4,512,1024]{3,2,1,0:T(8,128)(2,1)} %collective-permute-done.refs_1_, bf16[2,4,1024,512]{3,2,1,0:T(8,128)(2,1)} %collective-permute-done.1.refs_2_), custom_call_target="tpu_custom_call" | custom-call | flops 3000000000 | bytes 8388608 | tf_op jit(solution)/shard_map/pallas_call | solution.py:372
  39.8 0.4 collective-permute-done.3.refs_1_
  40.2 1.7 %shard_map.114 = (bf16[192,512]{1,0:T(8,128)(2,1)S(1)}, bf16[96,512]{1,0:T(8,128)(2,1)S(1)}, bf16[96,512]{1,0:T(8,128)(2,1)S(1)}) custom-call(bf16[192,512]{1,0:T(8,128)(2,1)S(1)} %collective-permute-done.2.refs_0_, bf16[96,512]{1,0:T(8,128)(2,1)S(1)} %collective-permute-done.3.refs_1_, bf16[96,512]{1,0:T(8,128)(2,1)S(1)} %collective-permute-done.4.refs_2_, ...), custom_call_target="tpu_custom_call" | custom-call | flops 3000000000 | bytes 1048576 | tf_op jit(solution)/shard_map/pallas_call | solution.py:391
  41.9 2.7 %collective-permute-start.7 = (bf16[192,512]{1,0:T(8,128)(2,1)S(1)}, bf16[192,512]{1,0:T(8,128)(2,1)S(1)}, u32[]{:S(2)}, u32[]{:S(2)}) collective-permute-start(bf16[192,512]{1,0:T(8,128)(2,1)S(1)} %get-tuple-element.89), channel_id=1, source_target_pairs={{0,2},{1,3},{2,0},{3,1},{4,6},{5,7},{6,4},{7,5},{8,10},{9,11},{10,... | collective-permute-start | bytes 589832 | tf_op jit(solution)/shard_map/ppermute | solution.py:417
  44.7 1.5 %collective-permute-start.11 = (bf16[96,512]{1,0:T(8,128)(2,1)S(1)}, bf16[96,512]{1,0:T(8,128)(2,1)S(1)}, u32[]{:S(2)}, u32[]{:S(2)}) collective-permute-start(bf16[96,512]{1,0:T(8,128)(2,1)S(1)} %get-tuple-element.95), channel_id=1, source_target_pairs={{0,6},{1,7},{2,4},{3,5},{4,2},{5,3},{6,0},{7,1},{8,14},{9,15},{10,... | collective-permute-start | bytes 294920 | tf_op jit(solution)/shard_map/ppermute | solution.py:417
  46.2 1.4 %collective-permute-start.9 = (bf16[96,512]{1,0:T(8,128)(2,1)S(1)}, bf16[96,512]{1,0:T(8,128)(2,1)S(1)}, u32[]{:S(2)}, u32[]{:S(2)}) collective-permute-start(bf16[96,512]{1,0:T(8,128)(2,1)S(1)} %get-tuple-element.92), channel_id=1, source_target_pairs={{0,4},{1,5},{2,6},{3,7},{4,0},{5,1},{6,2},{7,3},{8,12},{9,13},{10,... | collective-permute-start | bytes 294920 | tf_op jit(solution)/shard_map/ppermute | solution.py:417
  47.6 4.2 %shard_map.110 = (f32[672,2]{1,0:T(8,128)S(1)}, f32[1,672]{1,0:T(1,128)S(1)}, bf16[512,1536]{1,0:T(8,128)(2,1)S(1)}, bf16[512,512]{1,0:T(8,128)(2,1)S(1)}) custom-call(s32[1,3]{1,0:T(1,128)} %add_bitcast_fusion.refs_0_, s32[2,1,576]{2,1,0:T(1,128)} %bitcast.13, s32[1,672]{1,0:T(1,128)} %constant.46.refs_2_, bf16[2,512,1536]{2,1,0:T(8,128)(2,1)} %refs_3_.1, ...), custom_call_target="tpu_custom_call" | custom-call | flops 2000000000 | bytes 4206220 | tf_op jit(solution)/shard_map/pallas_call | solution.py:358
  51.7 2.3 %collective-permute-done.11.refs_9_ = bf16[96,512]{1,0:T(8,128)(2,1)S(1)} collective-permute-done((bf16[96,512]{1,0:T(8,128)(2,1)S(1)}, bf16[96,512]{1,0:T(8,128)(2,1)S(1)}, u32[]{:S(2)}, u32[]{:S(2)}) %collective-permute-start.11) | collective-permute-done | bytes 98336 | tf_op jit(solution)/shard_map/ppermute | solution.py:417
  54.1 2.3 %collective-permute-done.9.refs_7_ = bf16[96,512]{1,0:T(8,128)(2,1)S(1)} collective-permute-done((bf16[96,512]{1,0:T(8,128)(2,1)S(1)}, bf16[96,512]{1,0:T(8,128)(2,1)S(1)}, u32[]{:S(2)}, u32[]{:S(2)}) %collective-permute-start.9) | collective-permute-done | bytes 98336 | tf_op jit(solution)/shard_map/ppermute | solution.py:417
  56.3 0.0 collective-permute-done.7.refs_5_
  56.3 0.7 shard_map.115
  57.0 2.5 %collective-permute-start.12 = (bf16[288,512]{1,0:T(8,128)(2,1)S(1)}, bf16[288,512]{1,0:T(8,128)(2,1)S(1)}, u32[]{:S(2)}, u32[]{:S(2)}) collective-permute-start(bf16[288,512]{1,0:T(8,128)(2,1)S(1)} %get-tuple-element.97), channel_id=1, source_target_pairs={{0,24},{1,25},{2,26},{3,27},{4,28},{5,29},{6,30},{7,31},{8,0},{9,1... | collective-permute-start | bytes 884744 | tf_op jit(solution)/shard_map/ppermute | solution.py:412
  59.5 1.3 %collective-permute-start.13 = (bf16[48,512]{1,0:T(8,128)(2,1)S(1)}, bf16[48,512]{1,0:T(8,128)(2,1)S(1)}, u32[]{:S(2)}, u32[]{:S(2)}) collective-permute-start(bf16[48,512]{1,0:T(8,128)(2,1)S(1)} %get-tuple-element.98), channel_id=1, source_target_pairs={{0,7},{1,0},{2,1},{3,2},{4,3},{5,4},{6,5},{7,6},{8,15},{9,8},{10,9... | collective-permute-start | bytes 147464 | tf_op jit(solution)/shard_map/ppermute | solution.py:412
  60.8 1.1 collective-permute-start.14
  62.0 0.6 collective-permute-done.13.refs_4_
  62.6 2.9 %collective-permute-done.14.refs_5_ = bf16[48,512]{1,0:T(8,128)(2,1)S(1)} collective-permute-done((bf16[48,512]{1,0:T(8,128)(2,1)S(1)}, bf16[48,512]{1,0:T(8,128)(2,1)S(1)}, u32[]{:S(2)}, u32[]{:S(2)}) %collective-permute-start.14) | collective-permute-done | bytes 49184 | tf_op jit(solution)/shard_map/ppermute | solution.py:412
  65.5 0.2 collective-permute-done.12.refs_3_
  65.7 8.3 %shard_map.116 = (bf16[288,512]{1,0:T(8,128)(2,1)S(1)}, bf16[288,512]{1,0:T(8,128)(2,1)S(1)}, bf16[48,512]{1,0:T(8,128)(2,1)S(1)}, bf16[48,512]{1,0:T(8,128)(2,1)S(1)}) custom-call(s32[1,3]{1,0:T(1,128)} %add_bitcast_fusion.refs_0_, f32[2,16]{1,0:T(2,128)} %refs_1_.6, bf16[288,512]{1,0:T(8,128)(2,1)S(1)} %get-tuple-element.96.refs_2_, ...), custom_call_target="tpu_custom_call" | custom-call | flops 3000000000 | bytes 2793612 | tf_op jit(solution)/shard_map/pallas_call | solution.py:358
  74.0 2.4 %collective-permute-start.15 = (bf16[288,512]{1,0:T(8,128)(2,1)S(1)}, bf16[288,512]{1,0:T(8,128)(2,1)S(1)}, u32[]{:S(2)}, u32[]{:S(2)}) collective-permute-start(bf16[288,512]{1,0:T(8,128)(2,1)S(1)} %get-tuple-element.103), channel_id=1, source_target_pairs={{0,8},{1,9},{2,10},{3,11},{4,12},{5,13},{6,14},{7,15},{8,16},{9,17... | collective-permute-start | bytes 884744 | tf_op jit(solution)/shard_map/ppermute | solution.py:412
  76.4 0.0 collective-permute-start.16
  76.4 0.9 collective-permute-start.17
  77.3 4.4 %collective-permute-done.16.refs_2_ = bf16[48,512]{1,0:T(8,128)(2,1)S(1)} collective-permute-done((bf16[48,512]{1,0:T(8,128)(2,1)S(1)}, bf16[48,512]{1,0:T(8,128)(2,1)S(1)}, u32[]{:S(2)}, u32[]{:S(2)}) %collective-permute-start.16) | collective-permute-done | bytes 49184 | tf_op jit(solution)/shard_map/ppermute | solution.py:412
  81.7 1.9 %collective-permute-done.17.refs_3_ = bf16[48,512]{1,0:T(8,128)(2,1)S(1)} collective-permute-done((bf16[48,512]{1,0:T(8,128)(2,1)S(1)}, bf16[48,512]{1,0:T(8,128)(2,1)S(1)}, u32[]{:S(2)}, u32[]{:S(2)}) %collective-permute-start.17) | collective-permute-done | bytes 49184 | tf_op jit(solution)/shard_map/ppermute | solution.py:412
  83.6 2.3 %shard_map.117 = (bf16[672,512]{1,0:T(8,128)(2,1)S(1)}, f32[672,2]{1,0:T(8,128)S(1)}, bf16[96,512]{1,0:T(8,128)(2,1)S(1)}, bf16[96,512]{1,0:T(8,128)(2,1)S(1)}, ...) custom-call(bf16[288,512]{1,0:T(8,128)(2,1)S(1)} %get-tuple-element., ...), custom_call_target="tpu_custom_call" | custom-call | flops 1000000000 | bytes 737152 | tf_op jit(solution)/shard_map/pallas_call | solution.py:358
  85.9 0.1 collective-permute-start.21
  86.0 3.9 %collective-permute-start.22 = (bf16[96,512]{1,0:T(8,128)(2,1)S(1)}, bf16[96,512]{1,0:T(8,128)(2,1)S(1)}, u32[]{:S(2)}, u32[]{:S(2)}) collective-permute-start(bf16[96,512]{1,0:T(8,128)(2,1)S(1)} %get-tuple-element.122), channel_id=1, source_target_pairs={{0,6},{1,7},{2,4},{3,5},{4,2},{5,3},{6,0},{7,1},{8,14},{9,15},{10,... | collective-permute-start | bytes 294920 | tf_op jit(solution)/shard_map/ppermute | solution.py:417
  89.8 0.5 collective-permute-start.18
  90.3 4.1 %shard_map.118 = (bf16[96,512]{1,0:T(8,128)(2,1)S(1)}, bf16[4,512,1024]{2,1,0:T(8,128)(2,1)S(1)}, bf16[4,1024,512]{2,1,0:T(8,128)(2,1)S(1)}) custom-call(bf16[96,512]{1,0:T(8,128)(2,1)S(1)} %get-tuple-element.109.refs_0_, bf16[2,4,512,1024]{3,2,1,0:T(8,128)(2,1)} %refs_1_.7, bf16[2,4,1024,512]{3,2,1,0:T(8,128)(2,1)} %refs_2_.3), custom_call_target="tpu_custom_call" | custom-call | flops 3000000000 | bytes 8388608 | tf_op jit(solution)/shard_map/pallas_call | solution.py:372
  94.5 1.5 %collective-permute-start.19 = (bf16[96,512]{1,0:T(8,128)(2,1)S(1)}, bf16[96,512]{1,0:T(8,128)(2,1)S(1)}, u32[]{:S(2)}, u32[]{:S(2)}) collective-permute-start(bf16[96,512]{1,0:T(8,128)(2,1)S(1)} %get-tuple-element.113), channel_id=1, source_target_pairs={{0,4},{1,5},{2,6},{3,7},{4,0},{5,1},{6,2},{7,3},{8,12},{9,13},{10,... | collective-permute-start | bytes 294920 | tf_op jit(solution)/shard_map/ppermute | solution.py:417
  96.0 2.4 %collective-permute-start.20 = (bf16[96,512]{1,0:T(8,128)(2,1)S(1)}, bf16[96,512]{1,0:T(8,128)(2,1)S(1)}, u32[]{:S(2)}, u32[]{:S(2)}) collective-permute-start(bf16[96,512]{1,0:T(8,128)(2,1)S(1)} %get-tuple-element.115), channel_id=1, source_target_pairs={{0,6},{1,7},{2,4},{3,5},{4,2},{5,3},{6,0},{7,1},{8,14},{9,15},{10,... | collective-permute-start | bytes 294920 | tf_op jit(solution)/shard_map/ppermute | solution.py:417
  98.5 4.1 %shard_map.119 = (bf16[96,512]{1,0:T(8,128)(2,1)S(1)}, bf16[4,512,1024]{2,1,0:T(8,128)(2,1)S(1)}, bf16[4,1024,512]{2,1,0:T(8,128)(2,1)S(1)}) custom-call(bf16[96,512]{1,0:T(8,128)(2,1)S(1)} %get-tuple-element.116.refs_0_, bf16[2,4,512,1024]{3,2,1,0:T(8,128)(2,1)} %collective-permute-done.refs_1_, bf16[2,4,1024,512]{3,2,1,0:T(8,128)(2,1)} %collective-permute-done.1.refs_2_), custom_call_target="tpu_custom_call" | custom-call | flops 3000000000 | bytes 8388608 | tf_op jit(solution)/shard_map/pallas_call | solution.py:372
  102.6 0.0 collective-permute-done.21.refs_1_
  102.6 0.0 collective-permute-done.22.refs_2_
  102.6 1.8 %shard_map.120 = (bf16[96,512]{1,0:T(8,128)(2,1)S(1)}, bf16[96,512]{1,0:T(8,128)(2,1)S(1)}, bf16[96,512]{1,0:T(8,128)(2,1)S(1)}) custom-call(bf16[192,512]{1,0:T(8,128)(2,1)S(1)} %collective-permute-done.18.refs_0_, bf16[96,512]{1,0:T(8,128)(2,1)S(1)} %collective-permute-done.21.refs_1_, bf16[96,512]{1,0:T(8,128)(2,1)S(1)} %collective-permute-done.22.refs_2_, ...), custom_call_target="tpu_custom_call" | custom-call | flops 3000000000 | bytes 1048576 | tf_op jit(solution)/shard_map/pallas_call | solution.py:391
  104.4 1.1 collective-permute-start.24
  105.5 0.9 collective-permute-start.26
  106.4 1.8 %shard_map.121 = (bf16[192,512]{1,0:T(8,128)(2,1)S(1)}, bf16[96,512]{1,0:T(8,128)(2,1)S(1)}, bf16[96,512]{1,0:T(8,128)(2,1)S(1)}) custom-call(bf16[192,512]{1,0:T(8,128)(2,1)S(1)} %collective-permute-done.18.refs_0_, bf16[96,512]{1,0:T(8,128)(2,1)S(1)} %collective-permute-done.19.refs_1_, bf16[96,512]{1,0:T(8,128)(2,1)S(1)} %collective-permute-done.20.refs_2_, ...), custom_call_target="tpu_custom_call" | custom-call | flops 3000000000 | bytes 1048576 | tf_op jit(solution)/shard_map/pallas_call | solution.py:391
  108.2 1.6 %collective-permute-start.23 = (bf16[192,512]{1,0:T(8,128)(2,1)S(1)}, bf16[192,512]{1,0:T(8,128)(2,1)S(1)}, u32[]{:S(2)}, u32[]{:S(2)}) collective-permute-start(bf16[192,512]{1,0:T(8,128)(2,1)S(1)} %get-tuple-element.126), channel_id=1, source_target_pairs={{0,2},{1,3},{2,0},{3,1},{4,6},{5,7},{6,4},{7,5},{8,10},{9,11},{10,... | collective-permute-start | bytes 589832 | tf_op jit(solution)/shard_map/ppermute | solution.py:417
  109.8 3.6 %collective-permute-done.24.refs_6_ = bf16[96,512]{1,0:T(8,128)(2,1)S(1)} collective-permute-done((bf16[96,512]{1,0:T(8,128)(2,1)S(1)}, bf16[96,512]{1,0:T(8,128)(2,1)S(1)}, u32[]{:S(2)}, u32[]{:S(2)}) %collective-permute-start.24) | collective-permute-done | bytes 98336 | tf_op jit(solution)/shard_map/ppermute | solution.py:417
  113.4 0.8 collective-permute-start.25
  114.2 0.0 collective-permute-done.26.refs_8_
  114.2 1.4 %collective-permute-start.27 = (bf16[96,512]{1,0:T(8,128)(2,1)S(1)}, bf16[96,512]{1,0:T(8,128)(2,1)S(1)}, u32[]{:S(2)}, u32[]{:S(2)}) collective-permute-start(bf16[96,512]{1,0:T(8,128)(2,1)S(1)} %get-tuple-element.132), channel_id=1, source_target_pairs={{0,6},{1,7},{2,4},{3,5},{4,2},{5,3},{6,0},{7,1},{8,14},{9,15},{10,... | collective-permute-start | bytes 294920 | tf_op jit(solution)/shard_map/ppermute | solution.py:417
  115.6 7.0 %collective-permute-done.25.refs_7_ = bf16[96,512]{1,0:T(8,128)(2,1)S(1)} collective-permute-done((bf16[96,512]{1,0:T(8,128)(2,1)S(1)}, bf16[96,512]{1,0:T(8,128)(2,1)S(1)}, u32[]{:S(2)}, u32[]{:S(2)}) %collective-permute-start.25) | collective-permute-done | bytes 98336 | tf_op jit(solution)/shard_map/ppermute | solution.py:417
  122.6 0.0 collective-permute-done.27.refs_9_
  122.6 0.0 collective-permute-done.23.refs_5_
  122.6 2.2 %shard_map.122 = bf16[576,512]{1,0:T(8,128)(2,1)} custom-call(bf16[672,512]{1,0:T(8,128)(2,1)S(1)} %get-tuple-element.107.refs_0_, f32[672,2]{1,0:T(8,128)S(1)} %get-tuple-element.108.refs_1_, s32[1,672]{1,0:T(1,128)} %constant.46.refs_2_, bf16[96,512]{1,0:T(8,128)(2,1)S(1)} %get-tuple-element.110.refs_3_, bf16[96,512]{1,0:T(8,128)(2,1)S(1)} %get-tuple-element.117.refs_4_, ...), custom_call_target="tpu_custom_call" | custom-call | flops 1000000000 | bytes 1482624 | tf_op jit(solution)/shard_map/pallas_call | solution.py:358
  (7 shorter events, 0.0 us)
Async XLA Ops:
  0.0 33.0 %collective-permute-start = (bf16[2,4,512,1024]{3,2,1,0:T(8,128)(2,1)}, bf16[2,4,512,1024]{3,2,1,0:T(8,128)(2,1)}, u32[]{:S(2)}, u32[]{:S(2)}) collective-permute-start(bf16[2,4,512,1024]{3,2,1,0:T(8,128)(2,1)} %refs_1_.7), channel_id=1, source_target_pairs={{0,1},{1,0},{2,3},{3,2},{4,5},{5,4},{6,7},{7,6},{8,9},{9,8},{10,11... | collective-permute-start | bytes 25165832 | tf_op jit(solution)/shard_map/ppermute | solution.py:417
  0.5 35.2 %collective-permute-start.1 = (bf16[2,4,1024,512]{3,2,1,0:T(8,128)(2,1)}, bf16[2,4,1024,512]{3,2,1,0:T(8,128)(2,1)}, u32[]{:S(2)}, u32[]{:S(2)}) collective-permute-start(bf16[2,4,1024,512]{3,2,1,0:T(8,128)(2,1)} %refs_2_.3), channel_id=1, source_target_pairs={{0,1},{1,0},{2,3},{3,2},{4,5},{5,4},{6,7},{7,6},{8,9},{9,8},{10,11... | collective-permute-start | bytes 25165832 | tf_op jit(solution)/shard_map/ppermute | solution.py:417
  14.0 12.0 %collective-permute-start.5 = (bf16[96,512]{1,0:T(8,128)(2,1)S(1)}, bf16[96,512]{1,0:T(8,128)(2,1)S(1)}, u32[]{:S(2)}, u32[]{:S(2)}) collective-permute-start(bf16[96,512]{1,0:T(8,128)(2,1)S(1)} %get-tuple-element.84), channel_id=1, source_target_pairs={{0,4},{1,5},{2,6},{3,7},{4,0},{5,1},{6,2},{7,3},{8,12},{9,13},{10,... | collective-permute-start | bytes 294920 | tf_op jit(solution)/shard_map/ppermute | solution.py:417
  18.1 8.6 %collective-permute-start.6 = (bf16[96,512]{1,0:T(8,128)(2,1)S(1)}, bf16[96,512]{1,0:T(8,128)(2,1)S(1)}, u32[]{:S(2)}, u32[]{:S(2)}) collective-permute-start(bf16[96,512]{1,0:T(8,128)(2,1)S(1)} %get-tuple-element.85), channel_id=1, source_target_pairs={{0,6},{1,7},{2,4},{3,5},{4,2},{5,3},{6,0},{7,1},{8,14},{9,15},{10,... | collective-permute-start | bytes 294920 | tf_op jit(solution)/shard_map/ppermute | solution.py:417
  19.5 10.4 %collective-permute-start.2 = (bf16[192,512]{1,0:T(8,128)(2,1)S(1)}, bf16[192,512]{1,0:T(8,128)(2,1)S(1)}, u32[]{:S(2)}, u32[]{:S(2)}) collective-permute-start(bf16[192,512]{1,0:T(8,128)(2,1)S(1)} %get-tuple-element.81), channel_id=1, source_target_pairs={{0,2},{1,3},{2,0},{3,1},{4,6},{5,7},{6,4},{7,5},{8,10},{9,11},{10,... | collective-permute-start | bytes 589832 | tf_op jit(solution)/shard_map/ppermute | solution.py:417
  26.0 14.2 %collective-permute-start.3 = (bf16[96,512]{1,0:T(8,128)(2,1)S(1)}, bf16[96,512]{1,0:T(8,128)(2,1)S(1)}, u32[]{:S(2)}, u32[]{:S(2)}) collective-permute-start(bf16[96,512]{1,0:T(8,128)(2,1)S(1)} %get-tuple-element.76), channel_id=1, source_target_pairs={{0,4},{1,5},{2,6},{3,7},{4,0},{5,1},{6,2},{7,3},{8,12},{9,13},{10,... | collective-permute-start | bytes 294920 | tf_op jit(solution)/shard_map/ppermute | solution.py:417
  26.7 13.4 %collective-permute-start.4 = (bf16[96,512]{1,0:T(8,128)(2,1)S(1)}, bf16[96,512]{1,0:T(8,128)(2,1)S(1)}, u32[]{:S(2)}, u32[]{:S(2)}) collective-permute-start(bf16[96,512]{1,0:T(8,128)(2,1)S(1)} %get-tuple-element.78), channel_id=1, source_target_pairs={{0,6},{1,7},{2,4},{3,5},{4,2},{5,3},{6,0},{7,1},{8,14},{9,15},{10,... | collective-permute-start | bytes 294920 | tf_op jit(solution)/shard_map/ppermute | solution.py:417
  31.8 12.9 %collective-permute-start.8 = (bf16[96,512]{1,0:T(8,128)(2,1)S(1)}, bf16[96,512]{1,0:T(8,128)(2,1)S(1)}, u32[]{:S(2)}, u32[]{:S(2)}) collective-permute-start(bf16[96,512]{1,0:T(8,128)(2,1)S(1)} %get-tuple-element.90), channel_id=1, source_target_pairs={{0,4},{1,5},{2,6},{3,7},{4,0},{5,1},{6,2},{7,3},{8,12},{9,13},{10,... | collective-permute-start | bytes 294920 | tf_op jit(solution)/shard_map/ppermute | solution.py:417
  33.0 11.7 %collective-permute-start.10 = (bf16[96,512]{1,0:T(8,128)(2,1)S(1)}, bf16[96,512]{1,0:T(8,128)(2,1)S(1)}, u32[]{:S(2)}, u32[]{:S(2)}) collective-permute-start(bf16[96,512]{1,0:T(8,128)(2,1)S(1)} %get-tuple-element.93), channel_id=1, source_target_pairs={{0,6},{1,7},{2,4},{3,5},{4,2},{5,3},{6,0},{7,1},{8,14},{9,15},{10,... | collective-permute-start | bytes 294920 | tf_op jit(solution)/shard_map/ppermute | solution.py:417
  41.9 14.4 %collective-permute-start.7 = (bf16[192,512]{1,0:T(8,128)(2,1)S(1)}, bf16[192,512]{1,0:T(8,128)(2,1)S(1)}, u32[]{:S(2)}, u32[]{:S(2)}) collective-permute-start(bf16[192,512]{1,0:T(8,128)(2,1)S(1)} %get-tuple-element.89), channel_id=1, source_target_pairs={{0,2},{1,3},{2,0},{3,1},{4,6},{5,7},{6,4},{7,5},{8,10},{9,11},{10,... | collective-permute-start | bytes 589832 | tf_op jit(solution)/shard_map/ppermute | solution.py:417
  44.7 9.4 %collective-permute-start.11 = (bf16[96,512]{1,0:T(8,128)(2,1)S(1)}, bf16[96,512]{1,0:T(8,128)(2,1)S(1)}, u32[]{:S(2)}, u32[]{:S(2)}) collective-permute-start(bf16[96,512]{1,0:T(8,128)(2,1)S(1)} %get-tuple-element.95), channel_id=1, source_target_pairs={{0,6},{1,7},{2,4},{3,5},{4,2},{5,3},{6,0},{7,1},{8,14},{9,15},{10,... | collective-permute-start | bytes 294920 | tf_op jit(solution)/shard_map/ppermute | solution.py:417
  46.2 10.1 %collective-permute-start.9 = (bf16[96,512]{1,0:T(8,128)(2,1)S(1)}, bf16[96,512]{1,0:T(8,128)(2,1)S(1)}, u32[]{:S(2)}, u32[]{:S(2)}) collective-permute-start(bf16[96,512]{1,0:T(8,128)(2,1)S(1)} %get-tuple-element.92), channel_id=1, source_target_pairs={{0,4},{1,5},{2,6},{3,7},{4,0},{5,1},{6,2},{7,3},{8,12},{9,13},{10,... | collective-permute-start | bytes 294920 | tf_op jit(solution)/shard_map/ppermute | solution.py:417
  57.0 8.6 %collective-permute-start.12 = (bf16[288,512]{1,0:T(8,128)(2,1)S(1)}, bf16[288,512]{1,0:T(8,128)(2,1)S(1)}, u32[]{:S(2)}, u32[]{:S(2)}) collective-permute-start(bf16[288,512]{1,0:T(8,128)(2,1)S(1)} %get-tuple-element.97), channel_id=1, source_target_pairs={{0,24},{1,25},{2,26},{3,27},{4,28},{5,29},{6,30},{7,31},{8,0},{9,1... | collective-permute-start | bytes 884744 | tf_op jit(solution)/shard_map/ppermute | solution.py:412
  59.5 3.1 %collective-permute-start.13 = (bf16[48,512]{1,0:T(8,128)(2,1)S(1)}, bf16[48,512]{1,0:T(8,128)(2,1)S(1)}, u32[]{:S(2)}, u32[]{:S(2)}) collective-permute-start(bf16[48,512]{1,0:T(8,128)(2,1)S(1)} %get-tuple-element.98), channel_id=1, source_target_pairs={{0,7},{1,0},{2,1},{3,2},{4,3},{5,4},{6,5},{7,6},{8,15},{9,8},{10,9... | collective-permute-start | bytes 147464 | tf_op jit(solution)/shard_map/ppermute | solution.py:412
  60.8 4.6 %collective-permute-start.14 = (bf16[48,512]{1,0:T(8,128)(2,1)S(1)}, bf16[48,512]{1,0:T(8,128)(2,1)S(1)}, u32[]{:S(2)}, u32[]{:S(2)}) collective-permute-start(bf16[48,512]{1,0:T(8,128)(2,1)S(1)} %get-tuple-element.99), channel_id=1, source_target_pairs={{0,31},{1,24},{2,25},{3,26},{4,27},{5,28},{6,29},{7,30},{8,7},{9,0... | collective-permute-start | bytes 147464 | tf_op jit(solution)/shard_map/ppermute | solution.py:412
  74.0 9.6 %collective-permute-start.15 = (bf16[288,512]{1,0:T(8,128)(2,1)S(1)}, bf16[288,512]{1,0:T(8,128)(2,1)S(1)}, u32[]{:S(2)}, u32[]{:S(2)}) collective-permute-start(bf16[288,512]{1,0:T(8,128)(2,1)S(1)} %get-tuple-element.103), channel_id=1, source_target_pairs={{0,8},{1,9},{2,10},{3,11},{4,12},{5,13},{6,14},{7,15},{8,16},{9,17... | collective-permute-start | bytes 884744 | tf_op jit(solution)/shard_map/ppermute | solution.py:412
  76.4 5.3 %collective-permute-start.16 = (bf16[48,512]{1,0:T(8,128)(2,1)S(1)}, bf16[48,512]{1,0:T(8,128)(2,1)S(1)}, u32[]{:S(2)}, u32[]{:S(2)}) collective-permute-start(bf16[48,512]{1,0:T(8,128)(2,1)S(1)} %get-tuple-element.104), channel_id=1, source_target_pairs={{0,1},{1,2},{2,3},{3,4},{4,5},{5,6},{6,7},{7,0},{8,9},{9,10},{10,1... | collective-permute-start | bytes 147464 | tf_op jit(solution)/shard_map/ppermute | solution.py:412
  76.4 7.2 %collective-permute-start.17 = (bf16[48,512]{1,0:T(8,128)(2,1)S(1)}, bf16[48,512]{1,0:T(8,128)(2,1)S(1)}, u32[]{:S(2)}, u32[]{:S(2)}) collective-permute-start(bf16[48,512]{1,0:T(8,128)(2,1)S(1)} %get-tuple-element.105), channel_id=1, source_target_pairs={{0,9},{1,10},{2,11},{3,12},{4,13},{5,14},{6,15},{7,8},{8,17},{9,18... | collective-permute-start | bytes 147464 | tf_op jit(solution)/shard_map/ppermute | solution.py:412
  85.9 16.7 %collective-permute-start.21 = (bf16[96,512]{1,0:T(8,128)(2,1)S(1)}, bf16[96,512]{1,0:T(8,128)(2,1)S(1)}, u32[]{:S(2)}, u32[]{:S(2)}) collective-permute-start(bf16[96,512]{1,0:T(8,128)(2,1)S(1)} %get-tuple-element.121), channel_id=1, source_target_pairs={{0,4},{1,5},{2,6},{3,7},{4,0},{5,1},{6,2},{7,3},{8,12},{9,13},{10,... | collective-permute-start | bytes 294920 | tf_op jit(solution)/shard_map/ppermute | solution.py:417
  86.0 16.7 %collective-permute-start.22 = (bf16[96,512]{1,0:T(8,128)(2,1)S(1)}, bf16[96,512]{1,0:T(8,128)(2,1)S(1)}, u32[]{:S(2)}, u32[]{:S(2)}) collective-permute-start(bf16[96,512]{1,0:T(8,128)(2,1)S(1)} %get-tuple-element.122), channel_id=1, source_target_pairs={{0,6},{1,7},{2,4},{3,5},{4,2},{5,3},{6,0},{7,1},{8,14},{9,15},{10,... | collective-permute-start | bytes 294920 | tf_op jit(solution)/shard_map/ppermute | solution.py:417
  89.8 12.8 %collective-permute-start.18 = (bf16[192,512]{1,0:T(8,128)(2,1)S(1)}, bf16[192,512]{1,0:T(8,128)(2,1)S(1)}, u32[]{:S(2)}, u32[]{:S(2)}) collective-permute-start(bf16[192,512]{1,0:T(8,128)(2,1)S(1)} %get-tuple-element.118), channel_id=1, source_target_pairs={{0,2},{1,3},{2,0},{3,1},{4,6},{5,7},{6,4},{7,5},{8,10},{9,11},{10,... | collective-permute-start | bytes 589832 | tf_op jit(solution)/shard_map/ppermute | solution.py:417
  94.5 12.0 %collective-permute-start.19 = (bf16[96,512]{1,0:T(8,128)(2,1)S(1)}, bf16[96,512]{1,0:T(8,128)(2,1)S(1)}, u32[]{:S(2)}, u32[]{:S(2)}) collective-permute-start(bf16[96,512]{1,0:T(8,128)(2,1)S(1)} %get-tuple-element.113), channel_id=1, source_target_pairs={{0,4},{1,5},{2,6},{3,7},{4,0},{5,1},{6,2},{7,3},{8,12},{9,13},{10,... | collective-permute-start | bytes 294920 | tf_op jit(solution)/shard_map/ppermute | solution.py:417
  96.0 10.4 %collective-permute-start.20 = (bf16[96,512]{1,0:T(8,128)(2,1)S(1)}, bf16[96,512]{1,0:T(8,128)(2,1)S(1)}, u32[]{:S(2)}, u32[]{:S(2)}) collective-permute-start(bf16[96,512]{1,0:T(8,128)(2,1)S(1)} %get-tuple-element.115), channel_id=1, source_target_pairs={{0,6},{1,7},{2,4},{3,5},{4,2},{5,3},{6,0},{7,1},{8,14},{9,15},{10,... | collective-permute-start | bytes 294920 | tf_op jit(solution)/shard_map/ppermute | solution.py:417
  104.4 9.0 %collective-permute-start.24 = (bf16[96,512]{1,0:T(8,128)(2,1)S(1)}, bf16[96,512]{1,0:T(8,128)(2,1)S(1)}, u32[]{:S(2)}, u32[]{:S(2)}) collective-permute-start(bf16[96,512]{1,0:T(8,128)(2,1)S(1)} %get-tuple-element.127), channel_id=1, source_target_pairs={{0,4},{1,5},{2,6},{3,7},{4,0},{5,1},{6,2},{7,3},{8,12},{9,13},{10,... | collective-permute-start | bytes 294920 | tf_op jit(solution)/shard_map/ppermute | solution.py:417
  105.5 8.7 %collective-permute-start.26 = (bf16[96,512]{1,0:T(8,128)(2,1)S(1)}, bf16[96,512]{1,0:T(8,128)(2,1)S(1)}, u32[]{:S(2)}, u32[]{:S(2)}) collective-permute-start(bf16[96,512]{1,0:T(8,128)(2,1)S(1)} %get-tuple-element.130), channel_id=1, source_target_pairs={{0,6},{1,7},{2,4},{3,5},{4,2},{5,3},{6,0},{7,1},{8,14},{9,15},{10,... | collective-permute-start | bytes 294920 | tf_op jit(solution)/shard_map/ppermute | solution.py:417
  108.2 14.4 %collective-permute-start.23 = (bf16[192,512]{1,0:T(8,128)(2,1)S(1)}, bf16[192,512]{1,0:T(8,128)(2,1)S(1)}, u32[]{:S(2)}, u32[]{:S(2)}) collective-permute-start(bf16[192,512]{1,0:T(8,128)(2,1)S(1)} %get-tuple-element.126), channel_id=1, source_target_pairs={{0,2},{1,3},{2,0},{3,1},{4,6},{5,7},{6,4},{7,5},{8,10},{9,11},{10,... | collective-permute-start | bytes 589832 | tf_op jit(solution)/shard_map/ppermute | solution.py:417
  113.4 9.2 %collective-permute-start.25 = (bf16[96,512]{1,0:T(8,128)(2,1)S(1)}, bf16[96,512]{1,0:T(8,128)(2,1)S(1)}, u32[]{:S(2)}, u32[]{:S(2)}) collective-permute-start(bf16[96,512]{1,0:T(8,128)(2,1)S(1)} %get-tuple-element.129), channel_id=1, source_target_pairs={{0,4},{1,5},{2,6},{3,7},{4,0},{5,1},{6,2},{7,3},{8,12},{9,13},{10,... | collective-permute-start | bytes 294920 | tf_op jit(solution)/shard_map/ppermute | solution.py:417
  114.2 8.4 %collective-permute-start.27 = (bf16[96,512]{1,0:T(8,128)(2,1)S(1)}, bf16[96,512]{1,0:T(8,128)(2,1)S(1)}, u32[]{:S(2)}, u32[]{:S(2)}) collective-permute-start(bf16[96,512]{1,0:T(8,128)(2,1)S(1)} %get-tuple-element.132), channel_id=1, source_target_pairs={{0,6},{1,7},{2,4},{3,5},{4,2},{5,3},{6,0},{7,1},{8,14},{9,15},{10,... | collective-permute-start | bytes 294920 | tf_op jit(solution)/shard_map/ppermute | solution.py:417

commit v4 on v3

--- a/solution.py
+++ b/solution.py
@@ -84,10 +84,11 @@
     chosen = lax.broadcasted_iota(jnp.int32, logits.shape, 1) == experts.astype(jnp.int32)
     picked = jnp.sum(jnp.where(chosen, logits, 0.0), axis=1, keepdims=True)
     target = target_row.astype(jnp.int32)
+    placed = dot(one_hot_rows(target, sum(ref.shape[0] for ref in piece_refs)), ynorm)
     start = 0
     for piece_ref in piece_refs:
         slots = piece_ref.shape[0]
-        piece_ref[...] = dot(one_hot_rows(target - start, slots), ynorm).astype(BF16)
+        piece_ref[...] = placed[start : start + slots].astype(BF16)
         start += slots
     return jax.nn.sigmoid(picked)
 
@@ -137,8 +138,8 @@
                 )
             peak = jnp.max(scores, axis=0, keepdims=True)
             weights = jnp.exp2((scores - peak) * scale)
-            shares = (weights * (1.0 / jnp.sum(weights, axis=0, keepdims=True))).astype(BF16)
-            mixed_t = dot(v, shares, ((0,), (0,)))
+            inverse = 1.0 / jnp.sum(weights, axis=0, keepdims=True)
+            mixed_t = dot(v, weights.astype(BF16), ((0,), (0,))) * inverse
             picked = jnp.concatenate(
                 [mixed_t[h * width : (h + 1) * width, h * main : (h + 1) * main] for h in range(group)], axis=0
             )

time: 125 us -> 124 us (level)
  Pallas kernels: 54.3 us -> 52.8 us
    pallas_call x6, Pallas kernels: 30.5 us -> 29 us  [call(): pl.pallas_call(body, in_specs=specs, out_specs=[IN_VMEM] * len(outs), out...]
  transfers between devices with their start and end apart: 28 -> 28, of which waited for: 12 -> 11; matrix products, arithmetic and copies ran while one was open for 0% -> 0% of each run, Pallas kernels for 33% -> 33%
where the time goes in v4:
time: 124 us
  Pallas kernels  52.8 us (43%)
  starting transfers between devices  41.6 us (34%)
  waiting for transfers between devices  28.2 us (23%)
    ppermute x22, starting transfers between devices, between(): lax.ppermute(value, 'lon', [(s, s ^ distance) for s in range(sectors)])  33.3 us
    pallas_call x6, Pallas kernels, call(): pl.pallas_call(body, in_specs=specs, out_specs=[IN_VMEM] * len(outs), out...  29 us
    ppermute x22, waiting for transfers between devices, between(): lax.ppermute(value, 'lon', [(s, s ^ distance) for s in range(sectors)])  18.2 us
    pallas_call x4, Pallas kernels, run_near(): pl.pallas_call(functools.partial(near_kernel, plan=plan, base=base, layer...  16.6 us
    ppermute x6, waiting for transfers between devices, shift(): lax.ppermute(value, ('lat', 'lon'), lat_lon_pairs(lat_step, lon_step))  10 us
    ppermute x6, starting transfers between devices, shift(): lax.ppermute(value, ('lat', 'lon'), lat_lon_pairs(lat_step, lon_step))  8.33 us
    pallas_call x4, Pallas kernels, run_away(): pl.pallas_call(functools.partial(away_kernel, whole=len(whole), cut=len(c...  7.23 us
  transfers between devices with their start and end apart: 28, of which 11 were waited for; matrix products, arithmetic and copies ran while one was open for 0% of the time, Pallas kernels for 33%

profile of v4, /device:TPU:0, one launch (start us, length us, event | category | flops | bytes accessed | tf_op | source)
XLA Modules:
  0.0 123.6 jit_solution(10765268816101499797)
XLA Ops:
  0.0 0.5 collective-permute-start
  0.5 0.1 collective-permute-start.1
  0.5 0.6 add_bitcast_fusion.refs_0_
  1.1 12.4 %shard_map.109 = (bf16[576,512]{1,0:T(8,128)(2,1)S(1)}, f32[576,2]{1,0:T(8,128)S(1)}, bf16[96,512]{1,0:T(8,128)(2,1)S(1)}, bf16[96,512]{1,0:T(8,128)(2,1)S(1)}, ...) custom-call(s32[1,3]{1,0:T(1,128)} %add_bitcast_fusion.refs_0_, ...), custom_call_target="tpu_custom_call" | custom-call | flops 4000000000 | bytes 4832140 | tf_op jit(solution)/shard_map/pallas_call | solution.py:359
  13.5 4.1 %collective-permute-start.5 = (bf16[96,512]{1,0:T(8,128)(2,1)S(1)}, bf16[96,512]{1,0:T(8,128)(2,1)S(1)}, u32[]{:S(2)}, u32[]{:S(2)}) collective-permute-start(bf16[96,512]{1,0:T(8,128)(2,1)S(1)} %get-tuple-element.84), channel_id=1, source_target_pairs={{0,4},{1,5},{2,6},{3,7},{4,0},{5,1},{6,2},{7,3},{8,12},{9,13},{10,... | collective-permute-start | bytes 294920 | tf_op jit(solution)/shard_map/ppermute | solution.py:418
  17.6 1.4 %collective-permute-start.6 = (bf16[96,512]{1,0:T(8,128)(2,1)S(1)}, bf16[96,512]{1,0:T(8,128)(2,1)S(1)}, u32[]{:S(2)}, u32[]{:S(2)}) collective-permute-start(bf16[96,512]{1,0:T(8,128)(2,1)S(1)} %get-tuple-element.85), channel_id=1, source_target_pairs={{0,6},{1,7},{2,4},{3,5},{4,2},{5,3},{6,0},{7,1},{8,14},{9,15},{10,... | collective-permute-start | bytes 294920 | tf_op jit(solution)/shard_map/ppermute | solution.py:418
  19.0 0.2 collective-permute-start.2
  19.2 4.1 %shard_map.111 = (bf16[96,512]{1,0:T(8,128)(2,1)S(1)}, bf16[4,512,1024]{2,1,0:T(8,128)(2,1)S(1)}, bf16[4,1024,512]{2,1,0:T(8,128)(2,1)S(1)}) custom-call(bf16[96,512]{1,0:T(8,128)(2,1)S(1)} %get-tuple-element.72.refs_0_, bf16[2,4,512,1024]{3,2,1,0:T(8,128)(2,1)} %refs_1_.7, bf16[2,4,1024,512]{3,2,1,0:T(8,128)(2,1)} %refs_2_.3), custom_call_target="tpu_custom_call" | custom-call | flops 3000000000 | bytes 8388608 | tf_op jit(solution)/shard_map/pallas_call | solution.py:373
  23.3 2.1 %collective-permute-done.5.refs_1_ = bf16[96,512]{1,0:T(8,128)(2,1)S(1)} collective-permute-done((bf16[96,512]{1,0:T(8,128)(2,1)S(1)}, bf16[96,512]{1,0:T(8,128)(2,1)S(1)}, u32[]{:S(2)}, u32[]{:S(2)}) %collective-permute-start.5) | collective-permute-done | bytes 98336 | tf_op jit(solution)/shard_map/ppermute | solution.py:418
  25.5 0.8 collective-permute-start.3
  26.2 0.0 collective-permute-done.6.refs_2_
  26.2 2.2 %collective-permute-start.4 = (bf16[96,512]{1,0:T(8,128)(2,1)S(1)}, bf16[96,512]{1,0:T(8,128)(2,1)S(1)}, u32[]{:S(2)}, u32[]{:S(2)}) collective-permute-start(bf16[96,512]{1,0:T(8,128)(2,1)S(1)} %get-tuple-element.78), channel_id=1, source_target_pairs={{0,6},{1,7},{2,4},{3,5},{4,2},{5,3},{6,0},{7,1},{8,14},{9,15},{10,... | collective-permute-start | bytes 294920 | tf_op jit(solution)/shard_map/ppermute | solution.py:418
  28.5 0.9 collective-permute-done.2.refs_0_
  29.3 1.9 %shard_map.113 = (bf16[96,512]{1,0:T(8,128)(2,1)S(1)}, bf16[96,512]{1,0:T(8,128)(2,1)S(1)}, bf16[96,512]{1,0:T(8,128)(2,1)S(1)}) custom-call(bf16[192,512]{1,0:T(8,128)(2,1)S(1)} %collective-permute-done.2.refs_0_, bf16[96,512]{1,0:T(8,128)(2,1)S(1)} %collective-permute-done.5.refs_1_, bf16[96,512]{1,0:T(8,128)(2,1)S(1)} %collective-permute-done.6.refs_2_, ...), custom_call_target="tpu_custom_call" | custom-call | flops 3000000000 | bytes 1048576 | tf_op jit(solution)/shard_map/pallas_call | solution.py:392
  31.3 1.2 collective-permute-start.8
  32.5 0.0 collective-permute-done.refs_1_
  32.5 2.6 %collective-permute-start.10 = (bf16[96,512]{1,0:T(8,128)(2,1)S(1)}, bf16[96,512]{1,0:T(8,128)(2,1)S(1)}, u32[]{:S(2)}, u32[]{:S(2)}) collective-permute-start(bf16[96,512]{1,0:T(8,128)(2,1)S(1)} %get-tuple-element.93), channel_id=1, source_target_pairs={{0,6},{1,7},{2,4},{3,5},{4,2},{5,3},{6,0},{7,1},{8,14},{9,15},{10,... | collective-permute-start | bytes 294920 | tf_op jit(solution)/shard_map/ppermute | solution.py:418
  35.2 0.0 collective-permute-done.1.refs_2_
  35.2 4.1 %shard_map.112 = (bf16[96,512]{1,0:T(8,128)(2,1)S(1)}, bf16[4,512,1024]{2,1,0:T(8,128)(2,1)S(1)}, bf16[4,1024,512]{2,1,0:T(8,128)(2,1)S(1)}) custom-call(bf16[96,512]{1,0:T(8,128)(2,1)S(1)} %get-tuple-element.79.refs_0_, bf16[2,4,512,1024]{3,2,1,0:T(8,128)(2,1)} %collective-permute-done.refs_1_, bf16[2,4,1024,512]{3,2,1,0:T(8,128)(2,1)} %collective-permute-done.1.refs_2_), custom_call_target="tpu_custom_call" | custom-call | flops 3000000000 | bytes 8388608 | tf_op jit(solution)/shard_map/pallas_call | solution.py:373
  39.3 0.0 collective-permute-done.3.refs_1_
  39.3 0.0 collective-permute-done.4.refs_2_
  39.3 1.7 %shard_map.114 = (bf16[192,512]{1,0:T(8,128)(2,1)S(1)}, bf16[96,512]{1,0:T(8,128)(2,1)S(1)}, bf16[96,512]{1,0:T(8,128)(2,1)S(1)}) custom-call(bf16[192,512]{1,0:T(8,128)(2,1)S(1)} %collective-permute-done.2.refs_0_, bf16[96,512]{1,0:T(8,128)(2,1)S(1)} %collective-permute-done.3.refs_1_, bf16[96,512]{1,0:T(8,128)(2,1)S(1)} %collective-permute-done.4.refs_2_, ...), custom_call_target="tpu_custom_call" | custom-call | flops 3000000000 | bytes 1048576 | tf_op jit(solution)/shard_map/pallas_call | solution.py:392
  41.1 3.1 %collective-permute-start.7 = (bf16[192,512]{1,0:T(8,128)(2,1)S(1)}, bf16[192,512]{1,0:T(8,128)(2,1)S(1)}, u32[]{:S(2)}, u32[]{:S(2)}) collective-permute-start(bf16[192,512]{1,0:T(8,128)(2,1)S(1)} %get-tuple-element.89), channel_id=1, source_target_pairs={{0,2},{1,3},{2,0},{3,1},{4,6},{5,7},{6,4},{7,5},{8,10},{9,11},{10,... | collective-permute-start | bytes 589832 | tf_op jit(solution)/shard_map/ppermute | solution.py:418
  44.1 0.0 collective-permute-done.8.refs_6_
  44.2 0.0 collective-permute-done.10.refs_8_
  44.2 1.5 %collective-permute-start.11 = (bf16[96,512]{1,0:T(8,128)(2,1)S(1)}, bf16[96,512]{1,0:T(8,128)(2,1)S(1)}, u32[]{:S(2)}, u32[]{:S(2)}) collective-permute-start(bf16[96,512]{1,0:T(8,128)(2,1)S(1)} %get-tuple-element.95), channel_id=1, source_target_pairs={{0,6},{1,7},{2,4},{3,5},{4,2},{5,3},{6,0},{7,1},{8,14},{9,15},{10,... | collective-permute-start | bytes 294920 | tf_op jit(solution)/shard_map/ppermute | solution.py:418
  45.7 1.4 %collective-permute-start.9 = (bf16[96,512]{1,0:T(8,128)(2,1)S(1)}, bf16[96,512]{1,0:T(8,128)(2,1)S(1)}, u32[]{:S(2)}, u32[]{:S(2)}) collective-permute-start(bf16[96,512]{1,0:T(8,128)(2,1)S(1)} %get-tuple-element.92), channel_id=1, source_target_pairs={{0,4},{1,5},{2,6},{3,7},{4,0},{5,1},{6,2},{7,3},{8,12},{9,13},{10,... | collective-permute-start | bytes 294920 | tf_op jit(solution)/shard_map/ppermute | solution.py:418
  47.1 4.2 %shard_map.110 = (f32[672,2]{1,0:T(8,128)S(1)}, f32[1,672]{1,0:T(1,128)S(1)}, bf16[512,1536]{1,0:T(8,128)(2,1)S(1)}, bf16[512,512]{1,0:T(8,128)(2,1)S(1)}) custom-call(s32[1,3]{1,0:T(1,128)} %add_bitcast_fusion.refs_0_, s32[2,1,576]{2,1,0:T(1,128)} %bitcast.13, s32[1,672]{1,0:T(1,128)} %constant.46.refs_2_, bf16[2,512,1536]{2,1,0:T(8,128)(2,1)} %refs_3_.1, ...), custom_call_target="tpu_custom_call" | custom-call | flops 2000000000 | bytes 4206220 | tf_op jit(solution)/shard_map/pallas_call | solution.py:359
  51.2 2.3 %collective-permute-done.11.refs_9_ = bf16[96,512]{1,0:T(8,128)(2,1)S(1)} collective-permute-done((bf16[96,512]{1,0:T(8,128)(2,1)S(1)}, bf16[96,512]{1,0:T(8,128)(2,1)S(1)}, u32[]{:S(2)}, u32[]{:S(2)}) %collective-permute-start.11) | collective-permute-done | bytes 98336 | tf_op jit(solution)/shard_map/ppermute | solution.py:418
  53.5 2.3 %collective-permute-done.9.refs_7_ = bf16[96,512]{1,0:T(8,128)(2,1)S(1)} collective-permute-done((bf16[96,512]{1,0:T(8,128)(2,1)S(1)}, bf16[96,512]{1,0:T(8,128)(2,1)S(1)}, u32[]{:S(2)}, u32[]{:S(2)}) %collective-permute-start.9) | collective-permute-done | bytes 98336 | tf_op jit(solution)/shard_map/ppermute | solution.py:418
  55.8 0.0 collective-permute-done.7.refs_5_
  55.8 0.7 shard_map.115
  56.5 2.5 %collective-permute-start.12 = (bf16[288,512]{1,0:T(8,128)(2,1)S(1)}, bf16[288,512]{1,0:T(8,128)(2,1)S(1)}, u32[]{:S(2)}, u32[]{:S(2)}) collective-permute-start(bf16[288,512]{1,0:T(8,128)(2,1)S(1)} %get-tuple-element.97), channel_id=1, source_target_pairs={{0,24},{1,25},{2,26},{3,27},{4,28},{5,29},{6,30},{7,31},{8,0},{9,1... | collective-permute-start | bytes 884744 | tf_op jit(solution)/shard_map/ppermute | solution.py:413
  59.0 1.3 %collective-permute-start.13 = (bf16[48,512]{1,0:T(8,128)(2,1)S(1)}, bf16[48,512]{1,0:T(8,128)(2,1)S(1)}, u32[]{:S(2)}, u32[]{:S(2)}) collective-permute-start(bf16[48,512]{1,0:T(8,128)(2,1)S(1)} %get-tuple-element.98), channel_id=1, source_target_pairs={{0,7},{1,0},{2,1},{3,2},{4,3},{5,4},{6,5},{7,6},{8,15},{9,8},{10,9... | collective-permute-start | bytes 147464 | tf_op jit(solution)/shard_map/ppermute | solution.py:413
  60.3 1.2 collective-permute-start.14
  61.5 0.6 collective-permute-done.13.refs_4_
  62.1 2.9 %collective-permute-done.14.refs_5_ = bf16[48,512]{1,0:T(8,128)(2,1)S(1)} collective-permute-done((bf16[48,512]{1,0:T(8,128)(2,1)S(1)}, bf16[48,512]{1,0:T(8,128)(2,1)S(1)}, u32[]{:S(2)}, u32[]{:S(2)}) %collective-permute-start.14) | collective-permute-done | bytes 49184 | tf_op jit(solution)/shard_map/ppermute | solution.py:413
  65.0 0.2 collective-permute-done.12.refs_3_
  65.2 7.5 %shard_map.116 = (bf16[288,512]{1,0:T(8,128)(2,1)S(1)}, bf16[288,512]{1,0:T(8,128)(2,1)S(1)}, bf16[48,512]{1,0:T(8,128)(2,1)S(1)}, bf16[48,512]{1,0:T(8,128)(2,1)S(1)}) custom-call(s32[1,3]{1,0:T(1,128)} %add_bitcast_fusion.refs_0_, f32[2,16]{1,0:T(2,128)} %refs_1_.6, bf16[288,512]{1,0:T(8,128)(2,1)S(1)} %get-tuple-element.96.refs_2_, ...), custom_call_target="tpu_custom_call" | custom-call | flops 3000000000 | bytes 2793612 | tf_op jit(solution)/shard_map/pallas_call | solution.py:359
  72.7 2.5 %collective-permute-start.15 = (bf16[288,512]{1,0:T(8,128)(2,1)S(1)}, bf16[288,512]{1,0:T(8,128)(2,1)S(1)}, u32[]{:S(2)}, u32[]{:S(2)}) collective-permute-start(bf16[288,512]{1,0:T(8,128)(2,1)S(1)} %get-tuple-element.103), channel_id=1, source_target_pairs={{0,8},{1,9},{2,10},{3,11},{4,12},{5,13},{6,14},{7,15},{8,16},{9,17... | collective-permute-start | bytes 884744 | tf_op jit(solution)/shard_map/ppermute | solution.py:413
  75.1 0.0 collective-permute-start.16
  75.1 0.9 collective-permute-start.17
  76.0 4.5 %collective-permute-done.16.refs_2_ = bf16[48,512]{1,0:T(8,128)(2,1)S(1)} collective-permute-done((bf16[48,512]{1,0:T(8,128)(2,1)S(1)}, bf16[48,512]{1,0:T(8,128)(2,1)S(1)}, u32[]{:S(2)}, u32[]{:S(2)}) %collective-permute-start.16) | collective-permute-done | bytes 49184 | tf_op jit(solution)/shard_map/ppermute | solution.py:413
  80.5 1.9 %collective-permute-done.17.refs_3_ = bf16[48,512]{1,0:T(8,128)(2,1)S(1)} collective-permute-done((bf16[48,512]{1,0:T(8,128)(2,1)S(1)}, bf16[48,512]{1,0:T(8,128)(2,1)S(1)}, u32[]{:S(2)}, u32[]{:S(2)}) %collective-permute-start.17) | collective-permute-done | bytes 49184 | tf_op jit(solution)/shard_map/ppermute | solution.py:413
  82.4 2.1 %shard_map.117 = (bf16[672,512]{1,0:T(8,128)(2,1)S(1)}, f32[672,2]{1,0:T(8,128)S(1)}, bf16[96,512]{1,0:T(8,128)(2,1)S(1)}, bf16[96,512]{1,0:T(8,128)(2,1)S(1)}, ...) custom-call(bf16[288,512]{1,0:T(8,128)(2,1)S(1)} %get-tuple-element., ...), custom_call_target="tpu_custom_call" | custom-call | flops 1000000000 | bytes 737152 | tf_op jit(solution)/shard_map/pallas_call | solution.py:359
  84.5 0.1 collective-permute-start.21
  84.6 3.8 %collective-permute-start.22 = (bf16[96,512]{1,0:T(8,128)(2,1)S(1)}, bf16[96,512]{1,0:T(8,128)(2,1)S(1)}, u32[]{:S(2)}, u32[]{:S(2)}) collective-permute-start(bf16[96,512]{1,0:T(8,128)(2,1)S(1)} %get-tuple-element.122), channel_id=1, source_target_pairs={{0,6},{1,7},{2,4},{3,5},{4,2},{5,3},{6,0},{7,1},{8,14},{9,15},{10,... | collective-permute-start | bytes 294920 | tf_op jit(solution)/shard_map/ppermute | solution.py:418
  88.4 0.5 collective-permute-start.18
  88.9 4.1 %shard_map.118 = (bf16[96,512]{1,0:T(8,128)(2,1)S(1)}, bf16[4,512,1024]{2,1,0:T(8,128)(2,1)S(1)}, bf16[4,1024,512]{2,1,0:T(8,128)(2,1)S(1)}) custom-call(bf16[96,512]{1,0:T(8,128)(2,1)S(1)} %get-tuple-element.109.refs_0_, bf16[2,4,512,1024]{3,2,1,0:T(8,128)(2,1)} %refs_1_.7, bf16[2,4,1024,512]{3,2,1,0:T(8,128)(2,1)} %refs_2_.3), custom_call_target="tpu_custom_call" | custom-call | flops 3000000000 | bytes 8388608 | tf_op jit(solution)/shard_map/pallas_call | solution.py:373
  93.0 1.5 %collective-permute-start.19 = (bf16[96,512]{1,0:T(8,128)(2,1)S(1)}, bf16[96,512]{1,0:T(8,128)(2,1)S(1)}, u32[]{:S(2)}, u32[]{:S(2)}) collective-permute-start(bf16[96,512]{1,0:T(8,128)(2,1)S(1)} %get-tuple-element.113), channel_id=1, source_target_pairs={{0,4},{1,5},{2,6},{3,7},{4,0},{5,1},{6,2},{7,3},{8,12},{9,13},{10,... | collective-permute-start | bytes 294920 | tf_op jit(solution)/shard_map/ppermute | solution.py:418
  94.6 2.4 %collective-permute-start.20 = (bf16[96,512]{1,0:T(8,128)(2,1)S(1)}, bf16[96,512]{1,0:T(8,128)(2,1)S(1)}, u32[]{:S(2)}, u32[]{:S(2)}) collective-permute-start(bf16[96,512]{1,0:T(8,128)(2,1)S(1)} %get-tuple-element.115), channel_id=1, source_target_pairs={{0,6},{1,7},{2,4},{3,5},{4,2},{5,3},{6,0},{7,1},{8,14},{9,15},{10,... | collective-permute-start | bytes 294920 | tf_op jit(solution)/shard_map/ppermute | solution.py:418
  97.0 4.1 %shard_map.119 = (bf16[96,512]{1,0:T(8,128)(2,1)S(1)}, bf16[4,512,1024]{2,1,0:T(8,128)(2,1)S(1)}, bf16[4,1024,512]{2,1,0:T(8,128)(2,1)S(1)}) custom-call(bf16[96,512]{1,0:T(8,128)(2,1)S(1)} %get-tuple-element.116.refs_0_, bf16[2,4,512,1024]{3,2,1,0:T(8,128)(2,1)} %collective-permute-done.refs_1_, bf16[2,4,1024,512]{3,2,1,0:T(8,128)(2,1)} %collective-permute-done.1.refs_2_), custom_call_target="tpu_custom_call" | custom-call | flops 3000000000 | bytes 8388608 | tf_op jit(solution)/shard_map/pallas_call | solution.py:373
  101.2 0.0 collective-permute-done.21.refs_1_
  101.2 1.8 %shard_map.120 = (bf16[96,512]{1,0:T(8,128)(2,1)S(1)}, bf16[96,512]{1,0:T(8,128)(2,1)S(1)}, bf16[96,512]{1,0:T(8,128)(2,1)S(1)}) custom-call(bf16[192,512]{1,0:T(8,128)(2,1)S(1)} %collective-permute-done.18.refs_0_, bf16[96,512]{1,0:T(8,128)(2,1)S(1)} %collective-permute-done.21.refs_1_, bf16[96,512]{1,0:T(8,128)(2,1)S(1)} %collective-permute-done.22.refs_2_, ...), custom_call_target="tpu_custom_call" | custom-call | flops 3000000000 | bytes 1048576 | tf_op jit(solution)/shard_map/pallas_call | solution.py:392
  103.0 1.1 collective-permute-start.24
  104.1 0.9 collective-permute-start.26
  105.0 1.8 %shard_map.121 = (bf16[192,512]{1,0:T(8,128)(2,1)S(1)}, bf16[96,512]{1,0:T(8,128)(2,1)S(1)}, bf16[96,512]{1,0:T(8,128)(2,1)S(1)}) custom-call(bf16[192,512]{1,0:T(8,128)(2,1)S(1)} %collective-permute-done.18.refs_0_, bf16[96,512]{1,0:T(8,128)(2,1)S(1)} %collective-permute-done.19.refs_1_, bf16[96,512]{1,0:T(8,128)(2,1)S(1)} %collective-permute-done.20.refs_2_, ...), custom_call_target="tpu_custom_call" | custom-call | flops 3000000000 | bytes 1048576 | tf_op jit(solution)/shard_map/pallas_call | solution.py:392
  106.8 1.7 %collective-permute-start.23 = (bf16[192,512]{1,0:T(8,128)(2,1)S(1)}, bf16[192,512]{1,0:T(8,128)(2,1)S(1)}, u32[]{:S(2)}, u32[]{:S(2)}) collective-permute-start(bf16[192,512]{1,0:T(8,128)(2,1)S(1)} %get-tuple-element.126), channel_id=1, source_target_pairs={{0,2},{1,3},{2,0},{3,1},{4,6},{5,7},{6,4},{7,5},{8,10},{9,11},{10,... | collective-permute-start | bytes 589832 | tf_op jit(solution)/shard_map/ppermute | solution.py:418
  108.5 3.5 %collective-permute-done.24.refs_6_ = bf16[96,512]{1,0:T(8,128)(2,1)S(1)} collective-permute-done((bf16[96,512]{1,0:T(8,128)(2,1)S(1)}, bf16[96,512]{1,0:T(8,128)(2,1)S(1)}, u32[]{:S(2)}, u32[]{:S(2)}) %collective-permute-start.24) | collective-permute-done | bytes 98336 | tf_op jit(solution)/shard_map/ppermute | solution.py:418
  112.0 0.8 collective-permute-start.25
  112.8 1.4 %collective-permute-start.27 = (bf16[96,512]{1,0:T(8,128)(2,1)S(1)}, bf16[96,512]{1,0:T(8,128)(2,1)S(1)}, u32[]{:S(2)}, u32[]{:S(2)}) collective-permute-start(bf16[96,512]{1,0:T(8,128)(2,1)S(1)} %get-tuple-element.132), channel_id=1, source_target_pairs={{0,6},{1,7},{2,4},{3,5},{4,2},{5,3},{6,0},{7,1},{8,14},{9,15},{10,... | collective-permute-start | bytes 294920 | tf_op jit(solution)/shard_map/ppermute | solution.py:418
  114.2 7.0 %collective-permute-done.25.refs_7_ = bf16[96,512]{1,0:T(8,128)(2,1)S(1)} collective-permute-done((bf16[96,512]{1,0:T(8,128)(2,1)S(1)}, bf16[96,512]{1,0:T(8,128)(2,1)S(1)}, u32[]{:S(2)}, u32[]{:S(2)}) %collective-permute-start.25) | collective-permute-done | bytes 98336 | tf_op jit(solution)/shard_map/ppermute | solution.py:418
  121.2 0.0 collective-permute-done.27.refs_9_
  121.2 2.2 %shard_map.122 = bf16[576,512]{1,0:T(8,128)(2,1)} custom-call(bf16[672,512]{1,0:T(8,128)(2,1)S(1)} %get-tuple-element.107.refs_0_, f32[672,2]{1,0:T(8,128)S(1)} %get-tuple-element.108.refs_1_, s32[1,672]{1,0:T(1,128)} %constant.46.refs_2_, bf16[96,512]{1,0:T(8,128)(2,1)S(1)} %get-tuple-element.110.refs_3_, bf16[96,512]{1,0:T(8,128)(2,1)S(1)} %get-tuple-element.117.refs_4_, ...), custom_call_target="tpu_custom_call" | custom-call | flops 1000000000 | bytes 1482624 | tf_op jit(solution)/shard_map/pallas_call | solution.py:359
  (7 shorter events, 0.0 us)
Async XLA Ops:
  0.0 32.5 %collective-permute-start = (bf16[2,4,512,1024]{3,2,1,0:T(8,128)(2,1)}, bf16[2,4,512,1024]{3,2,1,0:T(8,128)(2,1)}, u32[]{:S(2)}, u32[]{:S(2)}) collective-permute-start(bf16[2,4,512,1024]{3,2,1,0:T(8,128)(2,1)} %refs_1_.7), channel_id=1, source_target_pairs={{0,1},{1,0},{2,3},{3,2},{4,5},{5,4},{6,7},{7,6},{8,9},{9,8},{10,11... | collective-permute-start | bytes 25165832 | tf_op jit(solution)/shard_map/ppermute | solution.py:418
  0.5 34.7 %collective-permute-start.1 = (bf16[2,4,1024,512]{3,2,1,0:T(8,128)(2,1)}, bf16[2,4,1024,512]{3,2,1,0:T(8,128)(2,1)}, u32[]{:S(2)}, u32[]{:S(2)}) collective-permute-start(bf16[2,4,1024,512]{3,2,1,0:T(8,128)(2,1)} %refs_2_.3), channel_id=1, source_target_pairs={{0,1},{1,0},{2,3},{3,2},{4,5},{5,4},{6,7},{7,6},{8,9},{9,8},{10,11... | collective-permute-start | bytes 25165832 | tf_op jit(solution)/shard_map/ppermute | solution.py:418
  13.5 12.0 %collective-permute-start.5 = (bf16[96,512]{1,0:T(8,128)(2,1)S(1)}, bf16[96,512]{1,0:T(8,128)(2,1)S(1)}, u32[]{:S(2)}, u32[]{:S(2)}) collective-permute-start(bf16[96,512]{1,0:T(8,128)(2,1)S(1)} %get-tuple-element.84), channel_id=1, source_target_pairs={{0,4},{1,5},{2,6},{3,7},{4,0},{5,1},{6,2},{7,3},{8,12},{9,13},{10,... | collective-permute-start | bytes 294920 | tf_op jit(solution)/shard_map/ppermute | solution.py:418
  17.6 8.6 %collective-permute-start.6 = (bf16[96,512]{1,0:T(8,128)(2,1)S(1)}, bf16[96,512]{1,0:T(8,128)(2,1)S(1)}, u32[]{:S(2)}, u32[]{:S(2)}) collective-permute-start(bf16[96,512]{1,0:T(8,128)(2,1)S(1)} %get-tuple-element.85), channel_id=1, source_target_pairs={{0,6},{1,7},{2,4},{3,5},{4,2},{5,3},{6,0},{7,1},{8,14},{9,15},{10,... | collective-permute-start | bytes 294920 | tf_op jit(solution)/shard_map/ppermute | solution.py:418
  19.0 10.4 %collective-permute-start.2 = (bf16[192,512]{1,0:T(8,128)(2,1)S(1)}, bf16[192,512]{1,0:T(8,128)(2,1)S(1)}, u32[]{:S(2)}, u32[]{:S(2)}) collective-permute-start(bf16[192,512]{1,0:T(8,128)(2,1)S(1)} %get-tuple-element.81), channel_id=1, source_target_pairs={{0,2},{1,3},{2,0},{3,1},{4,6},{5,7},{6,4},{7,5},{8,10},{9,11},{10,... | collective-permute-start | bytes 589832 | tf_op jit(solution)/shard_map/ppermute | solution.py:418
  25.5 13.9 %collective-permute-start.3 = (bf16[96,512]{1,0:T(8,128)(2,1)S(1)}, bf16[96,512]{1,0:T(8,128)(2,1)S(1)}, u32[]{:S(2)}, u32[]{:S(2)}) collective-permute-start(bf16[96,512]{1,0:T(8,128)(2,1)S(1)} %get-tuple-element.76), channel_id=1, source_target_pairs={{0,4},{1,5},{2,6},{3,7},{4,0},{5,1},{6,2},{7,3},{8,12},{9,13},{10,... | collective-permute-start | bytes 294920 | tf_op jit(solution)/shard_map/ppermute | solution.py:418
  26.2 13.1 %collective-permute-start.4 = (bf16[96,512]{1,0:T(8,128)(2,1)S(1)}, bf16[96,512]{1,0:T(8,128)(2,1)S(1)}, u32[]{:S(2)}, u32[]{:S(2)}) collective-permute-start(bf16[96,512]{1,0:T(8,128)(2,1)S(1)} %get-tuple-element.78), channel_id=1, source_target_pairs={{0,6},{1,7},{2,4},{3,5},{4,2},{5,3},{6,0},{7,1},{8,14},{9,15},{10,... | collective-permute-start | bytes 294920 | tf_op jit(solution)/shard_map/ppermute | solution.py:418
  31.3 12.9 %collective-permute-start.8 = (bf16[96,512]{1,0:T(8,128)(2,1)S(1)}, bf16[96,512]{1,0:T(8,128)(2,1)S(1)}, u32[]{:S(2)}, u32[]{:S(2)}) collective-permute-start(bf16[96,512]{1,0:T(8,128)(2,1)S(1)} %get-tuple-element.90), channel_id=1, source_target_pairs={{0,4},{1,5},{2,6},{3,7},{4,0},{5,1},{6,2},{7,3},{8,12},{9,13},{10,... | collective-permute-start | bytes 294920 | tf_op jit(solution)/shard_map/ppermute | solution.py:418
  32.5 11.6 %collective-permute-start.10 = (bf16[96,512]{1,0:T(8,128)(2,1)S(1)}, bf16[96,512]{1,0:T(8,128)(2,1)S(1)}, u32[]{:S(2)}, u32[]{:S(2)}) collective-permute-start(bf16[96,512]{1,0:T(8,128)(2,1)S(1)} %get-tuple-element.93), channel_id=1, source_target_pairs={{0,6},{1,7},{2,4},{3,5},{4,2},{5,3},{6,0},{7,1},{8,14},{9,15},{10,... | collective-permute-start | bytes 294920 | tf_op jit(solution)/shard_map/ppermute | solution.py:418
  41.1 14.7 %collective-permute-start.7 = (bf16[192,512]{1,0:T(8,128)(2,1)S(1)}, bf16[192,512]{1,0:T(8,128)(2,1)S(1)}, u32[]{:S(2)}, u32[]{:S(2)}) collective-permute-start(bf16[192,512]{1,0:T(8,128)(2,1)S(1)} %get-tuple-element.89), channel_id=1, source_target_pairs={{0,2},{1,3},{2,0},{3,1},{4,6},{5,7},{6,4},{7,5},{8,10},{9,11},{10,... | collective-permute-start | bytes 589832 | tf_op jit(solution)/shard_map/ppermute | solution.py:418
  44.2 9.4 %collective-permute-start.11 = (bf16[96,512]{1,0:T(8,128)(2,1)S(1)}, bf16[96,512]{1,0:T(8,128)(2,1)S(1)}, u32[]{:S(2)}, u32[]{:S(2)}) collective-permute-start(bf16[96,512]{1,0:T(8,128)(2,1)S(1)} %get-tuple-element.95), channel_id=1, source_target_pairs={{0,6},{1,7},{2,4},{3,5},{4,2},{5,3},{6,0},{7,1},{8,14},{9,15},{10,... | collective-permute-start | bytes 294920 | tf_op jit(solution)/shard_map/ppermute | solution.py:418
  45.7 10.1 %collective-permute-start.9 = (bf16[96,512]{1,0:T(8,128)(2,1)S(1)}, bf16[96,512]{1,0:T(8,128)(2,1)S(1)}, u32[]{:S(2)}, u32[]{:S(2)}) collective-permute-start(bf16[96,512]{1,0:T(8,128)(2,1)S(1)} %get-tuple-element.92), channel_id=1, source_target_pairs={{0,4},{1,5},{2,6},{3,7},{4,0},{5,1},{6,2},{7,3},{8,12},{9,13},{10,... | collective-permute-start | bytes 294920 | tf_op jit(solution)/shard_map/ppermute | solution.py:418
  56.5 8.6 %collective-permute-start.12 = (bf16[288,512]{1,0:T(8,128)(2,1)S(1)}, bf16[288,512]{1,0:T(8,128)(2,1)S(1)}, u32[]{:S(2)}, u32[]{:S(2)}) collective-permute-start(bf16[288,512]{1,0:T(8,128)(2,1)S(1)} %get-tuple-element.97), channel_id=1, source_target_pairs={{0,24},{1,25},{2,26},{3,27},{4,28},{5,29},{6,30},{7,31},{8,0},{9,1... | collective-permute-start | bytes 884744 | tf_op jit(solution)/shard_map/ppermute | solution.py:413
  59.0 3.1 %collective-permute-start.13 = (bf16[48,512]{1,0:T(8,128)(2,1)S(1)}, bf16[48,512]{1,0:T(8,128)(2,1)S(1)}, u32[]{:S(2)}, u32[]{:S(2)}) collective-permute-start(bf16[48,512]{1,0:T(8,128)(2,1)S(1)} %get-tuple-element.98), channel_id=1, source_target_pairs={{0,7},{1,0},{2,1},{3,2},{4,3},{5,4},{6,5},{7,6},{8,15},{9,8},{10,9... | collective-permute-start | bytes 147464 | tf_op jit(solution)/shard_map/ppermute | solution.py:413
  60.3 4.6 %collective-permute-start.14 = (bf16[48,512]{1,0:T(8,128)(2,1)S(1)}, bf16[48,512]{1,0:T(8,128)(2,1)S(1)}, u32[]{:S(2)}, u32[]{:S(2)}) collective-permute-start(bf16[48,512]{1,0:T(8,128)(2,1)S(1)} %get-tuple-element.99), channel_id=1, source_target_pairs={{0,31},{1,24},{2,25},{3,26},{4,27},{5,28},{6,29},{7,30},{8,7},{9,0... | collective-permute-start | bytes 147464 | tf_op jit(solution)/shard_map/ppermute | solution.py:413
  72.7 9.7 %collective-permute-start.15 = (bf16[288,512]{1,0:T(8,128)(2,1)S(1)}, bf16[288,512]{1,0:T(8,128)(2,1)S(1)}, u32[]{:S(2)}, u32[]{:S(2)}) collective-permute-start(bf16[288,512]{1,0:T(8,128)(2,1)S(1)} %get-tuple-element.103), channel_id=1, source_target_pairs={{0,8},{1,9},{2,10},{3,11},{4,12},{5,13},{6,14},{7,15},{8,16},{9,17... | collective-permute-start | bytes 884744 | tf_op jit(solution)/shard_map/ppermute | solution.py:413
  75.1 5.3 %collective-permute-start.16 = (bf16[48,512]{1,0:T(8,128)(2,1)S(1)}, bf16[48,512]{1,0:T(8,128)(2,1)S(1)}, u32[]{:S(2)}, u32[]{:S(2)}) collective-permute-start(bf16[48,512]{1,0:T(8,128)(2,1)S(1)} %get-tuple-element.104), channel_id=1, source_target_pairs={{0,1},{1,2},{2,3},{3,4},{4,5},{5,6},{6,7},{7,0},{8,9},{9,10},{10,1... | collective-permute-start | bytes 147464 | tf_op jit(solution)/shard_map/ppermute | solution.py:413
  75.1 7.2 %collective-permute-start.17 = (bf16[48,512]{1,0:T(8,128)(2,1)S(1)}, bf16[48,512]{1,0:T(8,128)(2,1)S(1)}, u32[]{:S(2)}, u32[]{:S(2)}) collective-permute-start(bf16[48,512]{1,0:T(8,128)(2,1)S(1)} %get-tuple-element.105), channel_id=1, source_target_pairs={{0,9},{1,10},{2,11},{3,12},{4,13},{5,14},{6,15},{7,8},{8,17},{9,18... | collective-permute-start | bytes 147464 | tf_op jit(solution)/shard_map/ppermute | solution.py:413
  84.5 16.7 %collective-permute-start.21 = (bf16[96,512]{1,0:T(8,128)(2,1)S(1)}, bf16[96,512]{1,0:T(8,128)(2,1)S(1)}, u32[]{:S(2)}, u32[]{:S(2)}) collective-permute-start(bf16[96,512]{1,0:T(8,128)(2,1)S(1)} %get-tuple-element.121), channel_id=1, source_target_pairs={{0,4},{1,5},{2,6},{3,7},{4,0},{5,1},{6,2},{7,3},{8,12},{9,13},{10,... | collective-permute-start | bytes 294920 | tf_op jit(solution)/shard_map/ppermute | solution.py:418
  84.6 16.6 %collective-permute-start.22 = (bf16[96,512]{1,0:T(8,128)(2,1)S(1)}, bf16[96,512]{1,0:T(8,128)(2,1)S(1)}, u32[]{:S(2)}, u32[]{:S(2)}) collective-permute-start(bf16[96,512]{1,0:T(8,128)(2,1)S(1)} %get-tuple-element.122), channel_id=1, source_target_pairs={{0,6},{1,7},{2,4},{3,5},{4,2},{5,3},{6,0},{7,1},{8,14},{9,15},{10,... | collective-permute-start | bytes 294920 | tf_op jit(solution)/shard_map/ppermute | solution.py:418
  88.4 12.8 %collective-permute-start.18 = (bf16[192,512]{1,0:T(8,128)(2,1)S(1)}, bf16[192,512]{1,0:T(8,128)(2,1)S(1)}, u32[]{:S(2)}, u32[]{:S(2)}) collective-permute-start(bf16[192,512]{1,0:T(8,128)(2,1)S(1)} %get-tuple-element.118), channel_id=1, source_target_pairs={{0,2},{1,3},{2,0},{3,1},{4,6},{5,7},{6,4},{7,5},{8,10},{9,11},{10,... | collective-permute-start | bytes 589832 | tf_op jit(solution)/shard_map/ppermute | solution.py:418
  93.0 12.0 %collective-permute-start.19 = (bf16[96,512]{1,0:T(8,128)(2,1)S(1)}, bf16[96,512]{1,0:T(8,128)(2,1)S(1)}, u32[]{:S(2)}, u32[]{:S(2)}) collective-permute-start(bf16[96,512]{1,0:T(8,128)(2,1)S(1)} %get-tuple-element.113), channel_id=1, source_target_pairs={{0,4},{1,5},{2,6},{3,7},{4,0},{5,1},{6,2},{7,3},{8,12},{9,13},{10,... | collective-permute-start | bytes 294920 | tf_op jit(solution)/shard_map/ppermute | solution.py:418
  94.6 10.4 %collective-permute-start.20 = (bf16[96,512]{1,0:T(8,128)(2,1)S(1)}, bf16[96,512]{1,0:T(8,128)(2,1)S(1)}, u32[]{:S(2)}, u32[]{:S(2)}) collective-permute-start(bf16[96,512]{1,0:T(8,128)(2,1)S(1)} %get-tuple-element.115), channel_id=1, source_target_pairs={{0,6},{1,7},{2,4},{3,5},{4,2},{5,3},{6,0},{7,1},{8,14},{9,15},{10,... | collective-permute-start | bytes 294920 | tf_op jit(solution)/shard_map/ppermute | solution.py:418
  103.0 9.0 %collective-permute-start.24 = (bf16[96,512]{1,0:T(8,128)(2,1)S(1)}, bf16[96,512]{1,0:T(8,128)(2,1)S(1)}, u32[]{:S(2)}, u32[]{:S(2)}) collective-permute-start(bf16[96,512]{1,0:T(8,128)(2,1)S(1)} %get-tuple-element.127), channel_id=1, source_target_pairs={{0,4},{1,5},{2,6},{3,7},{4,0},{5,1},{6,2},{7,3},{8,12},{9,13},{10,... | collective-permute-start | bytes 294920 | tf_op jit(solution)/shard_map/ppermute | solution.py:418
  104.1 8.7 %collective-permute-start.26 = (bf16[96,512]{1,0:T(8,128)(2,1)S(1)}, bf16[96,512]{1,0:T(8,128)(2,1)S(1)}, u32[]{:S(2)}, u32[]{:S(2)}) collective-permute-start(bf16[96,512]{1,0:T(8,128)(2,1)S(1)} %get-tuple-element.130), channel_id=1, source_target_pairs={{0,6},{1,7},{2,4},{3,5},{4,2},{5,3},{6,0},{7,1},{8,14},{9,15},{10,... | collective-permute-start | bytes 294920 | tf_op jit(solution)/shard_map/ppermute | solution.py:418
  106.8 14.5 %collective-permute-start.23 = (bf16[192,512]{1,0:T(8,128)(2,1)S(1)}, bf16[192,512]{1,0:T(8,128)(2,1)S(1)}, u32[]{:S(2)}, u32[]{:S(2)}) collective-permute-start(bf16[192,512]{1,0:T(8,128)(2,1)S(1)} %get-tuple-element.126), channel_id=1, source_target_pairs={{0,2},{1,3},{2,0},{3,1},{4,6},{5,7},{6,4},{7,5},{8,10},{9,11},{10,... | collective-permute-start | bytes 589832 | tf_op jit(solution)/shard_map/ppermute | solution.py:418
  112.0 9.2 %collective-permute-start.25 = (bf16[96,512]{1,0:T(8,128)(2,1)S(1)}, bf16[96,512]{1,0:T(8,128)(2,1)S(1)}, u32[]{:S(2)}, u32[]{:S(2)}) collective-permute-start(bf16[96,512]{1,0:T(8,128)(2,1)S(1)} %get-tuple-element.129), channel_id=1, source_target_pairs={{0,4},{1,5},{2,6},{3,7},{4,0},{5,1},{6,2},{7,3},{8,12},{9,13},{10,... | collective-permute-start | bytes 294920 | tf_op jit(solution)/shard_map/ppermute | solution.py:418
  112.8 8.5 %collective-permute-start.27 = (bf16[96,512]{1,0:T(8,128)(2,1)S(1)}, bf16[96,512]{1,0:T(8,128)(2,1)S(1)}, u32[]{:S(2)}, u32[]{:S(2)}) collective-permute-start(bf16[96,512]{1,0:T(8,128)(2,1)S(1)} %get-tuple-element.132), channel_id=1, source_target_pairs={{0,6},{1,7},{2,4},{3,5},{4,2},{5,3},{6,0},{7,1},{8,14},{9,15},{10,... | collective-permute-start | bytes 294920 | tf_op jit(solution)/shard_map/ppermute | solution.py:418

commit v5 on v4

--- a/solution.py
+++ b/solution.py
@@ -143,12 +143,12 @@
             picked = jnp.concatenate(
                 [mixed_t[h * width : (h + 1) * width, h * main : (h + 1) * main] for h in range(group)], axis=0
             )
-            first = jnp.transpose(picked)
+            first = jnp.transpose(picked.astype(BF16))
             tail = jnp.transpose(mixed_t[:, group * main :])
             second = tail[:rest] * keep_f[0]
             for h in range(1, group):
                 second = second + tail[h * rest : (h + 1) * rest] * keep_f[h]
-            context = jnp.concatenate([first, second], axis=0).astype(BF16)
+            context = jnp.concatenate([first, second.astype(BF16)], axis=0)
             context_ref[rows, g * LANES : (g + 1) * LANES] = context
 
     for window in range(windows):

time: 124 us -> 124 us (level)
  no operation moved by 1% of the time
where the time goes in v5:
time: 124 us
  Pallas kernels  52.8 us (43%)
  starting transfers between devices  41.6 us (34%)
  waiting for transfers between devices  28.2 us (23%)
    ppermute x22, starting transfers between devices, between(): lax.ppermute(value, 'lon', [(s, s ^ distance) for s in range(sectors)])  33.3 us
    pallas_call x6, Pallas kernels, call(): pl.pallas_call(body, in_specs=specs, out_specs=[IN_VMEM] * len(outs), out...  29 us
    ppermute x22, waiting for transfers between devices, between(): lax.ppermute(value, 'lon', [(s, s ^ distance) for s in range(sectors)])  18.1 us
    pallas_call x4, Pallas kernels, run_near(): pl.pallas_call(functools.partial(near_kernel, plan=plan, base=base, layer...  16.6 us
    ppermute x6, waiting for transfers between devices, shift(): lax.ppermute(value, ('lat', 'lon'), lat_lon_pairs(lat_step, lon_step))  10 us
    ppermute x6, starting transfers between devices, shift(): lax.ppermute(value, ('lat', 'lon'), lat_lon_pairs(lat_step, lon_step))  8.3 us
    pallas_call x4, Pallas kernels, run_away(): pl.pallas_call(functools.partial(away_kernel, whole=len(whole), cut=len(c...  7.22 us
  transfers between devices with their start and end apart: 28, of which 11 were waited for; matrix products, arithmetic and copies ran while one was open for 0% of the time, Pallas kernels for 33%

profile of v5, /device:TPU:0, one launch (start us, length us, event | category | flops | bytes accessed | tf_op | source)
XLA Modules:
  0.0 123.5 jit_solution(6528490376646268915)
XLA Ops:
  0.0 0.5 collective-permute-start
  0.5 0.1 collective-permute-start.1
  0.5 0.6 add_bitcast_fusion.refs_0_
  1.1 12.3 %shard_map.109 = (bf16[576,512]{1,0:T(8,128)(2,1)S(1)}, f32[576,2]{1,0:T(8,128)S(1)}, bf16[96,512]{1,0:T(8,128)(2,1)S(1)}, bf16[96,512]{1,0:T(8,128)(2,1)S(1)}, ...) custom-call(s32[1,3]{1,0:T(1,128)} %add_bitcast_fusion.refs_0_, ...), custom_call_target="tpu_custom_call" | custom-call | flops 4000000000 | bytes 4832140 | tf_op jit(solution)/shard_map/pallas_call | solution.py:359
  13.4 4.1 %collective-permute-start.5 = (bf16[96,512]{1,0:T(8,128)(2,1)S(1)}, bf16[96,512]{1,0:T(8,128)(2,1)S(1)}, u32[]{:S(2)}, u32[]{:S(2)}) collective-permute-start(bf16[96,512]{1,0:T(8,128)(2,1)S(1)} %get-tuple-element.84), channel_id=1, source_target_pairs={{0,4},{1,5},{2,6},{3,7},{4,0},{5,1},{6,2},{7,3},{8,12},{9,13},{10,... | collective-permute-start | bytes 294920 | tf_op jit(solution)/shard_map/ppermute | solution.py:418
  17.5 1.4 %collective-permute-start.6 = (bf16[96,512]{1,0:T(8,128)(2,1)S(1)}, bf16[96,512]{1,0:T(8,128)(2,1)S(1)}, u32[]{:S(2)}, u32[]{:S(2)}) collective-permute-start(bf16[96,512]{1,0:T(8,128)(2,1)S(1)} %get-tuple-element.85), channel_id=1, source_target_pairs={{0,6},{1,7},{2,4},{3,5},{4,2},{5,3},{6,0},{7,1},{8,14},{9,15},{10,... | collective-permute-start | bytes 294920 | tf_op jit(solution)/shard_map/ppermute | solution.py:418
  18.9 0.2 collective-permute-start.2
  19.1 4.1 %shard_map.111 = (bf16[96,512]{1,0:T(8,128)(2,1)S(1)}, bf16[4,512,1024]{2,1,0:T(8,128)(2,1)S(1)}, bf16[4,1024,512]{2,1,0:T(8,128)(2,1)S(1)}) custom-call(bf16[96,512]{1,0:T(8,128)(2,1)S(1)} %get-tuple-element.72.refs_0_, bf16[2,4,512,1024]{3,2,1,0:T(8,128)(2,1)} %refs_1_.7, bf16[2,4,1024,512]{3,2,1,0:T(8,128)(2,1)} %refs_2_.3), custom_call_target="tpu_custom_call" | custom-call | flops 3000000000 | bytes 8388608 | tf_op jit(solution)/shard_map/pallas_call | solution.py:373
  23.3 2.1 %collective-permute-done.5.refs_1_ = bf16[96,512]{1,0:T(8,128)(2,1)S(1)} collective-permute-done((bf16[96,512]{1,0:T(8,128)(2,1)S(1)}, bf16[96,512]{1,0:T(8,128)(2,1)S(1)}, u32[]{:S(2)}, u32[]{:S(2)}) %collective-permute-start.5) | collective-permute-done | bytes 98336 | tf_op jit(solution)/shard_map/ppermute | solution.py:418
  25.4 0.8 collective-permute-start.3
  26.2 0.0 collective-permute-done.6.refs_2_
  26.2 2.2 %collective-permute-start.4 = (bf16[96,512]{1,0:T(8,128)(2,1)S(1)}, bf16[96,512]{1,0:T(8,128)(2,1)S(1)}, u32[]{:S(2)}, u32[]{:S(2)}) collective-permute-start(bf16[96,512]{1,0:T(8,128)(2,1)S(1)} %get-tuple-element.78), channel_id=1, source_target_pairs={{0,6},{1,7},{2,4},{3,5},{4,2},{5,3},{6,0},{7,1},{8,14},{9,15},{10,... | collective-permute-start | bytes 294920 | tf_op jit(solution)/shard_map/ppermute | solution.py:418
  28.4 0.9 collective-permute-done.2.refs_0_
  29.3 1.9 %shard_map.113 = (bf16[96,512]{1,0:T(8,128)(2,1)S(1)}, bf16[96,512]{1,0:T(8,128)(2,1)S(1)}, bf16[96,512]{1,0:T(8,128)(2,1)S(1)}) custom-call(bf16[192,512]{1,0:T(8,128)(2,1)S(1)} %collective-permute-done.2.refs_0_, bf16[96,512]{1,0:T(8,128)(2,1)S(1)} %collective-permute-done.5.refs_1_, bf16[96,512]{1,0:T(8,128)(2,1)S(1)} %collective-permute-done.6.refs_2_, ...), custom_call_target="tpu_custom_call" | custom-call | flops 3000000000 | bytes 1048576 | tf_op jit(solution)/shard_map/pallas_call | solution.py:392
  31.2 1.2 collective-permute-start.8
  32.4 0.0 collective-permute-done.refs_1_
  32.4 2.6 %collective-permute-start.10 = (bf16[96,512]{1,0:T(8,128)(2,1)S(1)}, bf16[96,512]{1,0:T(8,128)(2,1)S(1)}, u32[]{:S(2)}, u32[]{:S(2)}) collective-permute-start(bf16[96,512]{1,0:T(8,128)(2,1)S(1)} %get-tuple-element.93), channel_id=1, source_target_pairs={{0,6},{1,7},{2,4},{3,5},{4,2},{5,3},{6,0},{7,1},{8,14},{9,15},{10,... | collective-permute-start | bytes 294920 | tf_op jit(solution)/shard_map/ppermute | solution.py:418
  35.1 0.0 collective-permute-done.1.refs_2_
  35.1 4.1 %shard_map.112 = (bf16[96,512]{1,0:T(8,128)(2,1)S(1)}, bf16[4,512,1024]{2,1,0:T(8,128)(2,1)S(1)}, bf16[4,1024,512]{2,1,0:T(8,128)(2,1)S(1)}) custom-call(bf16[96,512]{1,0:T(8,128)(2,1)S(1)} %get-tuple-element.79.refs_0_, bf16[2,4,512,1024]{3,2,1,0:T(8,128)(2,1)} %collective-permute-done.refs_1_, bf16[2,4,1024,512]{3,2,1,0:T(8,128)(2,1)} %collective-permute-done.1.refs_2_), custom_call_target="tpu_custom_call" | custom-call | flops 3000000000 | bytes 8388608 | tf_op jit(solution)/shard_map/pallas_call | solution.py:373
  39.2 0.0 collective-permute-done.3.refs_1_
  39.2 0.0 collective-permute-done.4.refs_2_
  39.2 1.7 %shard_map.114 = (bf16[192,512]{1,0:T(8,128)(2,1)S(1)}, bf16[96,512]{1,0:T(8,128)(2,1)S(1)}, bf16[96,512]{1,0:T(8,128)(2,1)S(1)}) custom-call(bf16[192,512]{1,0:T(8,128)(2,1)S(1)} %collective-permute-done.2.refs_0_, bf16[96,512]{1,0:T(8,128)(2,1)S(1)} %collective-permute-done.3.refs_1_, bf16[96,512]{1,0:T(8,128)(2,1)S(1)} %collective-permute-done.4.refs_2_, ...), custom_call_target="tpu_custom_call" | custom-call | flops 3000000000 | bytes 1048576 | tf_op jit(solution)/shard_map/pallas_call | solution.py:392
  41.0 3.1 %collective-permute-start.7 = (bf16[192,512]{1,0:T(8,128)(2,1)S(1)}, bf16[192,512]{1,0:T(8,128)(2,1)S(1)}, u32[]{:S(2)}, u32[]{:S(2)}) collective-permute-start(bf16[192,512]{1,0:T(8,128)(2,1)S(1)} %get-tuple-element.89), channel_id=1, source_target_pairs={{0,2},{1,3},{2,0},{3,1},{4,6},{5,7},{6,4},{7,5},{8,10},{9,11},{10,... | collective-permute-start | bytes 589832 | tf_op jit(solution)/shard_map/ppermute | solution.py:418
  44.1 0.0 collective-permute-done.8.refs_6_
  44.1 1.5 %collective-permute-start.11 = (bf16[96,512]{1,0:T(8,128)(2,1)S(1)}, bf16[96,512]{1,0:T(8,128)(2,1)S(1)}, u32[]{:S(2)}, u32[]{:S(2)}) collective-permute-start(bf16[96,512]{1,0:T(8,128)(2,1)S(1)} %get-tuple-element.95), channel_id=1, source_target_pairs={{0,6},{1,7},{2,4},{3,5},{4,2},{5,3},{6,0},{7,1},{8,14},{9,15},{10,... | collective-permute-start | bytes 294920 | tf_op jit(solution)/shard_map/ppermute | solution.py:418
  45.6 1.4 %collective-permute-start.9 = (bf16[96,512]{1,0:T(8,128)(2,1)S(1)}, bf16[96,512]{1,0:T(8,128)(2,1)S(1)}, u32[]{:S(2)}, u32[]{:S(2)}) collective-permute-start(bf16[96,512]{1,0:T(8,128)(2,1)S(1)} %get-tuple-element.92), channel_id=1, source_target_pairs={{0,4},{1,5},{2,6},{3,7},{4,0},{5,1},{6,2},{7,3},{8,12},{9,13},{10,... | collective-permute-start | bytes 294920 | tf_op jit(solution)/shard_map/ppermute | solution.py:418
  47.0 4.2 %shard_map.110 = (f32[672,2]{1,0:T(8,128)S(1)}, f32[1,672]{1,0:T(1,128)S(1)}, bf16[512,1536]{1,0:T(8,128)(2,1)S(1)}, bf16[512,512]{1,0:T(8,128)(2,1)S(1)}) custom-call(s32[1,3]{1,0:T(1,128)} %add_bitcast_fusion.refs_0_, s32[2,1,576]{2,1,0:T(1,128)} %bitcast.13, s32[1,672]{1,0:T(1,128)} %constant.46.refs_2_, bf16[2,512,1536]{2,1,0:T(8,128)(2,1)} %refs_3_.1, ...), custom_call_target="tpu_custom_call" | custom-call | flops 2000000000 | bytes 4206220 | tf_op jit(solution)/shard_map/pallas_call | solution.py:359
  51.2 2.3 %collective-permute-done.11.refs_9_ = bf16[96,512]{1,0:T(8,128)(2,1)S(1)} collective-permute-done((bf16[96,512]{1,0:T(8,128)(2,1)S(1)}, bf16[96,512]{1,0:T(8,128)(2,1)S(1)}, u32[]{:S(2)}, u32[]{:S(2)}) %collective-permute-start.11) | collective-permute-done | bytes 98336 | tf_op jit(solution)/shard_map/ppermute | solution.py:418
  53.5 2.3 %collective-permute-done.9.refs_7_ = bf16[96,512]{1,0:T(8,128)(2,1)S(1)} collective-permute-done((bf16[96,512]{1,0:T(8,128)(2,1)S(1)}, bf16[96,512]{1,0:T(8,128)(2,1)S(1)}, u32[]{:S(2)}, u32[]{:S(2)}) %collective-permute-start.9) | collective-permute-done | bytes 98336 | tf_op jit(solution)/shard_map/ppermute | solution.py:418
  55.8 0.0 collective-permute-done.7.refs_5_
  55.8 0.7 shard_map.115
  56.5 2.5 %collective-permute-start.12 = (bf16[288,512]{1,0:T(8,128)(2,1)S(1)}, bf16[288,512]{1,0:T(8,128)(2,1)S(1)}, u32[]{:S(2)}, u32[]{:S(2)}) collective-permute-start(bf16[288,512]{1,0:T(8,128)(2,1)S(1)} %get-tuple-element.97), channel_id=1, source_target_pairs={{0,24},{1,25},{2,26},{3,27},{4,28},{5,29},{6,30},{7,31},{8,0},{9,1... | collective-permute-start | bytes 884744 | tf_op jit(solution)/shard_map/ppermute | solution.py:413
  58.9 1.3 %collective-permute-start.13 = (bf16[48,512]{1,0:T(8,128)(2,1)S(1)}, bf16[48,512]{1,0:T(8,128)(2,1)S(1)}, u32[]{:S(2)}, u32[]{:S(2)}) collective-permute-start(bf16[48,512]{1,0:T(8,128)(2,1)S(1)} %get-tuple-element.98), channel_id=1, source_target_pairs={{0,7},{1,0},{2,1},{3,2},{4,3},{5,4},{6,5},{7,6},{8,15},{9,8},{10,9... | collective-permute-start | bytes 147464 | tf_op jit(solution)/shard_map/ppermute | solution.py:413
  60.3 1.2 collective-permute-start.14
  61.4 0.6 collective-permute-done.13.refs_4_
  62.0 2.9 %collective-permute-done.14.refs_5_ = bf16[48,512]{1,0:T(8,128)(2,1)S(1)} collective-permute-done((bf16[48,512]{1,0:T(8,128)(2,1)S(1)}, bf16[48,512]{1,0:T(8,128)(2,1)S(1)}, u32[]{:S(2)}, u32[]{:S(2)}) %collective-permute-start.14) | collective-permute-done | bytes 49184 | tf_op jit(solution)/shard_map/ppermute | solution.py:413
  64.9 0.2 collective-permute-done.12.refs_3_
  65.1 7.5 %shard_map.116 = (bf16[288,512]{1,0:T(8,128)(2,1)S(1)}, bf16[288,512]{1,0:T(8,128)(2,1)S(1)}, bf16[48,512]{1,0:T(8,128)(2,1)S(1)}, bf16[48,512]{1,0:T(8,128)(2,1)S(1)}) custom-call(s32[1,3]{1,0:T(1,128)} %add_bitcast_fusion.refs_0_, f32[2,16]{1,0:T(2,128)} %refs_1_.6, bf16[288,512]{1,0:T(8,128)(2,1)S(1)} %get-tuple-element.96.refs_2_, ...), custom_call_target="tpu_custom_call" | custom-call | flops 3000000000 | bytes 2793612 | tf_op jit(solution)/shard_map/pallas_call | solution.py:359
  72.7 2.4 %collective-permute-start.15 = (bf16[288,512]{1,0:T(8,128)(2,1)S(1)}, bf16[288,512]{1,0:T(8,128)(2,1)S(1)}, u32[]{:S(2)}, u32[]{:S(2)}) collective-permute-start(bf16[288,512]{1,0:T(8,128)(2,1)S(1)} %get-tuple-element.103), channel_id=1, source_target_pairs={{0,8},{1,9},{2,10},{3,11},{4,12},{5,13},{6,14},{7,15},{8,16},{9,17... | collective-permute-start | bytes 884744 | tf_op jit(solution)/shard_map/ppermute | solution.py:413
  75.1 0.9 collective-permute-start.17
  76.0 4.4 %collective-permute-done.16.refs_2_ = bf16[48,512]{1,0:T(8,128)(2,1)S(1)} collective-permute-done((bf16[48,512]{1,0:T(8,128)(2,1)S(1)}, bf16[48,512]{1,0:T(8,128)(2,1)S(1)}, u32[]{:S(2)}, u32[]{:S(2)}) %collective-permute-start.16) | collective-permute-done | bytes 49184 | tf_op jit(solution)/shard_map/ppermute | solution.py:413
  80.4 1.9 %collective-permute-done.17.refs_3_ = bf16[48,512]{1,0:T(8,128)(2,1)S(1)} collective-permute-done((bf16[48,512]{1,0:T(8,128)(2,1)S(1)}, bf16[48,512]{1,0:T(8,128)(2,1)S(1)}, u32[]{:S(2)}, u32[]{:S(2)}) %collective-permute-start.17) | collective-permute-done | bytes 49184 | tf_op jit(solution)/shard_map/ppermute | solution.py:413
  82.3 2.1 %shard_map.117 = (bf16[672,512]{1,0:T(8,128)(2,1)S(1)}, f32[672,2]{1,0:T(8,128)S(1)}, bf16[96,512]{1,0:T(8,128)(2,1)S(1)}, bf16[96,512]{1,0:T(8,128)(2,1)S(1)}, ...) custom-call(bf16[288,512]{1,0:T(8,128)(2,1)S(1)} %get-tuple-element., ...), custom_call_target="tpu_custom_call" | custom-call | flops 1000000000 | bytes 737152 | tf_op jit(solution)/shard_map/pallas_call | solution.py:359
  84.4 0.1 collective-permute-start.21
  84.5 3.8 %collective-permute-start.22 = (bf16[96,512]{1,0:T(8,128)(2,1)S(1)}, bf16[96,512]{1,0:T(8,128)(2,1)S(1)}, u32[]{:S(2)}, u32[]{:S(2)}) collective-permute-start(bf16[96,512]{1,0:T(8,128)(2,1)S(1)} %get-tuple-element.122), channel_id=1, source_target_pairs={{0,6},{1,7},{2,4},{3,5},{4,2},{5,3},{6,0},{7,1},{8,14},{9,15},{10,... | collective-permute-start | bytes 294920 | tf_op jit(solution)/shard_map/ppermute | solution.py:418
  88.3 0.5 collective-permute-start.18
  88.8 4.1 %shard_map.118 = (bf16[96,512]{1,0:T(8,128)(2,1)S(1)}, bf16[4,512,1024]{2,1,0:T(8,128)(2,1)S(1)}, bf16[4,1024,512]{2,1,0:T(8,128)(2,1)S(1)}) custom-call(bf16[96,512]{1,0:T(8,128)(2,1)S(1)} %get-tuple-element.109.refs_0_, bf16[2,4,512,1024]{3,2,1,0:T(8,128)(2,1)} %refs_1_.7, bf16[2,4,1024,512]{3,2,1,0:T(8,128)(2,1)} %refs_2_.3), custom_call_target="tpu_custom_call" | custom-call | flops 3000000000 | bytes 8388608 | tf_op jit(solution)/shard_map/pallas_call | solution.py:373
  93.0 1.5 %collective-permute-start.19 = (bf16[96,512]{1,0:T(8,128)(2,1)S(1)}, bf16[96,512]{1,0:T(8,128)(2,1)S(1)}, u32[]{:S(2)}, u32[]{:S(2)}) collective-permute-start(bf16[96,512]{1,0:T(8,128)(2,1)S(1)} %get-tuple-element.113), channel_id=1, source_target_pairs={{0,4},{1,5},{2,6},{3,7},{4,0},{5,1},{6,2},{7,3},{8,12},{9,13},{10,... | collective-permute-start | bytes 294920 | tf_op jit(solution)/shard_map/ppermute | solution.py:418
  94.5 2.4 %collective-permute-start.20 = (bf16[96,512]{1,0:T(8,128)(2,1)S(1)}, bf16[96,512]{1,0:T(8,128)(2,1)S(1)}, u32[]{:S(2)}, u32[]{:S(2)}) collective-permute-start(bf16[96,512]{1,0:T(8,128)(2,1)S(1)} %get-tuple-element.115), channel_id=1, source_target_pairs={{0,6},{1,7},{2,4},{3,5},{4,2},{5,3},{6,0},{7,1},{8,14},{9,15},{10,... | collective-permute-start | bytes 294920 | tf_op jit(solution)/shard_map/ppermute | solution.py:418
  96.9 4.1 %shard_map.119 = (bf16[96,512]{1,0:T(8,128)(2,1)S(1)}, bf16[4,512,1024]{2,1,0:T(8,128)(2,1)S(1)}, bf16[4,1024,512]{2,1,0:T(8,128)(2,1)S(1)}) custom-call(bf16[96,512]{1,0:T(8,128)(2,1)S(1)} %get-tuple-element.116.refs_0_, bf16[2,4,512,1024]{3,2,1,0:T(8,128)(2,1)} %collective-permute-done.refs_1_, bf16[2,4,1024,512]{3,2,1,0:T(8,128)(2,1)} %collective-permute-done.1.refs_2_), custom_call_target="tpu_custom_call" | custom-call | flops 3000000000 | bytes 8388608 | tf_op jit(solution)/shard_map/pallas_call | solution.py:373
  101.1 0.0 collective-permute-done.21.refs_1_
  101.1 0.0 collective-permute-done.22.refs_2_
  101.1 1.8 %shard_map.120 = (bf16[96,512]{1,0:T(8,128)(2,1)S(1)}, bf16[96,512]{1,0:T(8,128)(2,1)S(1)}, bf16[96,512]{1,0:T(8,128)(2,1)S(1)}) custom-call(bf16[192,512]{1,0:T(8,128)(2,1)S(1)} %collective-permute-done.18.refs_0_, bf16[96,512]{1,0:T(8,128)(2,1)S(1)} %collective-permute-done.21.refs_1_, bf16[96,512]{1,0:T(8,128)(2,1)S(1)} %collective-permute-done.22.refs_2_, ...), custom_call_target="tpu_custom_call" | custom-call | flops 3000000000 | bytes 1048576 | tf_op jit(solution)/shard_map/pallas_call | solution.py:392
  102.9 1.1 collective-permute-start.24
  104.0 0.9 collective-permute-start.26
  104.9 0.0 collective-permute-done.19.refs_1_
  104.9 0.0 collective-permute-done.20.refs_2_
  104.9 1.8 %shard_map.121 = (bf16[192,512]{1,0:T(8,128)(2,1)S(1)}, bf16[96,512]{1,0:T(8,128)(2,1)S(1)}, bf16[96,512]{1,0:T(8,128)(2,1)S(1)}) custom-call(bf16[192,512]{1,0:T(8,128)(2,1)S(1)} %collective-permute-done.18.refs_0_, bf16[96,512]{1,0:T(8,128)(2,1)S(1)} %collective-permute-done.19.refs_1_, bf16[96,512]{1,0:T(8,128)(2,1)S(1)} %collective-permute-done.20.refs_2_, ...), custom_call_target="tpu_custom_call" | custom-call | flops 3000000000 | bytes 1048576 | tf_op jit(solution)/shard_map/pallas_call | solution.py:392
  106.7 1.7 %collective-permute-start.23 = (bf16[192,512]{1,0:T(8,128)(2,1)S(1)}, bf16[192,512]{1,0:T(8,128)(2,1)S(1)}, u32[]{:S(2)}, u32[]{:S(2)}) collective-permute-start(bf16[192,512]{1,0:T(8,128)(2,1)S(1)} %get-tuple-element.126), channel_id=1, source_target_pairs={{0,2},{1,3},{2,0},{3,1},{4,6},{5,7},{6,4},{7,5},{8,10},{9,11},{10,... | collective-permute-start | bytes 589832 | tf_op jit(solution)/shard_map/ppermute | solution.py:418
  108.4 3.5 %collective-permute-done.24.refs_6_ = bf16[96,512]{1,0:T(8,128)(2,1)S(1)} collective-permute-done((bf16[96,512]{1,0:T(8,128)(2,1)S(1)}, bf16[96,512]{1,0:T(8,128)(2,1)S(1)}, u32[]{:S(2)}, u32[]{:S(2)}) %collective-permute-start.24) | collective-permute-done | bytes 98336 | tf_op jit(solution)/shard_map/ppermute | solution.py:418
  111.9 0.8 collective-permute-start.25
  112.7 1.4 %collective-permute-start.27 = (bf16[96,512]{1,0:T(8,128)(2,1)S(1)}, bf16[96,512]{1,0:T(8,128)(2,1)S(1)}, u32[]{:S(2)}, u32[]{:S(2)}) collective-permute-start(bf16[96,512]{1,0:T(8,128)(2,1)S(1)} %get-tuple-element.132), channel_id=1, source_target_pairs={{0,6},{1,7},{2,4},{3,5},{4,2},{5,3},{6,0},{7,1},{8,14},{9,15},{10,... | collective-permute-start | bytes 294920 | tf_op jit(solution)/shard_map/ppermute | solution.py:418
  114.2 7.0 %collective-permute-done.25.refs_7_ = bf16[96,512]{1,0:T(8,128)(2,1)S(1)} collective-permute-done((bf16[96,512]{1,0:T(8,128)(2,1)S(1)}, bf16[96,512]{1,0:T(8,128)(2,1)S(1)}, u32[]{:S(2)}, u32[]{:S(2)}) %collective-permute-start.25) | collective-permute-done | bytes 98336 | tf_op jit(solution)/shard_map/ppermute | solution.py:418
  121.1 2.2 %shard_map.122 = bf16[576,512]{1,0:T(8,128)(2,1)} custom-call(bf16[672,512]{1,0:T(8,128)(2,1)S(1)} %get-tuple-element.107.refs_0_, f32[672,2]{1,0:T(8,128)S(1)} %get-tuple-element.108.refs_1_, s32[1,672]{1,0:T(1,128)} %constant.46.refs_2_, bf16[96,512]{1,0:T(8,128)(2,1)S(1)} %get-tuple-element.110.refs_3_, bf16[96,512]{1,0:T(8,128)(2,1)S(1)} %get-tuple-element.117.refs_4_, ...), custom_call_target="tpu_custom_call" | custom-call | flops 1000000000 | bytes 1482624 | tf_op jit(solution)/shard_map/pallas_call | solution.py:359
  (7 shorter events, 0.0 us)
Async XLA Ops:
  0.0 32.4 %collective-permute-start = (bf16[2,4,512,1024]{3,2,1,0:T(8,128)(2,1)}, bf16[2,4,512,1024]{3,2,1,0:T(8,128)(2,1)}, u32[]{:S(2)}, u32[]{:S(2)}) collective-permute-start(bf16[2,4,512,1024]{3,2,1,0:T(8,128)(2,1)} %refs_1_.7), channel_id=1, source_target_pairs={{0,1},{1,0},{2,3},{3,2},{4,5},{5,4},{6,7},{7,6},{8,9},{9,8},{10,11... | collective-permute-start | bytes 25165832 | tf_op jit(solution)/shard_map/ppermute | solution.py:418
  0.5 34.6 %collective-permute-start.1 = (bf16[2,4,1024,512]{3,2,1,0:T(8,128)(2,1)}, bf16[2,4,1024,512]{3,2,1,0:T(8,128)(2,1)}, u32[]{:S(2)}, u32[]{:S(2)}) collective-permute-start(bf16[2,4,1024,512]{3,2,1,0:T(8,128)(2,1)} %refs_2_.3), channel_id=1, source_target_pairs={{0,1},{1,0},{2,3},{3,2},{4,5},{5,4},{6,7},{7,6},{8,9},{9,8},{10,11... | collective-permute-start | bytes 25165832 | tf_op jit(solution)/shard_map/ppermute | solution.py:418
  13.4 12.0 %collective-permute-start.5 = (bf16[96,512]{1,0:T(8,128)(2,1)S(1)}, bf16[96,512]{1,0:T(8,128)(2,1)S(1)}, u32[]{:S(2)}, u32[]{:S(2)}) collective-permute-start(bf16[96,512]{1,0:T(8,128)(2,1)S(1)} %get-tuple-element.84), channel_id=1, source_target_pairs={{0,4},{1,5},{2,6},{3,7},{4,0},{5,1},{6,2},{7,3},{8,12},{9,13},{10,... | collective-permute-start | bytes 294920 | tf_op jit(solution)/shard_map/ppermute | solution.py:418
  17.5 8.6 %collective-permute-start.6 = (bf16[96,512]{1,0:T(8,128)(2,1)S(1)}, bf16[96,512]{1,0:T(8,128)(2,1)S(1)}, u32[]{:S(2)}, u32[]{:S(2)}) collective-permute-start(bf16[96,512]{1,0:T(8,128)(2,1)S(1)} %get-tuple-element.85), channel_id=1, source_target_pairs={{0,6},{1,7},{2,4},{3,5},{4,2},{5,3},{6,0},{7,1},{8,14},{9,15},{10,... | collective-permute-start | bytes 294920 | tf_op jit(solution)/shard_map/ppermute | solution.py:418
  18.9 10.4 %collective-permute-start.2 = (bf16[192,512]{1,0:T(8,128)(2,1)S(1)}, bf16[192,512]{1,0:T(8,128)(2,1)S(1)}, u32[]{:S(2)}, u32[]{:S(2)}) collective-permute-start(bf16[192,512]{1,0:T(8,128)(2,1)S(1)} %get-tuple-element.81), channel_id=1, source_target_pairs={{0,2},{1,3},{2,0},{3,1},{4,6},{5,7},{6,4},{7,5},{8,10},{9,11},{10,... | collective-permute-start | bytes 589832 | tf_op jit(solution)/shard_map/ppermute | solution.py:418
  25.4 13.8 %collective-permute-start.3 = (bf16[96,512]{1,0:T(8,128)(2,1)S(1)}, bf16[96,512]{1,0:T(8,128)(2,1)S(1)}, u32[]{:S(2)}, u32[]{:S(2)}) collective-permute-start(bf16[96,512]{1,0:T(8,128)(2,1)S(1)} %get-tuple-element.76), channel_id=1, source_target_pairs={{0,4},{1,5},{2,6},{3,7},{4,0},{5,1},{6,2},{7,3},{8,12},{9,13},{10,... | collective-permute-start | bytes 294920 | tf_op jit(solution)/shard_map/ppermute | solution.py:418
  26.2 13.1 %collective-permute-start.4 = (bf16[96,512]{1,0:T(8,128)(2,1)S(1)}, bf16[96,512]{1,0:T(8,128)(2,1)S(1)}, u32[]{:S(2)}, u32[]{:S(2)}) collective-permute-start(bf16[96,512]{1,0:T(8,128)(2,1)S(1)} %get-tuple-element.78), channel_id=1, source_target_pairs={{0,6},{1,7},{2,4},{3,5},{4,2},{5,3},{6,0},{7,1},{8,14},{9,15},{10,... | collective-permute-start | bytes 294920 | tf_op jit(solution)/shard_map/ppermute | solution.py:418
  31.2 12.9 %collective-permute-start.8 = (bf16[96,512]{1,0:T(8,128)(2,1)S(1)}, bf16[96,512]{1,0:T(8,128)(2,1)S(1)}, u32[]{:S(2)}, u32[]{:S(2)}) collective-permute-start(bf16[96,512]{1,0:T(8,128)(2,1)S(1)} %get-tuple-element.90), channel_id=1, source_target_pairs={{0,4},{1,5},{2,6},{3,7},{4,0},{5,1},{6,2},{7,3},{8,12},{9,13},{10,... | collective-permute-start | bytes 294920 | tf_op jit(solution)/shard_map/ppermute | solution.py:418
  32.4 11.7 %collective-permute-start.10 = (bf16[96,512]{1,0:T(8,128)(2,1)S(1)}, bf16[96,512]{1,0:T(8,128)(2,1)S(1)}, u32[]{:S(2)}, u32[]{:S(2)}) collective-permute-start(bf16[96,512]{1,0:T(8,128)(2,1)S(1)} %get-tuple-element.93), channel_id=1, source_target_pairs={{0,6},{1,7},{2,4},{3,5},{4,2},{5,3},{6,0},{7,1},{8,14},{9,15},{10,... | collective-permute-start | bytes 294920 | tf_op jit(solution)/shard_map/ppermute | solution.py:418
  41.0 14.8 %collective-permute-start.7 = (bf16[192,512]{1,0:T(8,128)(2,1)S(1)}, bf16[192,512]{1,0:T(8,128)(2,1)S(1)}, u32[]{:S(2)}, u32[]{:S(2)}) collective-permute-start(bf16[192,512]{1,0:T(8,128)(2,1)S(1)} %get-tuple-element.89), channel_id=1, source_target_pairs={{0,2},{1,3},{2,0},{3,1},{4,6},{5,7},{6,4},{7,5},{8,10},{9,11},{10,... | collective-permute-start | bytes 589832 | tf_op jit(solution)/shard_map/ppermute | solution.py:418
  44.1 9.4 %collective-permute-start.11 = (bf16[96,512]{1,0:T(8,128)(2,1)S(1)}, bf16[96,512]{1,0:T(8,128)(2,1)S(1)}, u32[]{:S(2)}, u32[]{:S(2)}) collective-permute-start(bf16[96,512]{1,0:T(8,128)(2,1)S(1)} %get-tuple-element.95), channel_id=1, source_target_pairs={{0,6},{1,7},{2,4},{3,5},{4,2},{5,3},{6,0},{7,1},{8,14},{9,15},{10,... | collective-permute-start | bytes 294920 | tf_op jit(solution)/shard_map/ppermute | solution.py:418
  45.6 10.1 %collective-permute-start.9 = (bf16[96,512]{1,0:T(8,128)(2,1)S(1)}, bf16[96,512]{1,0:T(8,128)(2,1)S(1)}, u32[]{:S(2)}, u32[]{:S(2)}) collective-permute-start(bf16[96,512]{1,0:T(8,128)(2,1)S(1)} %get-tuple-element.92), channel_id=1, source_target_pairs={{0,4},{1,5},{2,6},{3,7},{4,0},{5,1},{6,2},{7,3},{8,12},{9,13},{10,... | collective-permute-start | bytes 294920 | tf_op jit(solution)/shard_map/ppermute | solution.py:418
  56.5 8.7 %collective-permute-start.12 = (bf16[288,512]{1,0:T(8,128)(2,1)S(1)}, bf16[288,512]{1,0:T(8,128)(2,1)S(1)}, u32[]{:S(2)}, u32[]{:S(2)}) collective-permute-start(bf16[288,512]{1,0:T(8,128)(2,1)S(1)} %get-tuple-element.97), channel_id=1, source_target_pairs={{0,24},{1,25},{2,26},{3,27},{4,28},{5,29},{6,30},{7,31},{8,0},{9,1... | collective-permute-start | bytes 884744 | tf_op jit(solution)/shard_map/ppermute | solution.py:413
  58.9 3.1 %collective-permute-start.13 = (bf16[48,512]{1,0:T(8,128)(2,1)S(1)}, bf16[48,512]{1,0:T(8,128)(2,1)S(1)}, u32[]{:S(2)}, u32[]{:S(2)}) collective-permute-start(bf16[48,512]{1,0:T(8,128)(2,1)S(1)} %get-tuple-element.98), channel_id=1, source_target_pairs={{0,7},{1,0},{2,1},{3,2},{4,3},{5,4},{6,5},{7,6},{8,15},{9,8},{10,9... | collective-permute-start | bytes 147464 | tf_op jit(solution)/shard_map/ppermute | solution.py:413
  60.3 4.6 %collective-permute-start.14 = (bf16[48,512]{1,0:T(8,128)(2,1)S(1)}, bf16[48,512]{1,0:T(8,128)(2,1)S(1)}, u32[]{:S(2)}, u32[]{:S(2)}) collective-permute-start(bf16[48,512]{1,0:T(8,128)(2,1)S(1)} %get-tuple-element.99), channel_id=1, source_target_pairs={{0,31},{1,24},{2,25},{3,26},{4,27},{5,28},{6,29},{7,30},{8,7},{9,0... | collective-permute-start | bytes 147464 | tf_op jit(solution)/shard_map/ppermute | solution.py:413
  72.7 9.7 %collective-permute-start.15 = (bf16[288,512]{1,0:T(8,128)(2,1)S(1)}, bf16[288,512]{1,0:T(8,128)(2,1)S(1)}, u32[]{:S(2)}, u32[]{:S(2)}) collective-permute-start(bf16[288,512]{1,0:T(8,128)(2,1)S(1)} %get-tuple-element.103), channel_id=1, source_target_pairs={{0,8},{1,9},{2,10},{3,11},{4,12},{5,13},{6,14},{7,15},{8,16},{9,17... | collective-permute-start | bytes 884744 | tf_op jit(solution)/shard_map/ppermute | solution.py:413
  75.1 5.3 %collective-permute-start.16 = (bf16[48,512]{1,0:T(8,128)(2,1)S(1)}, bf16[48,512]{1,0:T(8,128)(2,1)S(1)}, u32[]{:S(2)}, u32[]{:S(2)}) collective-permute-start(bf16[48,512]{1,0:T(8,128)(2,1)S(1)} %get-tuple-element.104), channel_id=1, source_target_pairs={{0,1},{1,2},{2,3},{3,4},{4,5},{5,6},{6,7},{7,0},{8,9},{9,10},{10,1... | collective-permute-start | bytes 147464 | tf_op jit(solution)/shard_map/ppermute | solution.py:413
  75.1 7.2 %collective-permute-start.17 = (bf16[48,512]{1,0:T(8,128)(2,1)S(1)}, bf16[48,512]{1,0:T(8,128)(2,1)S(1)}, u32[]{:S(2)}, u32[]{:S(2)}) collective-permute-start(bf16[48,512]{1,0:T(8,128)(2,1)S(1)} %get-tuple-element.105), channel_id=1, source_target_pairs={{0,9},{1,10},{2,11},{3,12},{4,13},{5,14},{6,15},{7,8},{8,17},{9,18... | collective-permute-start | bytes 147464 | tf_op jit(solution)/shard_map/ppermute | solution.py:413
  84.4 16.7 %collective-permute-start.21 = (bf16[96,512]{1,0:T(8,128)(2,1)S(1)}, bf16[96,512]{1,0:T(8,128)(2,1)S(1)}, u32[]{:S(2)}, u32[]{:S(2)}) collective-permute-start(bf16[96,512]{1,0:T(8,128)(2,1)S(1)} %get-tuple-element.121), channel_id=1, source_target_pairs={{0,4},{1,5},{2,6},{3,7},{4,0},{5,1},{6,2},{7,3},{8,12},{9,13},{10,... | collective-permute-start | bytes 294920 | tf_op jit(solution)/shard_map/ppermute | solution.py:418
  84.5 16.6 %collective-permute-start.22 = (bf16[96,512]{1,0:T(8,128)(2,1)S(1)}, bf16[96,512]{1,0:T(8,128)(2,1)S(1)}, u32[]{:S(2)}, u32[]{:S(2)}) collective-permute-start(bf16[96,512]{1,0:T(8,128)(2,1)S(1)} %get-tuple-element.122), channel_id=1, source_target_pairs={{0,6},{1,7},{2,4},{3,5},{4,2},{5,3},{6,0},{7,1},{8,14},{9,15},{10,... | collective-permute-start | bytes 294920 | tf_op jit(solution)/shard_map/ppermute | solution.py:418
  88.3 12.8 %collective-permute-start.18 = (bf16[192,512]{1,0:T(8,128)(2,1)S(1)}, bf16[192,512]{1,0:T(8,128)(2,1)S(1)}, u32[]{:S(2)}, u32[]{:S(2)}) collective-permute-start(bf16[192,512]{1,0:T(8,128)(2,1)S(1)} %get-tuple-element.118), channel_id=1, source_target_pairs={{0,2},{1,3},{2,0},{3,1},{4,6},{5,7},{6,4},{7,5},{8,10},{9,11},{10,... | collective-permute-start | bytes 589832 | tf_op jit(solution)/shard_map/ppermute | solution.py:418
  93.0 12.0 %collective-permute-start.19 = (bf16[96,512]{1,0:T(8,128)(2,1)S(1)}, bf16[96,512]{1,0:T(8,128)(2,1)S(1)}, u32[]{:S(2)}, u32[]{:S(2)}) collective-permute-start(bf16[96,512]{1,0:T(8,128)(2,1)S(1)} %get-tuple-element.113), channel_id=1, source_target_pairs={{0,4},{1,5},{2,6},{3,7},{4,0},{5,1},{6,2},{7,3},{8,12},{9,13},{10,... | collective-permute-start | bytes 294920 | tf_op jit(solution)/shard_map/ppermute | solution.py:418
  94.5 10.4 %collective-permute-start.20 = (bf16[96,512]{1,0:T(8,128)(2,1)S(1)}, bf16[96,512]{1,0:T(8,128)(2,1)S(1)}, u32[]{:S(2)}, u32[]{:S(2)}) collective-permute-start(bf16[96,512]{1,0:T(8,128)(2,1)S(1)} %get-tuple-element.115), channel_id=1, source_target_pairs={{0,6},{1,7},{2,4},{3,5},{4,2},{5,3},{6,0},{7,1},{8,14},{9,15},{10,... | collective-permute-start | bytes 294920 | tf_op jit(solution)/shard_map/ppermute | solution.py:418
  102.9 9.0 %collective-permute-start.24 = (bf16[96,512]{1,0:T(8,128)(2,1)S(1)}, bf16[96,512]{1,0:T(8,128)(2,1)S(1)}, u32[]{:S(2)}, u32[]{:S(2)}) collective-permute-start(bf16[96,512]{1,0:T(8,128)(2,1)S(1)} %get-tuple-element.127), channel_id=1, source_target_pairs={{0,4},{1,5},{2,6},{3,7},{4,0},{5,1},{6,2},{7,3},{8,12},{9,13},{10,... | collective-permute-start | bytes 294920 | tf_op jit(solution)/shard_map/ppermute | solution.py:418
  104.0 8.7 %collective-permute-start.26 = (bf16[96,512]{1,0:T(8,128)(2,1)S(1)}, bf16[96,512]{1,0:T(8,128)(2,1)S(1)}, u32[]{:S(2)}, u32[]{:S(2)}) collective-permute-start(bf16[96,512]{1,0:T(8,128)(2,1)S(1)} %get-tuple-element.130), channel_id=1, source_target_pairs={{0,6},{1,7},{2,4},{3,5},{4,2},{5,3},{6,0},{7,1},{8,14},{9,15},{10,... | collective-permute-start | bytes 294920 | tf_op jit(solution)/shard_map/ppermute | solution.py:418
  106.7 14.4 %collective-permute-start.23 = (bf16[192,512]{1,0:T(8,128)(2,1)S(1)}, bf16[192,512]{1,0:T(8,128)(2,1)S(1)}, u32[]{:S(2)}, u32[]{:S(2)}) collective-permute-start(bf16[192,512]{1,0:T(8,128)(2,1)S(1)} %get-tuple-element.126), channel_id=1, source_target_pairs={{0,2},{1,3},{2,0},{3,1},{4,6},{5,7},{6,4},{7,5},{8,10},{9,11},{10,... | collective-permute-start | bytes 589832 | tf_op jit(solution)/shard_map/ppermute | solution.py:418
  111.9 9.2 %collective-permute-start.25 = (bf16[96,512]{1,0:T(8,128)(2,1)S(1)}, bf16[96,512]{1,0:T(8,128)(2,1)S(1)}, u32[]{:S(2)}, u32[]{:S(2)}) collective-permute-start(bf16[96,512]{1,0:T(8,128)(2,1)S(1)} %get-tuple-element.129), channel_id=1, source_target_pairs={{0,4},{1,5},{2,6},{3,7},{4,0},{5,1},{6,2},{7,3},{8,12},{9,13},{10,... | collective-permute-start | bytes 294920 | tf_op jit(solution)/shard_map/ppermute | solution.py:418
  112.7 8.4 %collective-permute-start.27 = (bf16[96,512]{1,0:T(8,128)(2,1)S(1)}, bf16[96,512]{1,0:T(8,128)(2,1)S(1)}, u32[]{:S(2)}, u32[]{:S(2)}) collective-permute-start(bf16[96,512]{1,0:T(8,128)(2,1)S(1)} %get-tuple-element.132), channel_id=1, source_target_pairs={{0,6},{1,7},{2,4},{3,5},{4,2},{5,3},{6,0},{7,1},{8,14},{9,15},{10,... | collective-permute-start | bytes 294920 | tf_op jit(solution)/shard_map/ppermute | solution.py:418
